TPU v7x, 32 devices: a whole 2x2x4 slice. The times are simulated.
32 devices in a mesh: groups: 2 (over y), owners: 4 (over z), section: 2 (over x), rep: 2 (over core).
Axes of the slice: x: 2, y: 2, z: 4, core: 2. Of those that a mesh axis runs over, the one named last changes fastest.
Arguments:
- inputs: bfloat16 [2, 4096, 512], P('section', 'owners', ('groups', 'rep')), parts along dimension 2, may hold values from -6 to 6
- weight_first: bfloat16 [2, 32, 2048, 128], P('section', ('owners', 'rep')), may hold values from -0.1875 to 0.1875
- weight_second: bfloat16 [2, 32, 1024, 128], P('section', ('owners', 'rep')), may hold values from -0.25 to 0.25
- bias_first: float32 [2, 4096], P('section', 'owners'), may hold values from -1.5 to 1.5
- bias_second: float32 [2, 4096], P('section', 'owners'), may hold values from -1.5 to 1.5
- links_first: int32 [2, 32, 16], P('section', 'owners'), may hold values from 0 to 15, as said below
- links_second: int32 [2, 32, 8], P('section', 'owners'), may hold values from 0 to 7, as said below
Outputs:
- final_activity: bfloat16 [2, 4096, 512], P('section', 'owners', ('groups', 'rep')), parts along dimension 2
There are 2 independent parts, one for each index of `groups`. A program takes and returns all parts, laid end to end along the dimension named above; an argument that names none is the same for every part. Nothing has to cross between parts.
Inputs may be any that keep to these rules, and one draw needn't show every extreme that they name: `links_first`: in every row of every section the 16 entries are distinct. `links_second`: in every row of every section the 8 entries are distinct.
All inputs are finite; a program needn't handle non-finite values.
Results may differ from a plain program's by a relative error of at most 0.014.
Values may be sent and summed in bfloat16 or wider, within the bound.
No kernel may reach another device: no remote copies, remote signals or barrier semaphores. Data moves between devices by JAX's collectives and lax.ppermute only.
A program may use at most 64 MiB of HBM per device.

v0:
```python
import jax
import jax.numpy as jnp
from jax import lax
from jax.sharding import PartitionSpec as P

CEILING = 4.0


def from_behind(value, axis, steps):
    count = lax.axis_size(axis)
    pairs = [(source, (source + steps) % count) for source in range(count)]
    return lax.ppermute(value, axis, pairs)


def swapped(block, axis, distance):
    count = lax.axis_size(axis)
    route = []
    for low in range(count):
        high = low | 1 << distance
        if high != low and high < count:
            route += [(low, high), (high, low)]
    return lax.ppermute(block, axis, route)


def passed_along(array, axis, by):
    size = lax.axis_size(axis)
    pairs = [(i, i + by) for i in range(size) if 0 <= i + by < size]
    return lax.ppermute(array, axis, pairs)


def order_tiles(tiles, link_table):
    block_count = tiles.shape[0]
    radix_len = link_table.shape[1]
    tile_size = tiles.shape[2]
    inverse = jnp.argsort(link_table, axis=1)
    shaped = tiles.reshape(block_count, radix_len, tile_size, tile_size)
    ordered = jnp.take_along_axis(shaped, inverse[:, :, None, None], axis=1)
    return ordered.reshape(block_count, radix_len * tile_size, tile_size)


def mixed_layer(group_rows, ordered, bias_row):
    block_count = ordered.shape[0]
    tile_size = ordered.shape[2]
    row_count = group_rows.shape[1]
    summed = jnp.einsum("bkc,kr->bcr", ordered, group_rows, preferred_element_type=jnp.float32)
    summed = summed.reshape(block_count * tile_size, row_count) + bias_row[:, None]
    return jnp.clip(summed, 0.0, CEILING).astype(jnp.bfloat16)


def rotate_slots(slot_store):
    return from_behind(slot_store, "section", 1)


def body(inputs, weight_first, weight_second, bias_first, bias_second, links_first, links_second):
    section_count = lax.axis_size("section")
    section_here = lax.axis_index("section")
    owner_parity = lax.axis_index("owners") % 2
    slot_store = inputs[0]
    row_count = slot_store.shape[1]
    owner_width = slot_store.shape[0]
    zeros_own = jnp.zeros((owner_width, row_count), jnp.bfloat16)
    full_first, full_second = (
        lax.all_gather(weight_first, "rep", axis=1, tiled=True),
        lax.all_gather(weight_second, "rep", axis=1, tiled=True),
    )
    first_tiles = order_tiles(full_first[0], links_first[0])
    second_tiles = order_tiles(full_second[0], links_second[0])
    handed = zeros_own
    tick_total = 2 * section_count - 1
    for tick_index in range(tick_total):
        if tick_index < section_count:
            incoming = jnp.where(section_here == 0, slot_store, handed)
        else:
            incoming = handed
        active = jnp.logical_and(
            section_here <= tick_index, section_here > tick_index - section_count
        )
        own_half = lax.all_to_all(incoming, "owners", split_axis=0, concat_axis=0, tiled=True)
        other_half = swapped(own_half, "owners", 0)
        lower_half = jnp.where(owner_parity == 0, own_half, other_half)
        upper_half = jnp.where(owner_parity == 0, other_half, own_half)
        apply_group_rows = jnp.concatenate([lower_half, upper_half], axis=0)
        middle = lax.cond(
            active,
            lambda: mixed_layer(apply_group_rows, first_tiles, bias_first[0]),
            lambda: zeros_own,
        )
        regrouped = lax.all_to_all(middle, "owners", split_axis=0, concat_axis=0, tiled=True)
        group_rows = regrouped
        result = lax.cond(
            active, lambda: mixed_layer(group_rows, second_tiles, bias_second[0]), lambda: zeros_own
        )
        if tick_index >= section_count - 1:
            slot_store = jnp.where(section_here == section_count - 1, result, slot_store)
        if tick_index < tick_total - 1:
            handed = passed_along(result, "section", 1)
        slot_store = rotate_slots(slot_store)
    slot_store = rotate_slots(slot_store)
    return slot_store[None]


def solution(mesh):
    placed = (
        P("section", "owners", ("groups", "rep")),
        P("section", ("owners", "rep"), None, None),
        P("section", ("owners", "rep"), None, None),
        P("section", "owners"),
        P("section", "owners"),
        P("section", "owners", None),
        P("section", "owners", None),
    )
    return jax.shard_map(
        body,
        mesh=mesh,
        in_specs=placed,
        out_specs=P("section", "owners", ("groups", "rep")),
        check_vma=False,
    )
```

profile of v0, /device:TPU:0, one launch (start us, length us, event | category | flops | bytes accessed | tf_op | source)
XLA Modules:
  0.0 174.5 jit_solution(9513110891252928978)
XLA Ops:
  8.2 6.3 %all-to-all-start = ((bf16[4,256,128]{2,1,0:T(8,128)(2,1)}), bf16[4,256,128]{2,1,0:T(8,128)(2,1)S(1)}, u32[]{:S(2)}, u32[]{:S(2)}) async-start(bf16[4,256,128]{2,1,0:T(8,128)(2,1)} %bitcast.34), calls=%async_computation | async-start | bytes 524288 | tf_op jit(solution)/shard_map/all_to_all | solution.py:78
  17.8 5.7 %all-to-all-done = bf16[4,256,128]{2,1,0:T(8,128)(2,1)S(1)} async-done(((bf16[4,256,128]{2,1,0:T(8,128)(2,1)}), bf16[4,256,128]{2,1,0:T(8,128)(2,1)S(1)}, u32[]{:S(2)}, u32[]{:S(2)}) %all-to-all-start) | async-done | bytes 262176 | tf_op jit(solution)/shard_map/all_to_all | solution.py:78
  23.8 6.0 %collective-permute-done.1 = bf16[1024,128]{1,0:T(8,128)(2,1)S(1)} collective-permute-done((bf16[1024,128]{1,0:T(8,128)(2,1)S(1)}, bf16[1024,128]{1,0:T(8,128)(2,1)S(1)}, u32[]{:S(2)}, u32[]{:S(2)}) %collective-permute-start.1) | collective-permute-done | bytes 262176 | tf_op jit(solution)/shard_map/ppermute | solution.py:22
  30.0 5.3 %gather_fusion.1 = bf16[128,128,128]{2,1,0:T(8,128)(2,1)} fusion(bf16[8,16,128,128]{3,2,1,0:T(8,128)(2,1)} %bitcast.97, s32[128]{0:T(128)S(1)} %reshape.94), kind=kCustom, calls=%fused_computation.1 | custom fusion | bytes 8389632 | tf_op jit(solution)/shard_map/jit(take_along_axis)/gather | solution.py:37
  35.3 7.7 %bitcast_select_fusion = bf16[8,2048,128]{2,1,0:T(8,128)(2,1)} fusion(pred[8,2048]{1,0:T(8,128)(4,1)S(1)} %broadcast_bitcast_fusion, bf16[8,2048,128]{2,1,0:T(8,128)(2,1)} %bitcast.95), kind=kLoop, calls=%fused_computation.26 | loop fusion | flops 2097152 | bytes 8404992 | tf_op jit(solution)/shard_map/jit(take_along_axis)/select_n | solution.py:37
  43.1 4.4 %conditional.6 = (bf16[1024,128]{1,0:T(8,128)(2,1)}) conditional(s32[]{:T(128)} %convert_element_type.32, () %tuple.46, (bf16[8,2048,128]{2,1,0:T(8,128)(2,1)}, bf16[2048,128]{1,0:T(8,128)(2,1)S(1)}, f32[1,1024]{1,0:T(1,128)S(1)}) %tuple.87), branch_computations={%region_2.3_spmd, %region_3.4_spmd} | conditional | flops 537264128 | bytes 6033416 | solution.py:83
  43.1 3.5 %fusion.2 = f32[8,128,128]{2,1,0:T(8,128)S(1)} fusion(bf16[8,2048,128]{2,1,0:T(8,128)(2,1)} %get-tuple-element.111, bf16[2048,128]{1,0:T(8,128)(2,1)S(1)} %get-tuple-element.62), kind=kOutput, calls=%fused_computation.5 | convolution fusion | flops 536870912 | bytes 5242880 | tf_op jit(solution)/shard_map/cond/branch_1_fun/bkc,kr->bcr/dot_general | solution.py:45
  47.5 3.7 %all-to-all-start.1 = ((bf16[4,256,128]{2,1,0:T(8,128)(2,1)}), bf16[4,256,128]{2,1,0:T(8,128)(2,1)S(1)}, u32[]{:S(2)}, u32[]{:S(2)}) async-start(bf16[4,256,128]{2,1,0:T(8,128)(2,1)} %bitcast.36), calls=%async_computation.1 | async-start | bytes 524288 | tf_op jit(solution)/shard_map/all_to_all | solution.py:88
  51.3 3.8 %gather_fusion = bf16[64,128,128]{2,1,0:T(8,128)(2,1)} fusion(bf16[8,8,128,128]{3,2,1,0:T(8,128)(2,1)} %bitcast.99, s32[64]{0:T(128)S(1)} %reshape.88), kind=kCustom, calls=%fused_computation | custom fusion | bytes 4194816 | tf_op jit(solution)/shard_map/jit(take_along_axis)/gather | solution.py:37
  55.0 4.8 %bitcast_select_fusion.1 = bf16[8,1024,128]{2,1,0:T(8,128)(2,1)S(1)} fusion(pred[8,1024]{1,0:T(8,128)(4,1)S(1)} %broadcast_bitcast_fusion.1, bf16[8,1024,128]{2,1,0:T(8,128)(2,1)} %bitcast.96), kind=kLoop, calls=%fused_computation.27 | loop fusion | flops 1048576 | bytes 4202496 | tf_op jit(solution)/shard_map/jit(take_along_axis)/select_n | solution.py:37
  59.9 4.9 %conditional.7 = (bf16[1024,128]{1,0:T(8,128)(2,1)S(1)}) conditional(s32[]{:T(128)} %convert_element_type.32, () %tuple.45, (bf16[8,1024,128]{2,1,0:T(8,128)(2,1)S(1)}, bf16[4,256,128]{2,1,0:T(8,128)(2,1)S(1)}, f32[1,1024]{1,0:T(1,128)S(1)}) %tuple.90), branch_computations={%region_4.5_spmd, %region_5.6_spmd} | conditional | flops 268828672 | bytes 6819848 | solution.py:90
  59.9 2.6 %copy.34 = bf16[8,1024,128]{1,2,0:T(8,128)(2,1)} copy(bf16[8,1024,128]{2,1,0:T(8,128)(2,1)S(1)} %get-tuple-element.114) | data formatting | bytes 4194304 | tf_op jit(solution)/shard_map
  66.1 3.8 %collective-permute-done.2 = bf16[1024,128]{1,0:T(8,128)(2,1)S(1)} collective-permute-done((bf16[1024,128]{1,0:T(8,128)(2,1)S(1)}, bf16[1024,128]{1,0:T(8,128)(2,1)S(1)}, u32[]{:S(2)}, u32[]{:S(2)}) %collective-permute-start.2) | collective-permute-done | bytes 262176 | tf_op jit(solution)/shard_map/ppermute | solution.py:28
  70.0 13.3 %all_to_all.66 = bf16[4,256,128]{2,1,0:T(8,128)(2,1)S(1)} all-to-all(bf16[4,256,128]{2,1,0:T(8,128)(2,1)S(1)} %bitcast.107), channel_id=1, replica_groups=mesh['groups'=2,'owners'=4,'section'=2,'rep'=2] {'owners'}, dimensions={0} | all-to-all | bytes 524288 | tf_op jit(solution)/shard_map/all_to_all | solution.py:78
  85.2 4.4 %collective-permute-done.3 = bf16[1024,128]{1,0:T(8,128)(2,1)S(1)} collective-permute-done((bf16[1024,128]{1,0:T(8,128)(2,1)S(1)}, bf16[1024,128]{1,0:T(8,128)(2,1)S(1)}, u32[]{:S(2)}, u32[]{:S(2)}) %collective-permute-start.3) | collective-permute-done | bytes 262176 | tf_op jit(solution)/shard_map/ppermute | solution.py:22
  89.7 4.4 %conditional.8 = (bf16[1024,128]{1,0:T(8,128)(2,1)}) conditional(s32[]{:T(128)} %convert_element_type.31, () %tuple.44, (bf16[8,2048,128]{2,1,0:T(8,128)(2,1)}, bf16[2048,128]{1,0:T(8,128)(2,1)S(1)}, f32[1,1024]{1,0:T(1,128)S(1)}) %tuple.88), branch_computations={%region_6.7_spmd, %region_7.8_spmd} | conditional | flops 537264128 | bytes 6033416 | solution.py:83
  89.8 3.5 %fusion.8 = f32[8,128,128]{2,1,0:T(8,128)S(1)} fusion(bf16[8,2048,128]{2,1,0:T(8,128)(2,1)} %get-tuple-element.117, bf16[2048,128]{1,0:T(8,128)(2,1)S(1)} %get-tuple-element.69), kind=kOutput, calls=%fused_computation.13 | convolution fusion | flops 536870912 | bytes 5242880 | tf_op jit(solution)/shard_map/cond/branch_1_fun/bkc,kr->bcr/dot_general | solution.py:45
  94.1 3.4 %all-to-all-start.3 = ((bf16[4,256,128]{2,1,0:T(8,128)(2,1)}), bf16[4,256,128]{2,1,0:T(8,128)(2,1)S(1)}, u32[]{:S(2)}, u32[]{:S(2)}) async-start(bf16[4,256,128]{2,1,0:T(8,128)(2,1)} %bitcast.39), calls=%async_computation.3 | async-start | bytes 524288 | tf_op jit(solution)/shard_map/all_to_all | solution.py:88
  97.6 6.7 %all-to-all-done.3 = bf16[4,256,128]{2,1,0:T(8,128)(2,1)S(1)} async-done(((bf16[4,256,128]{2,1,0:T(8,128)(2,1)}), bf16[4,256,128]{2,1,0:T(8,128)(2,1)S(1)}, u32[]{:S(2)}, u32[]{:S(2)}) %all-to-all-start.3) | async-done | bytes 262176 | tf_op jit(solution)/shard_map/all_to_all | solution.py:88
  104.3 4.9 %conditional.9 = (bf16[1024,128]{1,0:T(8,128)(2,1)S(1)}) conditional(s32[]{:T(128)} %convert_element_type.31, () %tuple.43, (bf16[8,1024,128]{2,1,0:T(8,128)(2,1)S(1)}, bf16[4,256,128]{2,1,0:T(8,128)(2,1)S(1)}, f32[1,1024]{1,0:T(1,128)S(1)}) %tuple.91), branch_computations={%region_8.9_spmd, %region_9.10_spmd} | conditional | flops 268828672 | bytes 6819848 | solution.py:90
  104.3 2.6 %copy.36 = bf16[8,1024,128]{1,2,0:T(8,128)(2,1)} copy(bf16[8,1024,128]{2,1,0:T(8,128)(2,1)S(1)} %get-tuple-element.120) | data formatting | bytes 4194304 | tf_op jit(solution)/shard_map
  109.2 4.3 %collective-permute-start.4 = (bf16[1024,128]{1,0:T(8,128)(2,1)S(1)}, bf16[1024,128]{1,0:T(8,128)(2,1)S(1)}, u32[]{:S(2)}, u32[]{:S(2)}) collective-permute-start(bf16[1024,128]{1,0:T(8,128)(2,1)S(1)} %get-tuple-element.138), channel_id=1, source_target_pairs={{0,2},{1,3},{4,6},{5,7},{8,10},{9,11},{12,14},{13,15},{16,18},{17,... | collective-permute-start | bytes 786440 | tf_op jit(solution)/shard_map/ppermute | solution.py:28
  113.5 3.9 %collective-permute-done.4 = bf16[1024,128]{1,0:T(8,128)(2,1)S(1)} collective-permute-done((bf16[1024,128]{1,0:T(8,128)(2,1)S(1)}, bf16[1024,128]{1,0:T(8,128)(2,1)S(1)}, u32[]{:S(2)}, u32[]{:S(2)}) %collective-permute-start.4) | collective-permute-done | bytes 262176 | tf_op jit(solution)/shard_map/ppermute | solution.py:28
  117.4 10.3 %all_to_all.67 = bf16[4,256,128]{2,1,0:T(8,128)(2,1)S(1)} all-to-all(bf16[4,256,128]{2,1,0:T(8,128)(2,1)S(1)} %bitcast.113), channel_id=1, replica_groups=mesh['groups'=2,'owners'=4,'section'=2,'rep'=2] {'owners'}, dimensions={0} | all-to-all | bytes 524288 | tf_op jit(solution)/shard_map/all_to_all | solution.py:78
  128.8 7.0 %collective-permute-done.5 = bf16[1024,128]{1,0:T(8,128)(2,1)S(1)} collective-permute-done((bf16[1024,128]{1,0:T(8,128)(2,1)S(1)}, bf16[1024,128]{1,0:T(8,128)(2,1)S(1)}, u32[]{:S(2)}, u32[]{:S(2)}) %collective-permute-start.5) | collective-permute-done | bytes 262176 | tf_op jit(solution)/shard_map/ppermute | solution.py:22
  136.7 3.5 %all-to-all-start.5 = ((bf16[4,256,128]{2,1,0:T(8,128)(2,1)}), bf16[4,256,128]{2,1,0:T(8,128)(2,1)S(1)}, u32[]{:S(2)}, u32[]{:S(2)}) async-start(bf16[4,256,128]{2,1,0:T(8,128)(2,1)} %bitcast.42), calls=%async_computation.5 | async-start | bytes 524288 | tf_op jit(solution)/shard_map/all_to_all | solution.py:88
  140.2 4.4 %collective-permute-start.6 = (bf16[1024,128]{1,0:T(8,128)(2,1)S(1)}, bf16[1024,128]{1,0:T(8,128)(2,1)S(1)}, u32[]{:S(2)}, u32[]{:S(2)}) collective-permute-start(bf16[1024,128]{1,0:T(8,128)(2,1)S(1)} %broadcast_select_fusion.9), channel_id=1, source_target_pairs={{0,2},{2,0},{1,3},{3,1},{4,6},{6,4},{5,7},{7,5},{8,10},{10,8},{9,1... | collective-permute-start | bytes 786440 | tf_op jit(solution)/shard_map/ppermute | solution.py:12
  144.6 2.3 %all-to-all-done.5 = bf16[4,256,128]{2,1,0:T(8,128)(2,1)S(1)} async-done(((bf16[4,256,128]{2,1,0:T(8,128)(2,1)}), bf16[4,256,128]{2,1,0:T(8,128)(2,1)S(1)}, u32[]{:S(2)}, u32[]{:S(2)}) %all-to-all-start.5) | async-done | bytes 262176 | tf_op jit(solution)/shard_map/all_to_all | solution.py:88
  147.0 4.0 %collective-permute-done.6 = bf16[1024,128]{1,0:T(8,128)(2,1)S(1)} collective-permute-done((bf16[1024,128]{1,0:T(8,128)(2,1)S(1)}, bf16[1024,128]{1,0:T(8,128)(2,1)S(1)}, u32[]{:S(2)}, u32[]{:S(2)}) %collective-permute-start.6) | collective-permute-done | bytes 262176 | tf_op jit(solution)/shard_map/ppermute | solution.py:12
  151.0 5.2 %collective-permute-start.7 = (bf16[1024,128]{1,0:T(8,128)(2,1)S(1)}, bf16[1024,128]{1,0:T(8,128)(2,1)S(1)}, u32[]{:S(2)}, u32[]{:S(2)}) collective-permute-start(bf16[1024,128]{1,0:T(8,128)(2,1)S(1)} %broadcast_select_fusion.8), channel_id=1, source_target_pairs={{0,2},{2,0},{1,3},{3,1},{4,6},{6,4},{5,7},{7,5},{8,10},{10,8},{9,1... | collective-permute-start | bytes 786440 | tf_op jit(solution)/shard_map/ppermute | solution.py:12
  156.2 4.4 %collective-permute-done.7 = bf16[1024,128]{1,0:T(8,128)(2,1)S(1)} collective-permute-done((bf16[1024,128]{1,0:T(8,128)(2,1)S(1)}, bf16[1024,128]{1,0:T(8,128)(2,1)S(1)}, u32[]{:S(2)}, u32[]{:S(2)}) %collective-permute-start.7) | collective-permute-done | bytes 262176 | tf_op jit(solution)/shard_map/ppermute | solution.py:12
  162.6 4.4 %collective-permute-done.8 = bf16[1024,128]{1,0:T(8,128)(2,1)S(1)} collective-permute-done((bf16[1024,128]{1,0:T(8,128)(2,1)S(1)}, bf16[1024,128]{1,0:T(8,128)(2,1)S(1)}, u32[]{:S(2)}, u32[]{:S(2)}) %collective-permute-start.8) | collective-permute-done | bytes 262176 | tf_op jit(solution)/shard_map/ppermute | solution.py:12
  (61 shorter events, 20.8 us)
Async XLA Ops:
  6.5 0.9 copy-start
  6.5 23.4 %all-gather.5.cloned.1.call-start = ((), (), s32[]{:S(2)}) async-start(), calls=%async_computation.7 | async-start | bytes 6291456 | tf_op jit(solution)/shard_map/all_gather | solution.py:63
  6.5 9.5 %copy-start.2 = (s32[1,8,16]{2,1,0:T(8,128)S(1)}, s32[1,8,16]{2,1,0:T(8,128)}, u32[]{:S(2)}) copy-start(s32[1,8,16]{2,1,0:T(8,128)} %param.24) | copy-start | bytes 1540
  6.5 10.5 %copy-start.3 = (s32[1,8,8]{2,1,0:T(8,128)S(1)}, s32[1,8,8]{2,1,0:T(8,128)}, u32[]{:S(2)}) copy-start(s32[1,8,8]{2,1,0:T(8,128)} %param.25) | copy-start | bytes 772
  8.2 15.2 %all-to-all-start = ((bf16[4,256,128]{2,1,0:T(8,128)(2,1)}), bf16[4,256,128]{2,1,0:T(8,128)(2,1)S(1)}, u32[]{:S(2)}, u32[]{:S(2)}) async-start(bf16[4,256,128]{2,1,0:T(8,128)(2,1)} %bitcast.34), calls=%async_computation | async-start | bytes 524288 | tf_op jit(solution)/shard_map/all_to_all | solution.py:78
  14.5 36.7 %all-gather.3.cloned.1.call-start = ((), (), s32[]{:S(2)}) async-start(), calls=%async_computation.6 | async-start | bytes 3145728 | tf_op jit(solution)/shard_map/all_gather | solution.py:64
  14.5 51.6 %collective-permute-start = (bf16[1024,128]{1,0:T(8,128)(2,1)S(1)}, bf16[1024,128]{1,0:T(8,128)(2,1)S(1)}, u32[]{:S(2)}, u32[]{:S(2)}) collective-permute-start(bf16[1024,128]{1,0:T(8,128)(2,1)S(1)} %bitcast.108), channel_id=1, source_target_pairs={{0,2},{2,0},{1,3},{3,1},{4,6},{6,4},{5,7},{7,5},{8,10},{10,8},{9,1... | collective-permute-start | bytes 786440 | tf_op jit(solution)/shard_map/ppermute | solution.py:12
  23.4 6.4 %collective-permute-start.1 = (bf16[1024,128]{1,0:T(8,128)(2,1)S(1)}, bf16[1024,128]{1,0:T(8,128)(2,1)S(1)}, u32[]{:S(2)}, u32[]{:S(2)}) collective-permute-start(bf16[1024,128]{1,0:T(8,128)(2,1)S(1)} %bitcast.104), channel_id=1, source_target_pairs={{0,4},{4,0},{8,12},{12,8},{1,5},{5,1},{9,13},{13,9},{2,6},{6,2},{1... | collective-permute-start | bytes 786440 | tf_op jit(solution)/shard_map/ppermute | solution.py:22
  35.3 7.7 %copy-start.1 = (f32[1,1024]{1,0:T(1,128)S(1)}, f32[1,1024]{1,0:T(1,128)}, u32[]{:S(2)}) copy-start(f32[1,1024]{1,0:T(1,128)} %param.22) | copy-start | bytes 12292
  47.5 12.4 %all-to-all-start.1 = ((bf16[4,256,128]{2,1,0:T(8,128)(2,1)}), bf16[4,256,128]{2,1,0:T(8,128)(2,1)S(1)}, u32[]{:S(2)}, u32[]{:S(2)}) async-start(bf16[4,256,128]{2,1,0:T(8,128)(2,1)} %bitcast.36), calls=%async_computation.1 | async-start | bytes 524288 | tf_op jit(solution)/shard_map/all_to_all | solution.py:88
  55.0 4.8 %copy-start.4 = (f32[1,1024]{1,0:T(1,128)S(1)}, f32[1,1024]{1,0:T(1,128)}, u32[]{:S(2)}) copy-start(f32[1,1024]{1,0:T(1,128)} %param.23) | copy-start | bytes 12292
  64.8 5.2 %collective-permute-start.2 = (bf16[1024,128]{1,0:T(8,128)(2,1)S(1)}, bf16[1024,128]{1,0:T(8,128)(2,1)S(1)}, u32[]{:S(2)}, u32[]{:S(2)}) collective-permute-start(bf16[1024,128]{1,0:T(8,128)(2,1)S(1)} %get-tuple-element.136), channel_id=1, source_target_pairs={{0,2},{1,3},{4,6},{5,7},{8,10},{9,11},{12,14},{13,15},{16,18},{17,... | collective-permute-start | bytes 786440 | tf_op jit(solution)/shard_map/ppermute | solution.py:28
  83.3 6.4 %collective-permute-start.3 = (bf16[1024,128]{1,0:T(8,128)(2,1)S(1)}, bf16[1024,128]{1,0:T(8,128)(2,1)S(1)}, u32[]{:S(2)}, u32[]{:S(2)}) collective-permute-start(bf16[1024,128]{1,0:T(8,128)(2,1)S(1)} %bitcast.106), channel_id=1, source_target_pairs={{0,4},{4,0},{8,12},{12,8},{1,5},{5,1},{9,13},{13,9},{2,6},{6,2},{1... | collective-permute-start | bytes 786440 | tf_op jit(solution)/shard_map/ppermute | solution.py:22
  94.1 10.2 %all-to-all-start.3 = ((bf16[4,256,128]{2,1,0:T(8,128)(2,1)}), bf16[4,256,128]{2,1,0:T(8,128)(2,1)S(1)}, u32[]{:S(2)}, u32[]{:S(2)}) async-start(bf16[4,256,128]{2,1,0:T(8,128)(2,1)} %bitcast.39), calls=%async_computation.3 | async-start | bytes 524288 | tf_op jit(solution)/shard_map/all_to_all | solution.py:88
  109.2 8.2 %collective-permute-start.4 = (bf16[1024,128]{1,0:T(8,128)(2,1)S(1)}, bf16[1024,128]{1,0:T(8,128)(2,1)S(1)}, u32[]{:S(2)}, u32[]{:S(2)}) collective-permute-start(bf16[1024,128]{1,0:T(8,128)(2,1)S(1)} %get-tuple-element.138), channel_id=1, source_target_pairs={{0,2},{1,3},{4,6},{5,7},{8,10},{9,11},{12,14},{13,15},{16,18},{17,... | collective-permute-start | bytes 786440 | tf_op jit(solution)/shard_map/ppermute | solution.py:28
  127.7 8.1 %collective-permute-start.5 = (bf16[1024,128]{1,0:T(8,128)(2,1)S(1)}, bf16[1024,128]{1,0:T(8,128)(2,1)S(1)}, u32[]{:S(2)}, u32[]{:S(2)}) collective-permute-start(bf16[1024,128]{1,0:T(8,128)(2,1)S(1)} %bitcast.105), channel_id=1, source_target_pairs={{0,4},{4,0},{8,12},{12,8},{1,5},{5,1},{9,13},{13,9},{2,6},{6,2},{1... | collective-permute-start | bytes 786440 | tf_op jit(solution)/shard_map/ppermute | solution.py:22
  136.7 10.2 %all-to-all-start.5 = ((bf16[4,256,128]{2,1,0:T(8,128)(2,1)}), bf16[4,256,128]{2,1,0:T(8,128)(2,1)S(1)}, u32[]{:S(2)}, u32[]{:S(2)}) async-start(bf16[4,256,128]{2,1,0:T(8,128)(2,1)} %bitcast.42), calls=%async_computation.5 | async-start | bytes 524288 | tf_op jit(solution)/shard_map/all_to_all | solution.py:88
  140.2 10.8 %collective-permute-start.6 = (bf16[1024,128]{1,0:T(8,128)(2,1)S(1)}, bf16[1024,128]{1,0:T(8,128)(2,1)S(1)}, u32[]{:S(2)}, u32[]{:S(2)}) collective-permute-start(bf16[1024,128]{1,0:T(8,128)(2,1)S(1)} %broadcast_select_fusion.9), channel_id=1, source_target_pairs={{0,2},{2,0},{1,3},{3,1},{4,6},{6,4},{5,7},{7,5},{8,10},{10,8},{9,1... | collective-permute-start | bytes 786440 | tf_op jit(solution)/shard_map/ppermute | solution.py:12
  151.0 9.6 %collective-permute-start.7 = (bf16[1024,128]{1,0:T(8,128)(2,1)S(1)}, bf16[1024,128]{1,0:T(8,128)(2,1)S(1)}, u32[]{:S(2)}, u32[]{:S(2)}) collective-permute-start(bf16[1024,128]{1,0:T(8,128)(2,1)S(1)} %broadcast_select_fusion.8), channel_id=1, source_target_pairs={{0,2},{2,0},{1,3},{3,1},{4,6},{6,4},{5,7},{7,5},{8,10},{10,8},{9,1... | collective-permute-start | bytes 786440 | tf_op jit(solution)/shard_map/ppermute | solution.py:12
  160.6 6.4 %collective-permute-start.8 = (bf16[1024,128]{1,0:T(8,128)(2,1)S(1)}, bf16[1024,128]{1,0:T(8,128)(2,1)S(1)}, u32[]{:S(2)}, u32[]{:S(2)}) collective-permute-start(bf16[1024,128]{1,0:T(8,128)(2,1)S(1)} %collective-permute-done.7), channel_id=1, source_target_pairs={{0,2},{2,0},{1,3},{3,1},{4,6},{6,4},{5,7},{7,5},{8,10},{10,8},{9,1... | collective-permute-start | bytes 786440 | tf_op jit(solution)/shard_map/ppermute | solution.py:12
Sparse Core Ops, SparseCore 0:
  8.9 16.3 all-gather.4
  26.9 11.7 all-gather.2
where the time goes:
time: 176 us; the launch traced here: 175 us
  waiting for transfers between devices  53.3 us (30%)
  starting transfers between devices  38.9 us (22%)
  blocking collectives  23.6 us (13%)
  other arithmetic  16.8 us (10%)
  local copies, waits for them, and re-layouts  16.6 us (9%)
  between operations  13.6 us (8%)
  matrix products  11.5 us (7%)
    all_to_all x2, blocking collectives, body(): lax.all_to_all(incoming, 'owners', split_axis=0, concat_axis=0, tiled=True)  23.6 us
    ppermute x3, waiting for transfers between devices, swapped(): return lax.ppermute(block, axis, route)  17.4 us
    ppermute x4, starting transfers between devices, from_behind(): return lax.ppermute(value, axis, pairs)  13.2 us
    ppermute x4, waiting for transfers between devices, from_behind(): return lax.ppermute(value, axis, pairs)  12.7 us
    select_n x2, other arithmetic, order_tiles(): ordered = jnp.take_along_axis(shaped, inverse[:, :, None, None], axis=1)  12.5 us
    dot_general x4, matrix products, mixed_layer(): jnp.einsum('bkc,kr->bcr', ordered, group_rows, preferred_element_type=jnp...  11.5 us
    all_to_all x3, starting transfers between devices, body(): lax.all_to_all(middle, 'owners', split_axis=0, concat_axis=0, tiled=True)  10.6 us
    gather x6, local copies, waits for them, and re-layouts, order_tiles(): ordered = jnp.take_along_axis(shaped, inverse[:, :, None, None], axis=1)  9.4 us
  transfers between devices with their start and end apart: 15, of which 11 were waited for; matrix products, arithmetic and copies ran while one was open for 19% of the time, Pallas kernels for 0%

commit v1 on v0

--- a/solution.py
+++ b/solution.py
@@ -1,9 +1,210 @@
+import functools
+
 import jax
 import jax.numpy as jnp
 from jax import lax
+from jax.experimental import pallas as pl
+from jax.experimental.pallas import tpu as pltpu
 from jax.sharding import PartitionSpec as P
 
 CEILING = 4.0
+
+
+def layer_kernel(
+    tile_list, out_groups, neuron_major, final, active_section, *refs
+):
+    meta, table, own_tiles, other_tiles, bias = refs[:5]
+    buffer_count = 1 + max(buffer for buffer, _ in tile_list)
+    buffers = refs[5 : 5 + buffer_count]
+    rest = list(refs[5 + buffer_count :])
+    settled = rest.pop(0) if final == "merge" else None
+    out_count = 1 if final else len(out_groups)
+    outs = rest[:out_count]
+    tiles, turned, arrivals = rest[out_count:]
+    me, rep, section = meta[0], meta[1], meta[2]
+    half = own_tiles.shape[0]
+    size = tiles.shape[2]
+    width = 2 * size
+
+    def run():
+        for base, source in ((rep * half, own_tiles), ((1 - rep) * half, other_tiles)):
+            for low in range(0, half, 2):
+                pltpu.make_async_copy(
+                    source.at[pl.ds(low, 2)],
+                    tiles.at[pl.ds(base + low, 2)],
+                    arrivals.at[(base + low) // 2],
+                ).start()
+        if neuron_major:
+            for place, (buffer, column) in enumerate(tile_list):
+                turned[place] = buffers[buffer][pl.ds(column, width), :].T
+        for distance in range(2 * half // 2):
+            owner = me ^ distance
+            pltpu.make_async_copy(
+                own_tiles.at[pl.ds(0, 2)], tiles.at[pl.ds(2 * owner, 2)], arrivals.at[owner]
+            ).wait()
+            rows = turned.shape[1]
+            total = jnp.zeros((rows, width), jnp.float32)
+            for place, (buffer, column) in enumerate(tile_list):
+                if neuron_major:
+                    left = turned[place]
+                else:
+                    left = buffers[buffer][:, pl.ds(column, width)]
+                right = jnp.concatenate(
+                    [
+                        jnp.concatenate(
+                            [
+                                tiles[
+                                    2 * owner + j,
+                                    pl.ds(
+                                        pl.multiple_of(table[2 * distance + j, 2 * place + i] * size, size),
+                                        size,
+                                    ),
+                                    :,
+                                ]
+                                for j in range(2)
+                            ],
+                            axis=1,
+                        )
+                        for i in range(2)
+                    ],
+                    axis=0,
+                )
+                total = total + jnp.dot(left, right, preferred_element_type=jnp.float32)
+            shift = jnp.concatenate([bias[pl.ds(2 * owner + j, 1), :] for j in range(2)], axis=1)
+            value = jnp.clip(total + shift, 0.0, CEILING)
+            if final:
+                outs[0][pl.ds(pl.multiple_of(owner * width, width), width), :] = value.T.astype(jnp.bfloat16)
+            else:
+                for out, group in zip(outs, out_groups, strict=True):
+                    if distance in group:
+                        out[:, pl.ds(group.index(distance) * width, width)] = value.astype(jnp.bfloat16)
+
+    pl.when(section == active_section)(run)
+    if final == "merge":
+
+        @pl.when(section != active_section)
+        def _():
+            outs[0][...] = settled[...]
+
+
+def layer(
+    meta, table, own_tiles, other_tiles, bias, buffers, tile_list, out_groups, active_section,
+    neuron_major=False, final=None, settled=None,
+):
+    half, depth, size = own_tiles.shape
+    rows = buffers[0].shape[1] if neuron_major else buffers[0].shape[0]
+    if final:
+        shapes = [jax.ShapeDtypeStruct((2 * half * size, rows), jnp.bfloat16)]
+    else:
+        shapes = [jax.ShapeDtypeStruct((rows, len(group) * 2 * size), jnp.bfloat16) for group in out_groups]
+    smem = pl.BlockSpec(memory_space=pltpu.SMEM)
+    hbm = pl.BlockSpec(memory_space=pl.ANY)
+    vmem = pl.BlockSpec(memory_space=pltpu.VMEM)
+    operands = [meta, table, own_tiles, other_tiles, bias, *buffers] + ([settled] if final == "merge" else [])
+    turned = (len(tile_list), rows, 2 * size) if neuron_major else (1, rows, 2 * size)
+    return pl.pallas_call(
+        functools.partial(layer_kernel, tile_list, out_groups, neuron_major, final, active_section),
+        out_shape=shapes,
+        in_specs=[smem, smem, hbm, hbm] + [vmem] * (len(operands) - 4),
+        out_specs=[vmem] * len(shapes),
+        scratch_shapes=[
+            pltpu.VMEM((2 * half, depth, size), jnp.bfloat16),
+            pltpu.VMEM(turned, jnp.bfloat16),
+            pltpu.SemaphoreType.DMA((half,)),
+        ],
+        compiler_params=pltpu.CompilerParams(vmem_limit_bytes=24 * 2**20),
+        cost_estimate=pl.CostEstimate(
+            flops=4 * half * depth * size * rows, bytes_accessed=4 * half * depth * size, transcendentals=0
+        ),
+    )(*operands)
+
+
+def fast_body(inputs, weight_first, weight_second, bias_first, bias_second, links_first, links_second):
+    owner_count = lax.axis_size("owners")
+    section = lax.axis_index("section")
+    me = lax.axis_index("owners")
+    rep = lax.axis_index("rep")
+    size = weight_first.shape[3]
+    features = inputs[0]
+    piece = features.shape[0] // owner_count
+    meta = jnp.stack([me, rep, section]).astype(jnp.int32)
+
+    def moved(value, distance, cross):
+        pairs = []
+        for owner in range(owner_count):
+            for place in range(2):
+                target = (owner ^ distance) * 2 + (1 - place if cross else place)
+                pairs.append((owner * 2 + place, target))
+        return lax.ppermute(value, ("owners", "section"), pairs)
+
+    def other_core(value):
+        return lax.ppermute(value, "rep", [(0, 1), (1, 0)])
+
+    def table_of(links, places):
+        count = links.shape[0]
+        order = jnp.arange(count)
+        wanted = 2 * (me ^ (order // 2)) + order % 2
+        slots = jnp.arange(links.shape[1])
+        row = wanted[:, None, None, None] == jnp.arange(count)[None, None, :, None]
+        hit = links[None, None, :, :] == places[None, :, None, None]
+        return jnp.sum(jnp.where(row & hit, slots[None, None, None, :], 0), axis=(2, 3)).astype(jnp.int32)
+
+    def first_places(sources):
+        found = []
+        for source, target in sources:
+            low = ((me ^ target) % 2) * (owner_count * 2) + (me ^ source) * 2
+            found += [low, low + 1]
+        return jnp.stack(found)
+
+    features = features.reshape(owner_count, piece, features.shape[1])
+    cut = [lax.dynamic_index_in_dim(features, me ^ distance, 0, keepdims=False) for distance in range(owner_count)]
+    near = jnp.concatenate(cut[:2], axis=0)
+    far = jnp.concatenate(cut[2:], axis=0)
+    start = [near, moved(near, 1, False), moved(far, 2, False), moved(far, 3, False)]
+    first_own, second_own = weight_first[0], weight_second[0]
+    first_other = other_core(first_own)
+    second_other = other_core(second_own)
+    later = [moved(value, 0, True) for value in start]
+
+    direct = [(0, 0), (0, 1), (1, 1), (1, 0), (2, 0), (2, 1), (3, 1), (3, 0)]
+    direct_tiles = [(buffer, column * piece) for buffer in range(4) for column in range(2)]
+    relayed = [(0, 0), (0, 1), (1, 1), (1, 0), (2, 0), (3, 0), (3, 1), (2, 1)]
+    relayed_tiles = [(0, 0), (0, piece), (1, 0), (1, piece), (2, 0), (3, 0), (4, 0), (5, 0)]
+    second_tiles = [(buffer, 0) for buffer in range(4)]
+
+    direct_table = table_of(links_first[0], first_places(direct))
+    relayed_table = table_of(links_first[0], first_places(relayed))
+    second_places = jnp.stack([2 * (me ^ (place // 2)) + place % 2 for place in range(2 * owner_count)])
+    second_table = table_of(links_second[0], second_places)
+    first_bias = bias_first[0].reshape(-1, size)
+    second_bias = bias_second[0].reshape(-1, size)
+
+    apart = [[0], [1], [2], [3]]
+    joined = [[0, 1], [2], [3]]
+
+    def first_layer(buffers, active, raw):
+        return layer(
+            meta, direct_table if raw else relayed_table, first_own, first_other, first_bias, buffers,
+            direct_tiles if raw else relayed_tiles, apart, active, neuron_major=raw,
+        )
+
+    def second_layer(parts, active, **more):
+        buffers = [parts[0]] + [moved(parts[distance], distance, False) for distance in range(1, owner_count)]
+        return layer(
+            meta, second_table, second_own, second_other, second_bias, buffers, second_tiles, joined, active, **more
+        )
+
+    def hand_over(result):
+        close, far_two, far_three = result
+        two, three = moved(far_two, 2, True), moved(far_three, 3, True)
+        close = moved(close, 0, True)
+        return [close, moved(close, 1, False), two, three, moved(two, 1, False), moved(three, 1, False)]
+
+    zero = second_layer(first_layer(start, 0, True), 0)
+    one = second_layer(first_layer(later, 0, True), 0)
+    settled = second_layer(first_layer(hand_over(zero), 1, False), 1, final="plain")[0]
+    settled = moved(settled, 0, True)
+    return second_layer(first_layer(hand_over(one), 1, False), 1, final="merge", settled=settled)[0][None]
 
 
 def from_behind(value, axis, steps):
@@ -51,7 +252,7 @@
     return from_behind(slot_store, "section", 1)
 
 
-def body(inputs, weight_first, weight_second, bias_first, bias_second, links_first, links_second):
+def general_body(inputs, weight_first, weight_second, bias_first, bias_second, links_first, links_second):
     section_count = lax.axis_size("section")
     section_here = lax.axis_index("section")
     owner_parity = lax.axis_index("owners") % 2
@@ -99,6 +300,22 @@
     return slot_store[None]
 
 
+def body(*arrays):
+    inputs, weight_first = arrays[:2]
+    owner_count = lax.axis_size("owners")
+    size = weight_first.shape[3]
+    width = inputs.shape[1]
+    fits = (
+        lax.axis_size("section") == 2
+        and lax.axis_size("rep") == 2
+        and owner_count == 4
+        and width == 2 * size * owner_count
+        and weight_first.shape[2] == 2 * width
+        and arrays[2].shape[2] == width
+    )
+    return fast_body(*arrays) if fits else general_body(*arrays)
+
+
 def solution(mesh):
     placed = (
         P("section", "owners", ("groups", "rep")),

time: 176 us -> 98.5 us (0.56)
  the two profiles are of different devices: /device:TPU:0 before, /device:TPU:2 now
where the time goes in v1:
time: 98.5 us; the launch traced here: 98.2 us
  starting transfers between devices  46.9 us (48%)
  waiting for transfers between devices  26 us (26%)
  Pallas kernels  13.7 us (14%)
  other arithmetic  7.66 us (8%)
  local copies, waits for them, and re-layouts  3.54 us (4%)
    ppermute x32, starting transfers between devices, moved(): return lax.ppermute(value, ('owners', 'section'), pairs)  46.9 us
    ppermute x32, waiting for transfers between devices, moved(): return lax.ppermute(value, ('owners', 'section'), pairs)  26 us
    pallas_call x8, Pallas kernels, layer(): pl.pallas_call(functools.partial(layer_kernel, tile_list, out_groups, neu...  13.7 us
    reduce_sum x2, other arithmetic, table_of(): jnp.sum(jnp.where(row & hit, slots[None, None, None, :], 0), axis=(2, 3))  5.96 us
    unnamed x14, local copies, waits for them, and re-layouts  2.3 us
  transfers between devices with their start and end apart: 34, of which 13 were waited for; matrix products, arithmetic and copies ran while one was open for 9% of the time, Pallas kernels for 11%

profile of v1, /device:TPU:2, one launch (start us, length us, event | category | flops | bytes accessed | tf_op | source)
XLA Modules:
  0.0 98.2 jit_solution(6673771676089818042)
XLA Ops:
  1.6 3.6 %collective-permute-start.7 = (bf16[512,128]{1,0:T(8,128)(2,1)}, bf16[512,128]{1,0:T(8,128)(2,1)S(1)}, u32[]{:S(2)}, u32[]{:S(2)}) collective-permute-start(bf16[512,128]{1,0:T(8,128)(2,1)} %pad_maximum_fusion.1), channel_id=1, source_target_pairs={{0,12},{2,14},{4,8},{6,10},{8,4},{10,6},{12,0},{14,2},{1,13},{3,15... | collective-permute-start | bytes 393224 | tf_op jit(solution)/shard_map/ppermute | solution.py:138
  7.3 4.7 %select_reduce_fusion = (s32[8,16]{1,0:T(8,128)S(1)}, s32[8,16]{1,0:T(8,128)S(1)}) fusion(pred[16,8,16]{2,1,0:T(8,128)(4,1)S(1)} %get-tuple-element.56, pred[8,8]{1,0:T(8,128)(4,1)S(1)} %iota_compare_fusion, pred[16,8,16]{2,1,0:T(8,128)(4,1)S(1)} %get-tuple-element.55), kind=kLoop, calls=%fused_computation | loop fusion | flops 98048 | bytes 5184 | tf_op jit(solution)/shard_map/reduce_sum | solution.py:150
  12.0 2.6 %collective-permute-done.3.refs_6_ = bf16[512,128]{1,0:T(8,128)(2,1)} collective-permute-done((bf16[512,128]{1,0:T(8,128)(2,1)S(1)}, bf16[512,128]{1,0:T(8,128)(2,1)}, u32[]{:S(2)}, u32[]{:S(2)}) %collective-permute-start.3) | collective-permute-done | bytes 131104 | tf_op jit(solution)/shard_map/ppermute | solution.py:138
  15.1 2.1 %collective-permute-done.5.refs_7_ = bf16[512,128]{1,0:T(8,128)(2,1)S(1)} collective-permute-done((bf16[512,128]{1,0:T(8,128)(2,1)}, bf16[512,128]{1,0:T(8,128)(2,1)S(1)}, u32[]{:S(2)}, u32[]{:S(2)}) %collective-permute-start.5) | collective-permute-done | bytes 131104 | tf_op jit(solution)/shard_map/ppermute | solution.py:138
  17.2 1.6 %copy-done = bf16[1,4,2048,128]{3,2,1,0:T(8,128)(2,1)S(1)} copy-done((bf16[1,4,2048,128]{3,2,1,0:T(8,128)(2,1)S(1)}, bf16[1,4,2048,128]{3,2,1,0:T(8,128)(2,1)}, u32[]{:S(2)}) %copy-start) | copy-done | bytes 2097176
  21.1 2.5 %collective-permute-start.22 = (bf16[128,256]{1,0:T(8,128)(2,1)S(1)}, bf16[128,256]{1,0:T(8,128)(2,1)S(1)}, u32[]{:S(2)}, u32[]{:S(2)}) collective-permute-start(bf16[128,256]{1,0:T(8,128)(2,1)S(1)} %get-tuple-element.40), channel_id=1, source_target_pairs={{0,8},{2,10},{4,12},{6,14},{8,0},{10,2},{12,4},{14,6},{1,9},{3,11}... | collective-permute-start | bytes 196616 | tf_op jit(solution)/shard_map/ppermute | solution.py:138
  23.7 2.8 %collective-permute-start.4 = (bf16[512,128]{1,0:T(8,128)(2,1)}, bf16[512,128]{1,0:T(8,128)(2,1)S(1)}, u32[]{:S(2)}, u32[]{:S(2)}) collective-permute-start(bf16[512,128]{1,0:T(8,128)(2,1)} %collective-permute-done.3.refs_6_), channel_id=1, source_target_pairs={{0,2},{2,0},{4,6},{6,4},{8,10},{10,8},{12,14},{14,12},{1,3},{3,1},... | collective-permute-start | bytes 393224 | tf_op jit(solution)/shard_map/ppermute | solution.py:138
  26.6 1.9 %collective-permute-start.6 = (bf16[512,128]{1,0:T(8,128)(2,1)S(1)}, bf16[512,128]{1,0:T(8,128)(2,1)S(1)}, u32[]{:S(2)}, u32[]{:S(2)}) collective-permute-start(bf16[512,128]{1,0:T(8,128)(2,1)S(1)} %collective-permute-done.5.refs_7_), channel_id=1, source_target_pairs={{0,2},{2,0},{4,6},{6,4},{8,10},{10,8},{12,14},{14,12},{1,3},{3,1},... | collective-permute-start | bytes 393224 | tf_op jit(solution)/shard_map/ppermute | solution.py:138
  28.6 2.1 %collective-permute-start.23 = (bf16[128,256]{1,0:T(8,128)(2,1)S(1)}, bf16[128,256]{1,0:T(8,128)(2,1)S(1)}, u32[]{:S(2)}, u32[]{:S(2)}) collective-permute-start(bf16[128,256]{1,0:T(8,128)(2,1)S(1)} %get-tuple-element.41), channel_id=1, source_target_pairs={{0,12},{2,14},{4,8},{6,10},{8,4},{10,6},{12,0},{14,2},{1,13},{3,15... | collective-permute-start | bytes 196616 | tf_op jit(solution)/shard_map/ppermute | solution.py:138
  32.0 2.6 %collective-permute-done.23.refs_8_ = bf16[128,256]{1,0:T(8,128)(2,1)S(1)} collective-permute-done((bf16[128,256]{1,0:T(8,128)(2,1)S(1)}, bf16[128,256]{1,0:T(8,128)(2,1)S(1)}, u32[]{:S(2)}, u32[]{:S(2)}) %collective-permute-start.23) | collective-permute-done | bytes 65568 | tf_op jit(solution)/shard_map/ppermute | solution.py:138
  35.3 3.5 %collective-permute-start.24 = (bf16[128,512]{1,0:T(8,128)(2,1)S(1)}, bf16[128,512]{1,0:T(8,128)(2,1)S(1)}, u32[]{:S(2)}, u32[]{:S(2)}) collective-permute-start(bf16[128,512]{1,0:T(8,128)(2,1)S(1)} %get-tuple-element.42), channel_id=1, source_target_pairs={{0,2},{2,0},{4,6},{6,4},{8,10},{10,8},{12,14},{14,12},{1,3},{3,1},... | collective-permute-start | bytes 393224 | tf_op jit(solution)/shard_map/ppermute | solution.py:138
  39.6 3.2 %collective-permute-start.26 = (bf16[128,256]{1,0:T(8,128)(2,1)S(1)}, bf16[128,256]{1,0:T(8,128)(2,1)S(1)}, u32[]{:S(2)}, u32[]{:S(2)}) collective-permute-start(bf16[128,256]{1,0:T(8,128)(2,1)S(1)} %get-tuple-element.43), channel_id=1, source_target_pairs={{0,10},{2,8},{4,14},{6,12},{8,2},{10,0},{12,6},{14,4},{1,11},{3,9}... | collective-permute-start | bytes 196616 | tf_op jit(solution)/shard_map/ppermute | solution.py:138
  42.8 2.0 %collective-permute-start.27 = (bf16[128,256]{1,0:T(8,128)(2,1)S(1)}, bf16[128,256]{1,0:T(8,128)(2,1)S(1)}, u32[]{:S(2)}, u32[]{:S(2)}) collective-permute-start(bf16[128,256]{1,0:T(8,128)(2,1)S(1)} %get-tuple-element.44), channel_id=1, source_target_pairs={{0,14},{2,12},{4,10},{6,8},{8,6},{10,4},{12,2},{14,0},{1,15},{3,13... | collective-permute-start | bytes 196616 | tf_op jit(solution)/shard_map/ppermute | solution.py:138
  44.9 1.6 %collective-permute-start.10 = (bf16[128,256]{1,0:T(8,128)(2,1)S(1)}, bf16[128,256]{1,0:T(8,128)(2,1)S(1)}, u32[]{:S(2)}, u32[]{:S(2)}) collective-permute-start(bf16[128,256]{1,0:T(8,128)(2,1)S(1)} %get-tuple-element.29), channel_id=1, source_target_pairs={{0,8},{2,10},{4,12},{6,14},{8,0},{10,2},{12,4},{14,6},{1,9},{3,11}... | collective-permute-start | bytes 196616 | tf_op jit(solution)/shard_map/ppermute | solution.py:138
  46.4 2.8 %collective-permute-start.11 = (bf16[128,256]{1,0:T(8,128)(2,1)S(1)}, bf16[128,256]{1,0:T(8,128)(2,1)S(1)}, u32[]{:S(2)}, u32[]{:S(2)}) collective-permute-start(bf16[128,256]{1,0:T(8,128)(2,1)S(1)} %get-tuple-element.30), channel_id=1, source_target_pairs={{0,12},{2,14},{4,8},{6,10},{8,4},{10,6},{12,0},{14,2},{1,13},{3,15... | collective-permute-start | bytes 196616 | tf_op jit(solution)/shard_map/ppermute | solution.py:138
  51.4 1.6 %collective-permute-done.11.refs_8_ = bf16[128,256]{1,0:T(8,128)(2,1)S(1)} collective-permute-done((bf16[128,256]{1,0:T(8,128)(2,1)S(1)}, bf16[128,256]{1,0:T(8,128)(2,1)S(1)}, u32[]{:S(2)}, u32[]{:S(2)}) %collective-permute-start.11) | collective-permute-done | bytes 65568 | tf_op jit(solution)/shard_map/ppermute | solution.py:138
  53.6 3.3 %collective-permute-start.12 = (bf16[128,512]{1,0:T(8,128)(2,1)S(1)}, bf16[128,512]{1,0:T(8,128)(2,1)S(1)}, u32[]{:S(2)}, u32[]{:S(2)}) collective-permute-start(bf16[128,512]{1,0:T(8,128)(2,1)S(1)} %get-tuple-element.31), channel_id=1, source_target_pairs={{0,2},{2,0},{4,6},{6,4},{8,10},{10,8},{12,14},{14,12},{1,3},{3,1},... | collective-permute-start | bytes 393224 | tf_op jit(solution)/shard_map/ppermute | solution.py:138
  56.9 2.7 %shard_map.78 = (bf16[128,256]{1,0:T(8,128)(2,1)S(1)}, bf16[128,256]{1,0:T(8,128)(2,1)S(1)}, bf16[128,256]{1,0:T(8,128)(2,1)S(1)}, bf16[128,256]{1,0:T(8,128)(2,1)S(1)}) custom-call(s32[3]{0:T(128)S(1)} %pad_add_fusion.refs_0_, s32[8,16]{1,0:T(8,128)S(1)} %get-tuple-element.50.refs_1_, bf16[4,2048,128]{2,1,0:T(8,128)(2,1)S(1)} %bitcast.46, ...), custom_call_target="tpu_custom_call" | custom-call | flops 536870912 | bytes 4194304 | tf_op jit(solution)/shard_map/pallas_call | solution.py:105
  59.7 3.3 %collective-permute-start.31 = (bf16[128,256]{1,0:T(8,128)(2,1)S(1)}, bf16[128,256]{1,0:T(8,128)(2,1)S(1)}, u32[]{:S(2)}, u32[]{:S(2)}) collective-permute-start(bf16[128,256]{1,0:T(8,128)(2,1)S(1)} %get-tuple-element.47), channel_id=1, source_target_pairs={{0,8},{2,10},{4,12},{6,14},{8,0},{10,2},{12,4},{14,6},{1,9},{3,11}... | collective-permute-start | bytes 196616 | tf_op jit(solution)/shard_map/ppermute | solution.py:138
  65.2 3.8 %collective-permute-done.32.refs_8_ = bf16[128,256]{1,0:T(8,128)(2,1)S(1)} collective-permute-done((bf16[128,256]{1,0:T(8,128)(2,1)S(1)}, bf16[128,256]{1,0:T(8,128)(2,1)S(1)}, u32[]{:S(2)}, u32[]{:S(2)}) %collective-permute-start.32) | collective-permute-done | bytes 65568 | tf_op jit(solution)/shard_map/ppermute | solution.py:138
  69.1 2.4 %shard_map.79 = bf16[1024,128]{1,0:T(8,128)(2,1)S(1)} custom-call(s32[3]{0:T(128)S(1)} %pad_add_fusion.refs_0_, s32[8,8]{1,0:T(8,128)S(1)} %select_reduce_fusion.2.refs_1_, bf16[4,1024,128]{2,1,0:T(8,128)(2,1)S(1)} %bitcast.51, bf16[4,1024,128]{2,1,0:T(8,128)(2,1)S(1)} %collective-permute-done.refs_3_, f32[8,128]{1,0:T(8,128)S(1)} %bitcast.59, ...), custom_call_target="tpu_custom_call" | custom-call | flops 268435456 | bytes 2097152 | tf_op jit(solution)/shard_map/pallas_call | solution.py:105
  72.2 1.9 %collective-permute-start.15 = (bf16[128,256]{1,0:T(8,128)(2,1)S(1)}, bf16[128,256]{1,0:T(8,128)(2,1)S(1)}, u32[]{:S(2)}, u32[]{:S(2)}) collective-permute-start(bf16[128,256]{1,0:T(8,128)(2,1)S(1)} %get-tuple-element.33), channel_id=1, source_target_pairs={{0,14},{2,12},{4,10},{6,8},{8,6},{10,4},{12,2},{14,0},{1,15},{3,13... | collective-permute-start | bytes 196616 | tf_op jit(solution)/shard_map/ppermute | solution.py:138
  74.1 2.0 %collective-permute-start.13 = (bf16[128,512]{1,0:T(8,128)(2,1)S(1)}, bf16[128,512]{1,0:T(8,128)(2,1)S(1)}, u32[]{:S(2)}, u32[]{:S(2)}) collective-permute-start(bf16[128,512]{1,0:T(8,128)(2,1)S(1)} %collective-permute-done.12.refs_5_), channel_id=1, source_target_pairs={{0,4},{2,6},{4,0},{6,2},{8,12},{10,14},{12,8},{14,10},{1,5},{3,7},... | collective-permute-start | bytes 393224 | tf_op jit(solution)/shard_map/ppermute | solution.py:138
  76.0 1.8 %collective-permute-done.14.refs_7_ = bf16[128,256]{1,0:T(8,128)(2,1)S(1)} collective-permute-done((bf16[128,256]{1,0:T(8,128)(2,1)S(1)}, bf16[128,256]{1,0:T(8,128)(2,1)S(1)}, u32[]{:S(2)}, u32[]{:S(2)}) %collective-permute-start.14) | collective-permute-done | bytes 65568 | tf_op jit(solution)/shard_map/ppermute | solution.py:138
  77.8 1.5 %collective-permute-done.15.refs_8_ = bf16[128,256]{1,0:T(8,128)(2,1)S(1)} collective-permute-done((bf16[128,256]{1,0:T(8,128)(2,1)S(1)}, bf16[128,256]{1,0:T(8,128)(2,1)S(1)}, u32[]{:S(2)}, u32[]{:S(2)}) %collective-permute-start.15) | collective-permute-done | bytes 65568 | tf_op jit(solution)/shard_map/ppermute | solution.py:138
  80.4 1.7 %collective-permute-done.16.refs_9_ = bf16[128,256]{1,0:T(8,128)(2,1)S(1)} collective-permute-done((bf16[128,256]{1,0:T(8,128)(2,1)S(1)}, bf16[128,256]{1,0:T(8,128)(2,1)S(1)}, u32[]{:S(2)}, u32[]{:S(2)}) %collective-permute-start.16) | collective-permute-done | bytes 65568 | tf_op jit(solution)/shard_map/ppermute | solution.py:138
  82.1 2.2 %collective-permute-done.17.refs_10_ = bf16[128,256]{1,0:T(8,128)(2,1)S(1)} collective-permute-done((bf16[128,256]{1,0:T(8,128)(2,1)S(1)}, bf16[128,256]{1,0:T(8,128)(2,1)S(1)}, u32[]{:S(2)}, u32[]{:S(2)}) %collective-permute-start.17) | collective-permute-done | bytes 65568 | tf_op jit(solution)/shard_map/ppermute | solution.py:138
  84.3 2.7 %shard_map.75 = (bf16[128,256]{1,0:T(8,128)(2,1)S(1)}, bf16[128,256]{1,0:T(8,128)(2,1)S(1)}, bf16[128,256]{1,0:T(8,128)(2,1)S(1)}, bf16[128,256]{1,0:T(8,128)(2,1)S(1)}) custom-call(s32[3]{0:T(128)S(1)} %pad_add_fusion.refs_0_, s32[8,16]{1,0:T(8,128)S(1)} %get-tuple-element.50.refs_1_, bf16[4,2048,128]{2,1,0:T(8,128)(2,1)S(1)} %bitcast.47, ...), custom_call_target="tpu_custom_call" | custom-call | flops 536870912 | bytes 4194304 | tf_op jit(solution)/shard_map/pallas_call | solution.py:105
  87.4 1.6 %collective-permute-start.19 = (bf16[128,256]{1,0:T(8,128)(2,1)S(1)}, bf16[128,256]{1,0:T(8,128)(2,1)S(1)}, u32[]{:S(2)}, u32[]{:S(2)}) collective-permute-start(bf16[128,256]{1,0:T(8,128)(2,1)S(1)} %get-tuple-element.36), channel_id=1, source_target_pairs={{0,8},{2,10},{4,12},{6,14},{8,0},{10,2},{12,4},{14,6},{1,9},{3,11}... | collective-permute-start | bytes 196616 | tf_op jit(solution)/shard_map/ppermute | solution.py:138
  89.0 2.4 %collective-permute-start.20 = (bf16[128,256]{1,0:T(8,128)(2,1)S(1)}, bf16[128,256]{1,0:T(8,128)(2,1)S(1)}, u32[]{:S(2)}, u32[]{:S(2)}) collective-permute-start(bf16[128,256]{1,0:T(8,128)(2,1)S(1)} %get-tuple-element.37), channel_id=1, source_target_pairs={{0,12},{2,14},{4,8},{6,10},{8,4},{10,6},{12,0},{14,2},{1,13},{3,15... | collective-permute-start | bytes 196616 | tf_op jit(solution)/shard_map/ppermute | solution.py:138
  92.6 2.5 %collective-permute-done.20.refs_8_ = bf16[128,256]{1,0:T(8,128)(2,1)S(1)} collective-permute-done((bf16[128,256]{1,0:T(8,128)(2,1)S(1)}, bf16[128,256]{1,0:T(8,128)(2,1)S(1)}, u32[]{:S(2)}, u32[]{:S(2)}) %collective-permute-start.20) | collective-permute-done | bytes 65568 | tf_op jit(solution)/shard_map/ppermute | solution.py:138
  95.1 3.0 %shard_map.80 = bf16[1024,128]{1,0:T(8,128)(2,1)} custom-call(s32[3]{0:T(128)S(1)} %pad_add_fusion.refs_0_, s32[8,8]{1,0:T(8,128)S(1)} %select_reduce_fusion.2.refs_1_, bf16[4,1024,128]{2,1,0:T(8,128)(2,1)S(1)} %bitcast.52, bf16[4,1024,128]{2,1,0:T(8,128)(2,1)S(1)} %collective-permute-done.refs_3_, f32[8,128]{1,0:T(8,128)S(1)} %bitcast.60, ...), custom_call_target="tpu_custom_call" | custom-call | flops 268435456 | bytes 2097152 | tf_op jit(solution)/shard_map/pallas_call | solution.py:105
  (71 shorter events, 17.8 us)
Async XLA Ops:
  0.0 17.2 %collective-permute-start.1 = (bf16[4,2048,128]{2,1,0:T(8,128)(2,1)}, bf16[4,2048,128]{2,1,0:T(8,128)(2,1)S(1)}, u32[]{:S(2)}, u32[]{:S(2)}) collective-permute-start(bf16[4,2048,128]{2,1,0:T(8,128)(2,1)} %bitcast.43), channel_id=1, source_target_pairs={{0,1},{1,0},{2,3},{3,2},{4,5},{5,4},{6,7},{7,6},{8,9},{9,8},{10,11... | collective-permute-start | bytes 6291464 | tf_op jit(solution)/shard_map/ppermute | solution.py:141
  1.6 13.5 %collective-permute-start.7 = (bf16[512,128]{1,0:T(8,128)(2,1)}, bf16[512,128]{1,0:T(8,128)(2,1)S(1)}, u32[]{:S(2)}, u32[]{:S(2)}) collective-permute-start(bf16[512,128]{1,0:T(8,128)(2,1)} %pad_maximum_fusion.1), channel_id=1, source_target_pairs={{0,12},{2,14},{4,8},{6,10},{8,4},{10,6},{12,0},{14,2},{1,13},{3,15... | collective-permute-start | bytes 393224 | tf_op jit(solution)/shard_map/ppermute | solution.py:138
  5.2 12.0 %collective-permute-start.5 = (bf16[512,128]{1,0:T(8,128)(2,1)}, bf16[512,128]{1,0:T(8,128)(2,1)S(1)}, u32[]{:S(2)}, u32[]{:S(2)}) collective-permute-start(bf16[512,128]{1,0:T(8,128)(2,1)} %pad_maximum_fusion.1), channel_id=1, source_target_pairs={{0,8},{2,10},{4,12},{6,14},{8,0},{10,2},{12,4},{14,6},{1,9},{3,11}... | collective-permute-start | bytes 393224 | tf_op jit(solution)/shard_map/ppermute | solution.py:138
  5.2 9.3 %collective-permute-start.3 = (bf16[512,128]{1,0:T(8,128)(2,1)S(1)}, bf16[512,128]{1,0:T(8,128)(2,1)}, u32[]{:S(2)}, u32[]{:S(2)}) collective-permute-start(bf16[512,128]{1,0:T(8,128)(2,1)S(1)} %pad_maximum_fusion.refs_5_), channel_id=1, source_target_pairs={{0,4},{2,6},{4,0},{6,2},{8,12},{10,14},{12,8},{14,10},{1,5},{3,7},... | collective-permute-start | bytes 393224 | tf_op jit(solution)/shard_map/ppermute | solution.py:138
  6.1 20.4 %collective-permute-start = (bf16[4,1024,128]{2,1,0:T(8,128)(2,1)}, bf16[4,1024,128]{2,1,0:T(8,128)(2,1)S(1)}, u32[]{:S(2)}, u32[]{:S(2)}) collective-permute-start(bf16[4,1024,128]{2,1,0:T(8,128)(2,1)} %bitcast.48), channel_id=1, source_target_pairs={{0,1},{1,0},{2,3},{3,2},{4,5},{5,4},{6,7},{7,6},{8,9},{9,8},{10,11... | collective-permute-start | bytes 3145736 | tf_op jit(solution)/shard_map/ppermute | solution.py:141
  14.6 24.2 %collective-permute-start.2 = (bf16[512,128]{1,0:T(8,128)(2,1)S(1)}, bf16[512,128]{1,0:T(8,128)(2,1)S(1)}, u32[]{:S(2)}, u32[]{:S(2)}) collective-permute-start(bf16[512,128]{1,0:T(8,128)(2,1)S(1)} %pad_maximum_fusion.refs_5_), channel_id=1, source_target_pairs={{0,2},{2,0},{4,6},{6,4},{8,10},{10,8},{12,14},{14,12},{1,3},{3,1},... | collective-permute-start | bytes 393224 | tf_op jit(solution)/shard_map/ppermute | solution.py:138
  20.6 6.1 %collective-permute-start.21 = (bf16[128,256]{1,0:T(8,128)(2,1)S(1)}, bf16[128,256]{1,0:T(8,128)(2,1)S(1)}, u32[]{:S(2)}, u32[]{:S(2)}) collective-permute-start(bf16[128,256]{1,0:T(8,128)(2,1)S(1)} %get-tuple-element.39), channel_id=1, source_target_pairs={{0,4},{2,6},{4,0},{6,2},{8,12},{10,14},{12,8},{14,10},{1,5},{3,7},... | collective-permute-start | bytes 196616 | tf_op jit(solution)/shard_map/ppermute | solution.py:138
  21.1 7.4 %collective-permute-start.22 = (bf16[128,256]{1,0:T(8,128)(2,1)S(1)}, bf16[128,256]{1,0:T(8,128)(2,1)S(1)}, u32[]{:S(2)}, u32[]{:S(2)}) collective-permute-start(bf16[128,256]{1,0:T(8,128)(2,1)S(1)} %get-tuple-element.40), channel_id=1, source_target_pairs={{0,8},{2,10},{4,12},{6,14},{8,0},{10,2},{12,4},{14,6},{1,9},{3,11}... | collective-permute-start | bytes 196616 | tf_op jit(solution)/shard_map/ppermute | solution.py:138
  23.7 15.1 %collective-permute-start.4 = (bf16[512,128]{1,0:T(8,128)(2,1)}, bf16[512,128]{1,0:T(8,128)(2,1)S(1)}, u32[]{:S(2)}, u32[]{:S(2)}) collective-permute-start(bf16[512,128]{1,0:T(8,128)(2,1)} %collective-permute-done.3.refs_6_), channel_id=1, source_target_pairs={{0,2},{2,0},{4,6},{6,4},{8,10},{10,8},{12,14},{14,12},{1,3},{3,1},... | collective-permute-start | bytes 393224 | tf_op jit(solution)/shard_map/ppermute | solution.py:138
  26.5 12.3 %collective-permute-start.8 = (bf16[512,128]{1,0:T(8,128)(2,1)S(1)}, bf16[512,128]{1,0:T(8,128)(2,1)S(1)}, u32[]{:S(2)}, u32[]{:S(2)}) collective-permute-start(bf16[512,128]{1,0:T(8,128)(2,1)S(1)} %collective-permute-done.7.refs_8_), channel_id=1, source_target_pairs={{0,2},{2,0},{4,6},{6,4},{8,10},{10,8},{12,14},{14,12},{1,3},{3,1},... | collective-permute-start | bytes 393224 | tf_op jit(solution)/shard_map/ppermute | solution.py:138
  26.6 12.2 %collective-permute-start.6 = (bf16[512,128]{1,0:T(8,128)(2,1)S(1)}, bf16[512,128]{1,0:T(8,128)(2,1)S(1)}, u32[]{:S(2)}, u32[]{:S(2)}) collective-permute-start(bf16[512,128]{1,0:T(8,128)(2,1)S(1)} %collective-permute-done.5.refs_7_), channel_id=1, source_target_pairs={{0,2},{2,0},{4,6},{6,4},{8,10},{10,8},{12,14},{14,12},{1,3},{3,1},... | collective-permute-start | bytes 393224 | tf_op jit(solution)/shard_map/ppermute | solution.py:138
  28.6 6.1 %collective-permute-start.23 = (bf16[128,256]{1,0:T(8,128)(2,1)S(1)}, bf16[128,256]{1,0:T(8,128)(2,1)S(1)}, u32[]{:S(2)}, u32[]{:S(2)}) collective-permute-start(bf16[128,256]{1,0:T(8,128)(2,1)S(1)} %get-tuple-element.41), channel_id=1, source_target_pairs={{0,12},{2,14},{4,8},{6,10},{8,4},{10,6},{12,0},{14,2},{1,13},{3,15... | collective-permute-start | bytes 196616 | tf_op jit(solution)/shard_map/ppermute | solution.py:138
  35.3 9.6 %collective-permute-start.24 = (bf16[128,512]{1,0:T(8,128)(2,1)S(1)}, bf16[128,512]{1,0:T(8,128)(2,1)S(1)}, u32[]{:S(2)}, u32[]{:S(2)}) collective-permute-start(bf16[128,512]{1,0:T(8,128)(2,1)S(1)} %get-tuple-element.42), channel_id=1, source_target_pairs={{0,2},{2,0},{4,6},{6,4},{8,10},{10,8},{12,14},{14,12},{1,3},{3,1},... | collective-permute-start | bytes 393224 | tf_op jit(solution)/shard_map/ppermute | solution.py:138
  39.5 6.9 %collective-permute-start.9 = (bf16[128,256]{1,0:T(8,128)(2,1)S(1)}, bf16[128,256]{1,0:T(8,128)(2,1)S(1)}, u32[]{:S(2)}, u32[]{:S(2)}) collective-permute-start(bf16[128,256]{1,0:T(8,128)(2,1)S(1)} %get-tuple-element.28), channel_id=1, source_target_pairs={{0,4},{2,6},{4,0},{6,2},{8,12},{10,14},{12,8},{14,10},{1,5},{3,7},... | collective-permute-start | bytes 196616 | tf_op jit(solution)/shard_map/ppermute | solution.py:138
  39.6 9.7 %collective-permute-start.26 = (bf16[128,256]{1,0:T(8,128)(2,1)S(1)}, bf16[128,256]{1,0:T(8,128)(2,1)S(1)}, u32[]{:S(2)}, u32[]{:S(2)}) collective-permute-start(bf16[128,256]{1,0:T(8,128)(2,1)S(1)} %get-tuple-element.43), channel_id=1, source_target_pairs={{0,10},{2,8},{4,14},{6,12},{8,2},{10,0},{12,6},{14,4},{1,11},{3,9}... | collective-permute-start | bytes 196616 | tf_op jit(solution)/shard_map/ppermute | solution.py:138
  42.8 7.7 %collective-permute-start.27 = (bf16[128,256]{1,0:T(8,128)(2,1)S(1)}, bf16[128,256]{1,0:T(8,128)(2,1)S(1)}, u32[]{:S(2)}, u32[]{:S(2)}) collective-permute-start(bf16[128,256]{1,0:T(8,128)(2,1)S(1)} %get-tuple-element.44), channel_id=1, source_target_pairs={{0,14},{2,12},{4,10},{6,8},{8,6},{10,4},{12,2},{14,0},{1,15},{3,13... | collective-permute-start | bytes 196616 | tf_op jit(solution)/shard_map/ppermute | solution.py:138
  44.9 12.0 %collective-permute-start.25 = (bf16[128,512]{1,0:T(8,128)(2,1)S(1)}, bf16[128,512]{1,0:T(8,128)(2,1)S(1)}, u32[]{:S(2)}, u32[]{:S(2)}) collective-permute-start(bf16[128,512]{1,0:T(8,128)(2,1)S(1)} %collective-permute-done.24.refs_5_), channel_id=1, source_target_pairs={{0,4},{2,6},{4,0},{6,2},{8,12},{10,14},{12,8},{14,10},{1,5},{3,7},... | collective-permute-start | bytes 393224 | tf_op jit(solution)/shard_map/ppermute | solution.py:138
  44.9 6.5 %collective-permute-start.10 = (bf16[128,256]{1,0:T(8,128)(2,1)S(1)}, bf16[128,256]{1,0:T(8,128)(2,1)S(1)}, u32[]{:S(2)}, u32[]{:S(2)}) collective-permute-start(bf16[128,256]{1,0:T(8,128)(2,1)S(1)} %get-tuple-element.29), channel_id=1, source_target_pairs={{0,8},{2,10},{4,12},{6,14},{8,0},{10,2},{12,4},{14,6},{1,9},{3,11}... | collective-permute-start | bytes 196616 | tf_op jit(solution)/shard_map/ppermute | solution.py:138
  46.4 6.5 %collective-permute-start.11 = (bf16[128,256]{1,0:T(8,128)(2,1)S(1)}, bf16[128,256]{1,0:T(8,128)(2,1)S(1)}, u32[]{:S(2)}, u32[]{:S(2)}) collective-permute-start(bf16[128,256]{1,0:T(8,128)(2,1)S(1)} %get-tuple-element.30), channel_id=1, source_target_pairs={{0,12},{2,14},{4,8},{6,10},{8,4},{10,6},{12,0},{14,2},{1,13},{3,15... | collective-permute-start | bytes 196616 | tf_op jit(solution)/shard_map/ppermute | solution.py:138
  49.2 7.6 %collective-permute-start.28 = (bf16[128,256]{1,0:T(8,128)(2,1)S(1)}, bf16[128,256]{1,0:T(8,128)(2,1)S(1)}, u32[]{:S(2)}, u32[]{:S(2)}) collective-permute-start(bf16[128,256]{1,0:T(8,128)(2,1)S(1)} %collective-permute-done.26.refs_7_), channel_id=1, source_target_pairs={{0,4},{2,6},{4,0},{6,2},{8,12},{10,14},{12,8},{14,10},{1,5},{3,7},... | collective-permute-start | bytes 196616 | tf_op jit(solution)/shard_map/ppermute | solution.py:138
  50.5 6.4 %collective-permute-start.29 = (bf16[128,256]{1,0:T(8,128)(2,1)S(1)}, bf16[128,256]{1,0:T(8,128)(2,1)S(1)}, u32[]{:S(2)}, u32[]{:S(2)}) collective-permute-start(bf16[128,256]{1,0:T(8,128)(2,1)S(1)} %collective-permute-done.27.refs_8_), channel_id=1, source_target_pairs={{0,4},{2,6},{4,0},{6,2},{8,12},{10,14},{12,8},{14,10},{1,5},{3,7},... | collective-permute-start | bytes 196616 | tf_op jit(solution)/shard_map/ppermute | solution.py:138
  53.6 20.5 %collective-permute-start.12 = (bf16[128,512]{1,0:T(8,128)(2,1)S(1)}, bf16[128,512]{1,0:T(8,128)(2,1)S(1)}, u32[]{:S(2)}, u32[]{:S(2)}) collective-permute-start(bf16[128,512]{1,0:T(8,128)(2,1)S(1)} %get-tuple-element.31), channel_id=1, source_target_pairs={{0,2},{2,0},{4,6},{6,4},{8,10},{10,8},{12,14},{14,12},{1,3},{3,1},... | collective-permute-start | bytes 393224 | tf_op jit(solution)/shard_map/ppermute | solution.py:138
  59.6 4.5 %collective-permute-start.30 = (bf16[128,256]{1,0:T(8,128)(2,1)S(1)}, bf16[128,256]{1,0:T(8,128)(2,1)S(1)}, u32[]{:S(2)}, u32[]{:S(2)}) collective-permute-start(bf16[128,256]{1,0:T(8,128)(2,1)S(1)} %get-tuple-element.46), channel_id=1, source_target_pairs={{0,4},{2,6},{4,0},{6,2},{8,12},{10,14},{12,8},{14,10},{1,5},{3,7},... | collective-permute-start | bytes 196616 | tf_op jit(solution)/shard_map/ppermute | solution.py:138
  59.7 5.6 %collective-permute-start.31 = (bf16[128,256]{1,0:T(8,128)(2,1)S(1)}, bf16[128,256]{1,0:T(8,128)(2,1)S(1)}, u32[]{:S(2)}, u32[]{:S(2)}) collective-permute-start(bf16[128,256]{1,0:T(8,128)(2,1)S(1)} %get-tuple-element.47), channel_id=1, source_target_pairs={{0,8},{2,10},{4,12},{6,14},{8,0},{10,2},{12,4},{14,6},{1,9},{3,11}... | collective-permute-start | bytes 196616 | tf_op jit(solution)/shard_map/ppermute | solution.py:138
  63.0 6.1 %collective-permute-start.32 = (bf16[128,256]{1,0:T(8,128)(2,1)S(1)}, bf16[128,256]{1,0:T(8,128)(2,1)S(1)}, u32[]{:S(2)}, u32[]{:S(2)}) collective-permute-start(bf16[128,256]{1,0:T(8,128)(2,1)S(1)} %get-tuple-element.48), channel_id=1, source_target_pairs={{0,12},{2,14},{4,8},{6,10},{8,4},{10,6},{12,0},{14,2},{1,13},{3,15... | collective-permute-start | bytes 196616 | tf_op jit(solution)/shard_map/ppermute | solution.py:138
  71.5 23.6 %collective-permute-start.33 = (bf16[1024,128]{1,0:T(8,128)(2,1)S(1)}, bf16[1024,128]{1,0:T(8,128)(2,1)S(1)}, u32[]{:S(2)}, u32[]{:S(2)}) collective-permute-start(bf16[1024,128]{1,0:T(8,128)(2,1)S(1)} %shard_map.79), channel_id=1, source_target_pairs={{0,2},{2,0},{4,6},{6,4},{8,10},{10,8},{12,14},{14,12},{1,3},{3,1},... | collective-permute-start | bytes 786440 | tf_op jit(solution)/shard_map/ppermute | solution.py:138
  71.6 6.2 %collective-permute-start.14 = (bf16[128,256]{1,0:T(8,128)(2,1)S(1)}, bf16[128,256]{1,0:T(8,128)(2,1)S(1)}, u32[]{:S(2)}, u32[]{:S(2)}) collective-permute-start(bf16[128,256]{1,0:T(8,128)(2,1)S(1)} %get-tuple-element.32), channel_id=1, source_target_pairs={{0,10},{2,8},{4,14},{6,12},{8,2},{10,0},{12,6},{14,4},{1,11},{3,9}... | collective-permute-start | bytes 196616 | tf_op jit(solution)/shard_map/ppermute | solution.py:138
  72.2 7.1 %collective-permute-start.15 = (bf16[128,256]{1,0:T(8,128)(2,1)S(1)}, bf16[128,256]{1,0:T(8,128)(2,1)S(1)}, u32[]{:S(2)}, u32[]{:S(2)}) collective-permute-start(bf16[128,256]{1,0:T(8,128)(2,1)S(1)} %get-tuple-element.33), channel_id=1, source_target_pairs={{0,14},{2,12},{4,10},{6,8},{8,6},{10,4},{12,2},{14,0},{1,15},{3,13... | collective-permute-start | bytes 196616 | tf_op jit(solution)/shard_map/ppermute | solution.py:138
  74.1 10.3 %collective-permute-start.13 = (bf16[128,512]{1,0:T(8,128)(2,1)S(1)}, bf16[128,512]{1,0:T(8,128)(2,1)S(1)}, u32[]{:S(2)}, u32[]{:S(2)}) collective-permute-start(bf16[128,512]{1,0:T(8,128)(2,1)S(1)} %collective-permute-done.12.refs_5_), channel_id=1, source_target_pairs={{0,4},{2,6},{4,0},{6,2},{8,12},{10,14},{12,8},{14,10},{1,5},{3,7},... | collective-permute-start | bytes 393224 | tf_op jit(solution)/shard_map/ppermute | solution.py:138
  79.3 5.0 %collective-permute-start.17 = (bf16[128,256]{1,0:T(8,128)(2,1)S(1)}, bf16[128,256]{1,0:T(8,128)(2,1)S(1)}, u32[]{:S(2)}, u32[]{:S(2)}) collective-permute-start(bf16[128,256]{1,0:T(8,128)(2,1)S(1)} %collective-permute-done.15.refs_8_), channel_id=1, source_target_pairs={{0,4},{2,6},{4,0},{6,2},{8,12},{10,14},{12,8},{14,10},{1,5},{3,7},... | collective-permute-start | bytes 196616 | tf_op jit(solution)/shard_map/ppermute | solution.py:138
  87.4 5.2 %collective-permute-start.19 = (bf16[128,256]{1,0:T(8,128)(2,1)S(1)}, bf16[128,256]{1,0:T(8,128)(2,1)S(1)}, u32[]{:S(2)}, u32[]{:S(2)}) collective-permute-start(bf16[128,256]{1,0:T(8,128)(2,1)S(1)} %get-tuple-element.36), channel_id=1, source_target_pairs={{0,8},{2,10},{4,12},{6,14},{8,0},{10,2},{12,4},{14,6},{1,9},{3,11}... | collective-permute-start | bytes 196616 | tf_op jit(solution)/shard_map/ppermute | solution.py:138
  89.0 6.1 %collective-permute-start.20 = (bf16[128,256]{1,0:T(8,128)(2,1)S(1)}, bf16[128,256]{1,0:T(8,128)(2,1)S(1)}, u32[]{:S(2)}, u32[]{:S(2)}) collective-permute-start(bf16[128,256]{1,0:T(8,128)(2,1)S(1)} %get-tuple-element.37), channel_id=1, source_target_pairs={{0,12},{2,14},{4,8},{6,10},{8,4},{10,6},{12,0},{14,2},{1,13},{3,15... | collective-permute-start | bytes 196616 | tf_op jit(solution)/shard_map/ppermute | solution.py:138
  (9 other events, 82.1 us)

commit v2 on v0

--- a/solution.py
+++ b/solution.py
@@ -1,9 +1,178 @@
+import functools
+
 import jax
 import jax.numpy as jnp
 from jax import lax
+from jax.experimental import pallas as pl
+from jax.experimental.pallas import tpu as pltpu
 from jax.sharding import PartitionSpec as P
 
 CEILING = 4.0
+
+
+def order_kernel(links, own_tiles, other_tiles, bias, ordered, shifts):
+    owner_count = ordered.shape[0]
+    me, rep = lax.axis_index("owners"), lax.axis_index("rep")
+    half, _, size = own_tiles.shape
+    slots = links.shape[1]
+    width = 2 * size
+    for ours, source in ((True, own_tiles), (False, other_tiles)):
+        first = (rep if ours else 1 - rep) * half
+        for block in range(half):
+            row = first + block
+            distance = (row // 2) ^ me
+            for slot in range(slots):
+                place = links[row, slot]
+                sender = ((place // 2) & (owner_count - 1)) ^ me
+                if slots > 2 * owner_count:
+                    part = (place // (2 * owner_count)) ^ (me & 1)
+                    key = 2 * sender + part
+                else:
+                    key = sender
+                low = pl.multiple_of(key * width + (place & 1) * size, size)
+                ordered[distance, pl.ds(low, size), pl.ds(block % 2 * size, size)] = source[
+                    block, pl.ds(slot * size, size), :
+                ]
+    for distance in range(owner_count):
+        for j in range(2):
+            shifts[pl.ds(distance, 1), pl.ds(j * size, size)] = bias[pl.ds(2 * (me ^ distance) + j, 1), :]
+
+
+def order_weights(links, own_tiles, other_tiles, bias):
+    half, depth, size = own_tiles.shape
+    vmem = pl.BlockSpec(memory_space=pltpu.VMEM)
+    return pl.pallas_call(
+        order_kernel,
+        out_shape=[
+            jax.ShapeDtypeStruct((half, depth, 2 * size), jnp.bfloat16),
+            jax.ShapeDtypeStruct((half, 2 * size), jnp.float32),
+        ],
+        in_specs=[pl.BlockSpec(memory_space=pltpu.SMEM), vmem, vmem, vmem],
+        out_specs=[vmem, vmem],
+        compiler_params=pltpu.CompilerParams(vmem_limit_bytes=24 * 2**20),
+        cost_estimate=pl.CostEstimate(flops=1, bytes_accessed=1, transcendentals=0),
+    )(links, own_tiles, other_tiles, bias)
+
+
+def layer_kernel(tile_list, out_groups, raw, final, active_section, *refs):
+    ordered, shifts = refs[:2]
+    buffer_count = 1 + max(buffer for buffer, _, _ in tile_list)
+    buffers = refs[2 : 2 + buffer_count]
+    rest = list(refs[2 + buffer_count :])
+    settled = rest.pop(0) if final == "merge" else None
+    out_count = 1 if final else len(out_groups)
+    outs = rest[:out_count]
+    turned = rest[out_count] if raw else None
+    section = lax.axis_index("section")
+    me = lax.axis_index("owners")
+    width = ordered.shape[2]
+
+    def run():
+        if raw:
+            for place, (buffer, column, _) in enumerate(tile_list):
+                turned[place] = buffers[buffer][pl.ds(column, width), :].T
+        for distance in reversed(range(ordered.shape[0])):
+            total = shifts[pl.ds(distance, 1), :]
+            for place, (buffer, column, key) in enumerate(tile_list):
+                left = turned[place] if raw else buffers[buffer][:, pl.ds(column, width)]
+                if raw:
+                    key = (key & ~1) + ((key & 1) ^ (me & 1))
+                low = pl.multiple_of(key * width, width) if raw else key * width
+                right = ordered[distance, pl.ds(low, width), :]
+                total = total + jnp.dot(left, right, preferred_element_type=jnp.float32)
+            value = jnp.clip(total, 0.0, CEILING).astype(jnp.bfloat16)
+            if final:
+                outs[0][pl.ds(pl.multiple_of((me ^ distance) * width, width), width), :] = value.T
+            else:
+                for out, group in zip(outs, out_groups, strict=True):
+                    if distance in group:
+                        out[:, pl.ds(group.index(distance) * width, width)] = value
+
+    pl.when(section == active_section)(run)
+    if final == "merge":
+
+        @pl.when(section != active_section)
+        def _():
+            outs[0][...] = settled[...]
+
+
+def layer(ordered, shifts, buffers, tile_list, out_groups, active_section, raw=False, final=None, settled=None):
+    count, depth, width = ordered.shape
+    rows = buffers[0].shape[1] if raw else buffers[0].shape[0]
+    if final:
+        shapes = [jax.ShapeDtypeStruct((count * width, rows), jnp.bfloat16)]
+    else:
+        shapes = [jax.ShapeDtypeStruct((rows, len(group) * width), jnp.bfloat16) for group in out_groups]
+    vmem = pl.BlockSpec(memory_space=pltpu.VMEM)
+    operands = [ordered, shifts, *buffers] + ([settled] if final == "merge" else [])
+    return pl.pallas_call(
+        functools.partial(layer_kernel, tile_list, out_groups, raw, final, active_section),
+        out_shape=shapes,
+        in_specs=[vmem] * len(operands),
+        out_specs=[vmem] * len(shapes),
+        scratch_shapes=[pltpu.VMEM((len(tile_list), rows, width), jnp.bfloat16)] if raw else [],
+        compiler_params=pltpu.CompilerParams(vmem_limit_bytes=16 * 2**20),
+        cost_estimate=pl.CostEstimate(flops=1, bytes_accessed=1, transcendentals=0),
+    )(*operands)
+
+
+def fast_body(inputs, weight_first, weight_second, bias_first, bias_second, links_first, links_second):
+    owner_count = lax.axis_size("owners")
+    me = lax.axis_index("owners")
+    size = weight_first.shape[3]
+    features = inputs[0]
+    piece = features.shape[0] // owner_count
+
+    def moved(value, distance, cross):
+        pairs = []
+        for owner in range(owner_count):
+            for place in range(2):
+                target = (owner ^ distance) * 2 + (1 - place if cross else place)
+                pairs.append((owner * 2 + place, target))
+        return lax.ppermute(value, ("owners", "section"), pairs)
+
+    def other_core(value):
+        return lax.ppermute(value, "rep", [(0, 1), (1, 0)])
+
+    halves = features.reshape(2, 2 * piece, features.shape[1])
+    near = lax.dynamic_index_in_dim(halves, me // 2, 0, keepdims=False)
+    far = lax.dynamic_index_in_dim(halves, 1 - me // 2, 0, keepdims=False)
+    three, two, one = moved(far, 3, False), moved(far, 2, False), moved(near, 1, False)
+    start = [near, one, two, three]
+    first_own, second_own = weight_first[0], weight_second[0]
+    first = order_weights(links_first[0], first_own, other_core(first_own), bias_first[0].reshape(-1, size))
+    second = order_weights(links_second[0], second_own, other_core(second_own), bias_second[0].reshape(-1, size))
+
+    raw_tiles = [(buffer, column * piece, 2 * buffer + column) for buffer in range(4) for column in range(2)]
+    relayed = [(0, 0), (0, 1), (1, 1), (1, 0), (2, 0), (3, 0), (3, 1), (2, 1)]
+    relayed_spots = [(0, 0), (0, piece), (1, 0), (1, piece), (2, 0), (3, 0), (4, 0), (5, 0)]
+    relayed_tiles = [
+        (*spot, 2 * sender + part) for spot, (sender, part) in zip(relayed_spots, relayed, strict=True)
+    ]
+    second_tiles = [(buffer, 0, buffer) for buffer in range(4)]
+
+    apart = [[0], [1], [2], [3]]
+    joined = [[0, 1], [2], [3]]
+
+    def first_layer(buffers, active, raw):
+        return layer(*first, buffers, raw_tiles if raw else relayed_tiles, apart, active, raw=raw)
+
+    def second_layer(parts, active, **more):
+        arrived = [moved(parts[distance], distance, False) for distance in (3, 2, 1)]
+        return layer(*second, [parts[0], *arrived[::-1]], second_tiles, joined, active, **more)
+
+    def hand_over(result):
+        close, far_two, far_three = result
+        two, three = moved(far_two, 2, True), moved(far_three, 3, True)
+        close = moved(close, 0, True)
+        return [close, moved(close, 1, False), two, three, moved(two, 1, False), moved(three, 1, False)]
+
+    later = [moved(value, 0, True) for value in start]
+    zero = second_layer(first_layer(start, 0, True), 0)
+    one = second_layer(first_layer(later, 0, True), 0)
+    settled = second_layer(first_layer(hand_over(zero), 1, False), 1, final="plain")[0]
+    settled = moved(settled, 0, True)
+    return second_layer(first_layer(hand_over(one), 1, False), 1, final="merge", settled=settled)[0][None]
 
 
 def from_behind(value, axis, steps):
@@ -51,7 +220,7 @@
     return from_behind(slot_store, "section", 1)
 
 
-def body(inputs, weight_first, weight_second, bias_first, bias_second, links_first, links_second):
+def general_body(inputs, weight_first, weight_second, bias_first, bias_second, links_first, links_second):
     section_count = lax.axis_size("section")
     section_here = lax.axis_index("section")
     owner_parity = lax.axis_index("owners") % 2
@@ -99,6 +268,22 @@
     return slot_store[None]
 
 
+def body(*arrays):
+    inputs, weight_first = arrays[:2]
+    owner_count = lax.axis_size("owners")
+    size = weight_first.shape[3]
+    width = inputs.shape[1]
+    fits = (
+        lax.axis_size("section") == 2
+        and lax.axis_size("rep") == 2
+        and owner_count == 4
+        and width == 2 * size * owner_count
+        and weight_first.shape[2] == 2 * width
+        and arrays[2].shape[2] == width
+    )
+    return fast_body(*arrays) if fits else general_body(*arrays)
+
+
 def solution(mesh):
     placed = (
         P("section", "owners", ("groups", "rep")),

time: 176 us -> 87.6 us (0.50)
  blocking collectives: 23.6 us -> 0 us
  waiting for transfers between devices: 53.3 us -> 33 us
  other arithmetic: 16.8 us -> 0 us
  between operations: 13.6 us -> 0.12 us
  local copies, waits for them, and re-layouts: 16.6 us -> 3.96 us
  matrix products: 11.5 us -> 0 us
  Pallas kernels: 0 us -> 7.45 us
  starting transfers between devices: 38.9 us -> 42.4 us
    all_to_all x2 -> x0, blocking collectives: 23.6 us -> none  [body(): lax.all_to_all(incoming, 'owners', split_axis=0, concat_axis=0, tiled=True)]
    ppermute x9 -> x34, starting transfers between devices: 22 us -> 42.4 us  [the longest x32 41.9 us: moved(): return lax.ppermute(value, ('owners', 'section'), pairs)]
    all_to_all x4 -> x0, starting transfers between devices: 16.9 us -> none  [the longest x3 10.6 us: body(): lax.all_to_all(middle, 'owners', split_axis=0, concat_axis=0, tiled=True)]
    all_to_all x4 -> x0, waiting for transfers between devices: 14.7 us -> none  [the longest x3 9.06 us: body(): lax.all_to_all(middle, 'owners', split_axis=0, concat_axis=0, tiled=True)]
    select_n x9 -> x0, other arithmetic: 13.5 us -> none  [the longest x2 12.5 us: order_tiles(): ordered = jnp.take_along_axis(shaped, inverse[:, :, None, None], axis=1)]
    dot_general x4 -> x0, matrix products: 11.5 us -> none  [mixed_layer(): jnp.einsum('bkc,kr->bcr', ordered, group_rows, preferred_element_type=jnp...]
    gather x6 -> x0, local copies, waits for them, and re-layouts: 9.4 us -> none  [order_tiles(): ordered = jnp.take_along_axis(shaped, inverse[:, :, None, None], axis=1)]
    pallas_call x0 -> x10, Pallas kernels: none -> 7.45 us  [the longest x2 4.28 us: order_weights(): pl.pallas_call(order_kernel, out_shape=[jax.ShapeDtypeStruct((half, depth...]
  transfers between devices with their start and end apart: 15 -> 34, of which waited for: 11 -> 18; matrix products, arithmetic and copies ran while one was open for 19% -> 1% of each run, Pallas kernels for 0% -> 8%
where the time goes in v2:
time: 87.6 us; the launch traced here: 86.9 us
  starting transfers between devices  42.4 us (48%)
  waiting for transfers between devices  33 us (38%)
  Pallas kernels  7.45 us (9%)
  local copies, waits for them, and re-layouts  3.96 us (5%)
    ppermute x32, starting transfers between devices, moved(): return lax.ppermute(value, ('owners', 'section'), pairs)  41.9 us
    ppermute x32, waiting for transfers between devices, moved(): return lax.ppermute(value, ('owners', 'section'), pairs)  33 us
    pallas_call x2, Pallas kernels, order_weights(): pl.pallas_call(order_kernel, out_shape=[jax.ShapeDtypeStruct((half, depth...  4.28 us
    pallas_call x8, Pallas kernels, layer(): pl.pallas_call(functools.partial(layer_kernel, tile_list, out_groups, raw...  3.17 us
    unnamed x12, local copies, waits for them, and re-layouts  2.97 us
  transfers between devices with their start and end apart: 34, of which 18 were waited for; matrix products, arithmetic and copies ran while one was open for 1% of the time, Pallas kernels for 8%

profile of v2, /device:TPU:0, one launch (start us, length us, event | category | flops | bytes accessed | tf_op | source)
XLA Modules:
  0.0 86.9 jit_solution(15105036651966164537)
XLA Ops:
  1.5 3.1 %collective-permute-start.3 = (bf16[512,128]{1,0:T(8,128)(2,1)S(1)}, bf16[512,128]{1,0:T(8,128)(2,1)S(1)}, u32[]{:S(2)}, u32[]{:S(2)}) collective-permute-start(bf16[512,128]{1,0:T(8,128)(2,1)S(1)} %get-tuple-element.58.refs_2_), channel_id=1, source_target_pairs={{0,4},{2,6},{4,0},{6,2},{8,12},{10,14},{12,8},{14,10},{1,5},{3,7},... | collective-permute-start | bytes 393224 | tf_op jit(solution)/shard_map/ppermute | solution.py:132
  4.6 2.6 %collective-permute-start.5 = (bf16[512,128]{1,0:T(8,128)(2,1)S(1)}, bf16[512,128]{1,0:T(8,128)(2,1)S(1)}, u32[]{:S(2)}, u32[]{:S(2)}) collective-permute-start(bf16[512,128]{1,0:T(8,128)(2,1)S(1)} %get-tuple-element.57), channel_id=1, source_target_pairs={{0,8},{2,10},{4,12},{6,14},{8,0},{10,2},{12,4},{14,6},{1,9},{3,11}... | collective-permute-start | bytes 393224 | tf_op jit(solution)/shard_map/ppermute | solution.py:132
  7.2 1.6 %copy-done = bf16[1,4,2048,128]{3,2,1,0:T(8,128)(2,1)S(1)} copy-done((bf16[1,4,2048,128]{3,2,1,0:T(8,128)(2,1)S(1)}, bf16[1,4,2048,128]{3,2,1,0:T(8,128)(2,1)}, u32[]{:S(2)}) %copy-start) | copy-done | bytes 2097176
  10.2 2.8 %shard_map.74 = (bf16[4,2048,256]{2,1,0:T(8,128)(2,1)S(1)}, f32[4,256]{1,0:T(4,128)S(1)}) custom-call(s32[8,16]{1,0:T(8,128)S(1)} %bitcast.18, bf16[4,2048,128]{2,1,0:T(8,128)(2,1)S(1)} %bitcast.13, bf16[4,2048,128]{2,1,0:T(8,128)(2,1)S(1)} %collective-permute-done.1.other_tiles, f32[8,128]{1,0:T(8,128)S(1)} %bitcast.19), custom_call_target="tpu_custom_call" | custom-call | flops 1 | bytes 1 | tf_op jit(solution)/shard_map/pallas_call | solution.py:44
  13.0 4.6 %collective-permute-done.5.refs_4_ = bf16[512,128]{1,0:T(8,128)(2,1)S(1)} collective-permute-done((bf16[512,128]{1,0:T(8,128)(2,1)S(1)}, bf16[512,128]{1,0:T(8,128)(2,1)S(1)}, u32[]{:S(2)}, u32[]{:S(2)}) %collective-permute-start.5) | collective-permute-done | bytes 131104 | tf_op jit(solution)/shard_map/ppermute | solution.py:132
  18.3 2.2 %collective-permute-start.21 = (bf16[128,256]{1,0:T(8,128)(2,1)S(1)}, bf16[128,256]{1,0:T(8,128)(2,1)S(1)}, u32[]{:S(2)}, u32[]{:S(2)}) collective-permute-start(bf16[128,256]{1,0:T(8,128)(2,1)S(1)} %get-tuple-element.47), channel_id=1, source_target_pairs={{0,4},{2,6},{4,0},{6,2},{8,12},{10,14},{12,8},{14,10},{1,5},{3,7},... | collective-permute-start | bytes 196616 | tf_op jit(solution)/shard_map/ppermute | solution.py:132
  21.6 1.4 %collective-permute-start.23 = (bf16[128,256]{1,0:T(8,128)(2,1)S(1)}, bf16[128,256]{1,0:T(8,128)(2,1)S(1)}, u32[]{:S(2)}, u32[]{:S(2)}) collective-permute-start(bf16[128,256]{1,0:T(8,128)(2,1)S(1)} %get-tuple-element.49), channel_id=1, source_target_pairs={{0,12},{2,14},{4,8},{6,10},{8,4},{10,6},{12,0},{14,2},{1,13},{3,15... | collective-permute-start | bytes 196616 | tf_op jit(solution)/shard_map/ppermute | solution.py:132
  23.7 1.3 %collective-permute-start.4 = (bf16[512,128]{1,0:T(8,128)(2,1)S(1)}, bf16[512,128]{1,0:T(8,128)(2,1)S(1)}, u32[]{:S(2)}, u32[]{:S(2)}) collective-permute-start(bf16[512,128]{1,0:T(8,128)(2,1)S(1)} %collective-permute-done.3.refs_3_), channel_id=1, source_target_pairs={{0,2},{2,0},{4,6},{6,4},{8,10},{10,8},{12,14},{14,12},{1,3},{3,1},... | collective-permute-start | bytes 393224 | tf_op jit(solution)/shard_map/ppermute | solution.py:132
  25.7 1.2 %collective-permute-done.22.refs_4_ = bf16[128,256]{1,0:T(8,128)(2,1)S(1)} collective-permute-done((bf16[128,256]{1,0:T(8,128)(2,1)S(1)}, bf16[128,256]{1,0:T(8,128)(2,1)S(1)}, u32[]{:S(2)}, u32[]{:S(2)}) %collective-permute-start.22) | collective-permute-done | bytes 65568 | tf_op jit(solution)/shard_map/ppermute | solution.py:132
  27.6 1.5 %shard_map.73 = (bf16[4,1024,256]{2,1,0:T(8,128)(2,1)S(1)}, f32[4,256]{1,0:T(4,128)S(1)}) custom-call(s32[8,8]{1,0:T(8,128)S(1)} %bitcast.16, bf16[4,1024,128]{2,1,0:T(8,128)(2,1)S(1)} %bitcast.15, bf16[4,1024,128]{2,1,0:T(8,128)(2,1)S(1)} %collective-permute-done.other_tiles, f32[8,128]{1,0:T(8,128)S(1)} %bitcast.17), custom_call_target="tpu_custom_call" | custom-call | flops 1 | bytes 1 | tf_op jit(solution)/shard_map/pallas_call | solution.py:44
  30.5 1.7 %collective-permute-done.4.refs_3_ = bf16[512,128]{1,0:T(8,128)(2,1)S(1)} collective-permute-done((bf16[512,128]{1,0:T(8,128)(2,1)S(1)}, bf16[512,128]{1,0:T(8,128)(2,1)S(1)}, u32[]{:S(2)}, u32[]{:S(2)}) %collective-permute-start.4) | collective-permute-done | bytes 131104 | tf_op jit(solution)/shard_map/ppermute | solution.py:132
  32.2 2.8 %collective-permute-done.6.refs_4_ = bf16[512,128]{1,0:T(8,128)(2,1)S(1)} collective-permute-done((bf16[512,128]{1,0:T(8,128)(2,1)S(1)}, bf16[512,128]{1,0:T(8,128)(2,1)S(1)}, u32[]{:S(2)}, u32[]{:S(2)}) %collective-permute-start.6) | collective-permute-done | bytes 131104 | tf_op jit(solution)/shard_map/ppermute | solution.py:132
  35.0 1.6 %collective-permute-done.8.refs_5_ = bf16[512,128]{1,0:T(8,128)(2,1)S(1)} collective-permute-done((bf16[512,128]{1,0:T(8,128)(2,1)S(1)}, bf16[512,128]{1,0:T(8,128)(2,1)S(1)}, u32[]{:S(2)}, u32[]{:S(2)}) %collective-permute-start.8) | collective-permute-done | bytes 131104 | tf_op jit(solution)/shard_map/ppermute | solution.py:132
  37.4 1.8 %collective-permute-start.10 = (bf16[128,256]{1,0:T(8,128)(2,1)S(1)}, bf16[128,256]{1,0:T(8,128)(2,1)S(1)}, u32[]{:S(2)}, u32[]{:S(2)}) collective-permute-start(bf16[128,256]{1,0:T(8,128)(2,1)S(1)} %get-tuple-element.37), channel_id=1, source_target_pairs={{0,8},{2,10},{4,12},{6,14},{8,0},{10,2},{12,4},{14,6},{1,9},{3,11}... | collective-permute-start | bytes 196616 | tf_op jit(solution)/shard_map/ppermute | solution.py:132
  39.7 4.0 %collective-permute-start.27 = (bf16[128,256]{1,0:T(8,128)(2,1)S(1)}, bf16[128,256]{1,0:T(8,128)(2,1)S(1)}, u32[]{:S(2)}, u32[]{:S(2)}) collective-permute-start(bf16[128,256]{1,0:T(8,128)(2,1)S(1)} %get-tuple-element.52), channel_id=1, source_target_pairs={{0,14},{2,12},{4,10},{6,8},{8,6},{10,4},{12,2},{14,0},{1,15},{3,13... | collective-permute-start | bytes 196616 | tf_op jit(solution)/shard_map/ppermute | solution.py:132
  43.7 1.4 %collective-permute-start.11 = (bf16[128,256]{1,0:T(8,128)(2,1)S(1)}, bf16[128,256]{1,0:T(8,128)(2,1)S(1)}, u32[]{:S(2)}, u32[]{:S(2)}) collective-permute-start(bf16[128,256]{1,0:T(8,128)(2,1)S(1)} %get-tuple-element.38), channel_id=1, source_target_pairs={{0,12},{2,14},{4,8},{6,10},{8,4},{10,6},{12,0},{14,2},{1,13},{3,15... | collective-permute-start | bytes 196616 | tf_op jit(solution)/shard_map/ppermute | solution.py:132
  45.1 1.1 %collective-permute-start.9 = (bf16[128,256]{1,0:T(8,128)(2,1)S(1)}, bf16[128,256]{1,0:T(8,128)(2,1)S(1)}, u32[]{:S(2)}, u32[]{:S(2)}) collective-permute-start(bf16[128,256]{1,0:T(8,128)(2,1)S(1)} %get-tuple-element.36), channel_id=1, source_target_pairs={{0,4},{2,6},{4,0},{6,2},{8,12},{10,14},{12,8},{14,10},{1,5},{3,7},... | collective-permute-start | bytes 196616 | tf_op jit(solution)/shard_map/ppermute | solution.py:132
  48.2 2.1 %collective-permute-done.11.refs_5_ = bf16[128,256]{1,0:T(8,128)(2,1)S(1)} collective-permute-done((bf16[128,256]{1,0:T(8,128)(2,1)S(1)}, bf16[128,256]{1,0:T(8,128)(2,1)S(1)}, u32[]{:S(2)}, u32[]{:S(2)}) %collective-permute-start.11) | collective-permute-done | bytes 65568 | tf_op jit(solution)/shard_map/ppermute | solution.py:132
  52.0 1.8 %collective-permute-done.29.refs_7_ = bf16[128,256]{1,0:T(8,128)(2,1)S(1)} collective-permute-done((bf16[128,256]{1,0:T(8,128)(2,1)S(1)}, bf16[128,256]{1,0:T(8,128)(2,1)S(1)}, u32[]{:S(2)}, u32[]{:S(2)}) %collective-permute-start.29) | collective-permute-done | bytes 65568 | tf_op jit(solution)/shard_map/ppermute | solution.py:132
  54.0 2.1 %collective-permute-start.31 = (bf16[128,256]{1,0:T(8,128)(2,1)S(1)}, bf16[128,256]{1,0:T(8,128)(2,1)S(1)}, u32[]{:S(2)}, u32[]{:S(2)}) collective-permute-start(bf16[128,256]{1,0:T(8,128)(2,1)S(1)} %get-tuple-element.55), channel_id=1, source_target_pairs={{0,8},{2,10},{4,12},{6,14},{8,0},{10,2},{12,4},{14,6},{1,9},{3,11}... | collective-permute-start | bytes 196616 | tf_op jit(solution)/shard_map/ppermute | solution.py:132
  56.1 2.1 %collective-permute-start.32 = (bf16[128,256]{1,0:T(8,128)(2,1)S(1)}, bf16[128,256]{1,0:T(8,128)(2,1)S(1)}, u32[]{:S(2)}, u32[]{:S(2)}) collective-permute-start(bf16[128,256]{1,0:T(8,128)(2,1)S(1)} %get-tuple-element.56), channel_id=1, source_target_pairs={{0,12},{2,14},{4,8},{6,10},{8,4},{10,6},{12,0},{14,2},{1,13},{3,15... | collective-permute-start | bytes 196616 | tf_op jit(solution)/shard_map/ppermute | solution.py:132
  59.2 3.4 %collective-permute-done.32.refs_5_ = bf16[128,256]{1,0:T(8,128)(2,1)S(1)} collective-permute-done((bf16[128,256]{1,0:T(8,128)(2,1)S(1)}, bf16[128,256]{1,0:T(8,128)(2,1)S(1)}, u32[]{:S(2)}, u32[]{:S(2)}) %collective-permute-start.32) | collective-permute-done | bytes 65568 | tf_op jit(solution)/shard_map/ppermute | solution.py:132
  62.6 2.1 %collective-permute-start.33 = (bf16[1024,128]{1,0:T(8,128)(2,1)S(1)}, bf16[1024,128]{1,0:T(8,128)(2,1)S(1)}, u32[]{:S(2)}, u32[]{:S(2)}) collective-permute-start(bf16[1024,128]{1,0:T(8,128)(2,1)S(1)} %shard_map.81), channel_id=1, source_target_pairs={{0,2},{2,0},{4,6},{6,4},{8,10},{10,8},{12,14},{14,12},{1,3},{3,1},... | collective-permute-start | bytes 786440 | tf_op jit(solution)/shard_map/ppermute | solution.py:132
  64.7 1.4 %collective-permute-start.14 = (bf16[128,256]{1,0:T(8,128)(2,1)S(1)}, bf16[128,256]{1,0:T(8,128)(2,1)S(1)}, u32[]{:S(2)}, u32[]{:S(2)}) collective-permute-start(bf16[128,256]{1,0:T(8,128)(2,1)S(1)} %get-tuple-element.40), channel_id=1, source_target_pairs={{0,10},{2,8},{4,14},{6,12},{8,2},{10,0},{12,6},{14,4},{1,11},{3,9}... | collective-permute-start | bytes 196616 | tf_op jit(solution)/shard_map/ppermute | solution.py:132
  66.1 3.2 %collective-permute-start.15 = (bf16[128,256]{1,0:T(8,128)(2,1)S(1)}, bf16[128,256]{1,0:T(8,128)(2,1)S(1)}, u32[]{:S(2)}, u32[]{:S(2)}) collective-permute-start(bf16[128,256]{1,0:T(8,128)(2,1)S(1)} %get-tuple-element.41), channel_id=1, source_target_pairs={{0,14},{2,12},{4,10},{6,8},{8,6},{10,4},{12,2},{14,0},{1,15},{3,13... | collective-permute-start | bytes 196616 | tf_op jit(solution)/shard_map/ppermute | solution.py:132
  69.3 1.4 %collective-permute-done.14.refs_4_ = bf16[128,256]{1,0:T(8,128)(2,1)S(1)} collective-permute-done((bf16[128,256]{1,0:T(8,128)(2,1)S(1)}, bf16[128,256]{1,0:T(8,128)(2,1)S(1)}, u32[]{:S(2)}, u32[]{:S(2)}) %collective-permute-start.14) | collective-permute-done | bytes 65568 | tf_op jit(solution)/shard_map/ppermute | solution.py:132
  70.7 1.4 %collective-permute-start.16 = (bf16[128,256]{1,0:T(8,128)(2,1)S(1)}, bf16[128,256]{1,0:T(8,128)(2,1)S(1)}, u32[]{:S(2)}, u32[]{:S(2)}) collective-permute-start(bf16[128,256]{1,0:T(8,128)(2,1)S(1)} %collective-permute-done.14.refs_4_), channel_id=1, source_target_pairs={{0,4},{2,6},{4,0},{6,2},{8,12},{10,14},{12,8},{14,10},{1,5},{3,7},... | collective-permute-start | bytes 196616 | tf_op jit(solution)/shard_map/ppermute | solution.py:132
  72.2 1.3 %collective-permute-done.15.refs_5_ = bf16[128,256]{1,0:T(8,128)(2,1)S(1)} collective-permute-done((bf16[128,256]{1,0:T(8,128)(2,1)S(1)}, bf16[128,256]{1,0:T(8,128)(2,1)S(1)}, u32[]{:S(2)}, u32[]{:S(2)}) %collective-permute-start.15) | collective-permute-done | bytes 65568 | tf_op jit(solution)/shard_map/ppermute | solution.py:132
  73.4 3.5 %collective-permute-done.16.refs_6_ = bf16[128,256]{1,0:T(8,128)(2,1)S(1)} collective-permute-done((bf16[128,256]{1,0:T(8,128)(2,1)S(1)}, bf16[128,256]{1,0:T(8,128)(2,1)S(1)}, u32[]{:S(2)}, u32[]{:S(2)}) %collective-permute-start.16) | collective-permute-done | bytes 65568 | tf_op jit(solution)/shard_map/ppermute | solution.py:132
  77.8 2.3 %collective-permute-start.19 = (bf16[128,256]{1,0:T(8,128)(2,1)S(1)}, bf16[128,256]{1,0:T(8,128)(2,1)S(1)}, u32[]{:S(2)}, u32[]{:S(2)}) collective-permute-start(bf16[128,256]{1,0:T(8,128)(2,1)S(1)} %get-tuple-element.44), channel_id=1, source_target_pairs={{0,8},{2,10},{4,12},{6,14},{8,0},{10,2},{12,4},{14,6},{1,9},{3,11}... | collective-permute-start | bytes 196616 | tf_op jit(solution)/shard_map/ppermute | solution.py:132
  80.1 2.0 %collective-permute-start.20 = (bf16[128,256]{1,0:T(8,128)(2,1)S(1)}, bf16[128,256]{1,0:T(8,128)(2,1)S(1)}, u32[]{:S(2)}, u32[]{:S(2)}) collective-permute-start(bf16[128,256]{1,0:T(8,128)(2,1)S(1)} %get-tuple-element.45), channel_id=1, source_target_pairs={{0,12},{2,14},{4,8},{6,10},{8,4},{10,6},{12,0},{14,2},{1,13},{3,15... | collective-permute-start | bytes 196616 | tf_op jit(solution)/shard_map/ppermute | solution.py:132
  83.0 3.2 %collective-permute-done.20.refs_5_ = bf16[128,256]{1,0:T(8,128)(2,1)S(1)} collective-permute-done((bf16[128,256]{1,0:T(8,128)(2,1)S(1)}, bf16[128,256]{1,0:T(8,128)(2,1)S(1)}, u32[]{:S(2)}, u32[]{:S(2)}) %collective-permute-start.20) | collective-permute-done | bytes 65568 | tf_op jit(solution)/shard_map/ppermute | solution.py:132
  (59 shorter events, 17.0 us)
Async XLA Ops:
  0.0 7.2 %collective-permute-start.1 = (bf16[4,2048,128]{2,1,0:T(8,128)(2,1)}, bf16[4,2048,128]{2,1,0:T(8,128)(2,1)S(1)}, u32[]{:S(2)}, u32[]{:S(2)}) collective-permute-start(bf16[4,2048,128]{2,1,0:T(8,128)(2,1)} %bitcast.12), channel_id=1, source_target_pairs={{0,1},{1,0},{2,3},{3,2},{4,5},{5,4},{6,7},{7,6},{8,9},{9,8},{10,11... | collective-permute-start | bytes 6291464 | tf_op jit(solution)/shard_map/ppermute | solution.py:135
  0.5 23.2 %collective-permute-start = (bf16[4,1024,128]{2,1,0:T(8,128)(2,1)}, bf16[4,1024,128]{2,1,0:T(8,128)(2,1)S(1)}, u32[]{:S(2)}, u32[]{:S(2)}) collective-permute-start(bf16[4,1024,128]{2,1,0:T(8,128)(2,1)} %bitcast.14), channel_id=1, source_target_pairs={{0,1},{1,0},{2,3},{3,2},{4,5},{5,4},{6,7},{7,6},{8,9},{9,8},{10,11... | collective-permute-start | bytes 3145736 | tf_op jit(solution)/shard_map/ppermute | solution.py:135
  1.5 11.4 %collective-permute-start.3 = (bf16[512,128]{1,0:T(8,128)(2,1)S(1)}, bf16[512,128]{1,0:T(8,128)(2,1)S(1)}, u32[]{:S(2)}, u32[]{:S(2)}) collective-permute-start(bf16[512,128]{1,0:T(8,128)(2,1)S(1)} %get-tuple-element.58.refs_2_), channel_id=1, source_target_pairs={{0,4},{2,6},{4,0},{6,2},{8,12},{10,14},{12,8},{14,10},{1,5},{3,7},... | collective-permute-start | bytes 393224 | tf_op jit(solution)/shard_map/ppermute | solution.py:132
  4.6 12.9 %collective-permute-start.5 = (bf16[512,128]{1,0:T(8,128)(2,1)S(1)}, bf16[512,128]{1,0:T(8,128)(2,1)S(1)}, u32[]{:S(2)}, u32[]{:S(2)}) collective-permute-start(bf16[512,128]{1,0:T(8,128)(2,1)S(1)} %get-tuple-element.57), channel_id=1, source_target_pairs={{0,8},{2,10},{4,12},{6,14},{8,0},{10,2},{12,4},{14,6},{1,9},{3,11}... | collective-permute-start | bytes 393224 | tf_op jit(solution)/shard_map/ppermute | solution.py:132
  7.2 10.3 %collective-permute-start.7 = (bf16[512,128]{1,0:T(8,128)(2,1)S(1)}, bf16[512,128]{1,0:T(8,128)(2,1)S(1)}, u32[]{:S(2)}, u32[]{:S(2)}) collective-permute-start(bf16[512,128]{1,0:T(8,128)(2,1)S(1)} %get-tuple-element.57), channel_id=1, source_target_pairs={{0,12},{2,14},{4,8},{6,10},{8,4},{10,6},{12,0},{14,2},{1,13},{3,15... | collective-permute-start | bytes 393224 | tf_op jit(solution)/shard_map/ppermute | solution.py:132
  18.3 6.7 %collective-permute-start.21 = (bf16[128,256]{1,0:T(8,128)(2,1)S(1)}, bf16[128,256]{1,0:T(8,128)(2,1)S(1)}, u32[]{:S(2)}, u32[]{:S(2)}) collective-permute-start(bf16[128,256]{1,0:T(8,128)(2,1)S(1)} %get-tuple-element.47), channel_id=1, source_target_pairs={{0,4},{2,6},{4,0},{6,2},{8,12},{10,14},{12,8},{14,10},{1,5},{3,7},... | collective-permute-start | bytes 196616 | tf_op jit(solution)/shard_map/ppermute | solution.py:132
  20.5 6.4 %collective-permute-start.22 = (bf16[128,256]{1,0:T(8,128)(2,1)S(1)}, bf16[128,256]{1,0:T(8,128)(2,1)S(1)}, u32[]{:S(2)}, u32[]{:S(2)}) collective-permute-start(bf16[128,256]{1,0:T(8,128)(2,1)S(1)} %get-tuple-element.48), channel_id=1, source_target_pairs={{0,8},{2,10},{4,12},{6,14},{8,0},{10,2},{12,4},{14,6},{1,9},{3,11}... | collective-permute-start | bytes 196616 | tf_op jit(solution)/shard_map/ppermute | solution.py:132
  21.6 7.6 %collective-permute-start.23 = (bf16[128,256]{1,0:T(8,128)(2,1)S(1)}, bf16[128,256]{1,0:T(8,128)(2,1)S(1)}, u32[]{:S(2)}, u32[]{:S(2)}) collective-permute-start(bf16[128,256]{1,0:T(8,128)(2,1)S(1)} %get-tuple-element.49), channel_id=1, source_target_pairs={{0,12},{2,14},{4,8},{6,10},{8,4},{10,6},{12,0},{14,2},{1,13},{3,15... | collective-permute-start | bytes 196616 | tf_op jit(solution)/shard_map/ppermute | solution.py:132
  23.0 7.6 %collective-permute-start.2 = (bf16[512,128]{1,0:T(8,128)(2,1)S(1)}, bf16[512,128]{1,0:T(8,128)(2,1)S(1)}, u32[]{:S(2)}, u32[]{:S(2)}) collective-permute-start(bf16[512,128]{1,0:T(8,128)(2,1)S(1)} %get-tuple-element.58.refs_2_), channel_id=1, source_target_pairs={{0,2},{2,0},{4,6},{6,4},{8,10},{10,8},{12,14},{14,12},{1,3},{3,1},... | collective-permute-start | bytes 393224 | tf_op jit(solution)/shard_map/ppermute | solution.py:132
  23.7 8.5 %collective-permute-start.4 = (bf16[512,128]{1,0:T(8,128)(2,1)S(1)}, bf16[512,128]{1,0:T(8,128)(2,1)S(1)}, u32[]{:S(2)}, u32[]{:S(2)}) collective-permute-start(bf16[512,128]{1,0:T(8,128)(2,1)S(1)} %collective-permute-done.3.refs_3_), channel_id=1, source_target_pairs={{0,2},{2,0},{4,6},{6,4},{8,10},{10,8},{12,14},{14,12},{1,3},{3,1},... | collective-permute-start | bytes 393224 | tf_op jit(solution)/shard_map/ppermute | solution.py:132
  25.0 10.0 %collective-permute-start.6 = (bf16[512,128]{1,0:T(8,128)(2,1)S(1)}, bf16[512,128]{1,0:T(8,128)(2,1)S(1)}, u32[]{:S(2)}, u32[]{:S(2)}) collective-permute-start(bf16[512,128]{1,0:T(8,128)(2,1)S(1)} %collective-permute-done.5.refs_4_), channel_id=1, source_target_pairs={{0,2},{2,0},{4,6},{6,4},{8,10},{10,8},{12,14},{14,12},{1,3},{3,1},... | collective-permute-start | bytes 393224 | tf_op jit(solution)/shard_map/ppermute | solution.py:132
  26.9 9.7 %collective-permute-start.8 = (bf16[512,128]{1,0:T(8,128)(2,1)S(1)}, bf16[512,128]{1,0:T(8,128)(2,1)S(1)}, u32[]{:S(2)}, u32[]{:S(2)}) collective-permute-start(bf16[512,128]{1,0:T(8,128)(2,1)S(1)} %collective-permute-done.7.refs_5_), channel_id=1, source_target_pairs={{0,2},{2,0},{4,6},{6,4},{8,10},{10,8},{12,14},{14,12},{1,3},{3,1},... | collective-permute-start | bytes 393224 | tf_op jit(solution)/shard_map/ppermute | solution.py:132
  29.6 14.1 %collective-permute-start.24 = (bf16[128,512]{1,0:T(8,128)(2,1)S(1)}, bf16[128,512]{1,0:T(8,128)(2,1)S(1)}, u32[]{:S(2)}, u32[]{:S(2)}) collective-permute-start(bf16[128,512]{1,0:T(8,128)(2,1)S(1)} %get-tuple-element.50), channel_id=1, source_target_pairs={{0,2},{2,0},{4,6},{6,4},{8,10},{10,8},{12,14},{14,12},{1,3},{3,1},... | collective-permute-start | bytes 393224 | tf_op jit(solution)/shard_map/ppermute | solution.py:132
  37.4 7.7 %collective-permute-start.10 = (bf16[128,256]{1,0:T(8,128)(2,1)S(1)}, bf16[128,256]{1,0:T(8,128)(2,1)S(1)}, u32[]{:S(2)}, u32[]{:S(2)}) collective-permute-start(bf16[128,256]{1,0:T(8,128)(2,1)S(1)} %get-tuple-element.37), channel_id=1, source_target_pairs={{0,8},{2,10},{4,12},{6,14},{8,0},{10,2},{12,4},{14,6},{1,9},{3,11}... | collective-permute-start | bytes 196616 | tf_op jit(solution)/shard_map/ppermute | solution.py:132
  39.2 7.0 %collective-permute-start.26 = (bf16[128,256]{1,0:T(8,128)(2,1)S(1)}, bf16[128,256]{1,0:T(8,128)(2,1)S(1)}, u32[]{:S(2)}, u32[]{:S(2)}) collective-permute-start(bf16[128,256]{1,0:T(8,128)(2,1)S(1)} %get-tuple-element.51), channel_id=1, source_target_pairs={{0,10},{2,8},{4,14},{6,12},{8,2},{10,0},{12,6},{14,4},{1,11},{3,9}... | collective-permute-start | bytes 196616 | tf_op jit(solution)/shard_map/ppermute | solution.py:132
  39.7 8.2 %collective-permute-start.27 = (bf16[128,256]{1,0:T(8,128)(2,1)S(1)}, bf16[128,256]{1,0:T(8,128)(2,1)S(1)}, u32[]{:S(2)}, u32[]{:S(2)}) collective-permute-start(bf16[128,256]{1,0:T(8,128)(2,1)S(1)} %get-tuple-element.52), channel_id=1, source_target_pairs={{0,14},{2,12},{4,10},{6,8},{8,6},{10,4},{12,2},{14,0},{1,15},{3,13... | collective-permute-start | bytes 196616 | tf_op jit(solution)/shard_map/ppermute | solution.py:132
  43.7 10.1 %collective-permute-start.25 = (bf16[128,512]{1,0:T(8,128)(2,1)S(1)}, bf16[128,512]{1,0:T(8,128)(2,1)S(1)}, u32[]{:S(2)}, u32[]{:S(2)}) collective-permute-start(bf16[128,512]{1,0:T(8,128)(2,1)S(1)} %collective-permute-done.24.refs_2_), channel_id=1, source_target_pairs={{0,4},{2,6},{4,0},{6,2},{8,12},{10,14},{12,8},{14,10},{1,5},{3,7},... | collective-permute-start | bytes 393224 | tf_op jit(solution)/shard_map/ppermute | solution.py:132
  43.7 6.7 %collective-permute-start.11 = (bf16[128,256]{1,0:T(8,128)(2,1)S(1)}, bf16[128,256]{1,0:T(8,128)(2,1)S(1)}, u32[]{:S(2)}, u32[]{:S(2)}) collective-permute-start(bf16[128,256]{1,0:T(8,128)(2,1)S(1)} %get-tuple-element.38), channel_id=1, source_target_pairs={{0,12},{2,14},{4,8},{6,10},{8,4},{10,6},{12,0},{14,2},{1,13},{3,15... | collective-permute-start | bytes 196616 | tf_op jit(solution)/shard_map/ppermute | solution.py:132
  45.1 5.9 %collective-permute-start.9 = (bf16[128,256]{1,0:T(8,128)(2,1)S(1)}, bf16[128,256]{1,0:T(8,128)(2,1)S(1)}, u32[]{:S(2)}, u32[]{:S(2)}) collective-permute-start(bf16[128,256]{1,0:T(8,128)(2,1)S(1)} %get-tuple-element.36), channel_id=1, source_target_pairs={{0,4},{2,6},{4,0},{6,2},{8,12},{10,14},{12,8},{14,10},{1,5},{3,7},... | collective-permute-start | bytes 196616 | tf_op jit(solution)/shard_map/ppermute | solution.py:132
  46.2 5.8 %collective-permute-start.28 = (bf16[128,256]{1,0:T(8,128)(2,1)S(1)}, bf16[128,256]{1,0:T(8,128)(2,1)S(1)}, u32[]{:S(2)}, u32[]{:S(2)}) collective-permute-start(bf16[128,256]{1,0:T(8,128)(2,1)S(1)} %collective-permute-done.26.refs_4_), channel_id=1, source_target_pairs={{0,4},{2,6},{4,0},{6,2},{8,12},{10,14},{12,8},{14,10},{1,5},{3,7},... | collective-permute-start | bytes 196616 | tf_op jit(solution)/shard_map/ppermute | solution.py:132
  47.9 5.9 %collective-permute-start.29 = (bf16[128,256]{1,0:T(8,128)(2,1)S(1)}, bf16[128,256]{1,0:T(8,128)(2,1)S(1)}, u32[]{:S(2)}, u32[]{:S(2)}) collective-permute-start(bf16[128,256]{1,0:T(8,128)(2,1)S(1)} %collective-permute-done.27.refs_5_), channel_id=1, source_target_pairs={{0,4},{2,6},{4,0},{6,2},{8,12},{10,14},{12,8},{14,10},{1,5},{3,7},... | collective-permute-start | bytes 196616 | tf_op jit(solution)/shard_map/ppermute | solution.py:132
  51.5 17.9 %collective-permute-start.12 = (bf16[128,512]{1,0:T(8,128)(2,1)S(1)}, bf16[128,512]{1,0:T(8,128)(2,1)S(1)}, u32[]{:S(2)}, u32[]{:S(2)}) collective-permute-start(bf16[128,512]{1,0:T(8,128)(2,1)S(1)} %get-tuple-element.39), channel_id=1, source_target_pairs={{0,2},{2,0},{4,6},{6,4},{8,10},{10,8},{12,14},{14,12},{1,3},{3,1},... | collective-permute-start | bytes 393224 | tf_op jit(solution)/shard_map/ppermute | solution.py:132
  53.8 4.4 %collective-permute-start.30 = (bf16[128,256]{1,0:T(8,128)(2,1)S(1)}, bf16[128,256]{1,0:T(8,128)(2,1)S(1)}, u32[]{:S(2)}, u32[]{:S(2)}) collective-permute-start(bf16[128,256]{1,0:T(8,128)(2,1)S(1)} %get-tuple-element.54), channel_id=1, source_target_pairs={{0,4},{2,6},{4,0},{6,2},{8,12},{10,14},{12,8},{14,10},{1,5},{3,7},... | collective-permute-start | bytes 196616 | tf_op jit(solution)/shard_map/ppermute | solution.py:132
  54.0 5.2 %collective-permute-start.31 = (bf16[128,256]{1,0:T(8,128)(2,1)S(1)}, bf16[128,256]{1,0:T(8,128)(2,1)S(1)}, u32[]{:S(2)}, u32[]{:S(2)}) collective-permute-start(bf16[128,256]{1,0:T(8,128)(2,1)S(1)} %get-tuple-element.55), channel_id=1, source_target_pairs={{0,8},{2,10},{4,12},{6,14},{8,0},{10,2},{12,4},{14,6},{1,9},{3,11}... | collective-permute-start | bytes 196616 | tf_op jit(solution)/shard_map/ppermute | solution.py:132
  56.1 6.5 %collective-permute-start.32 = (bf16[128,256]{1,0:T(8,128)(2,1)S(1)}, bf16[128,256]{1,0:T(8,128)(2,1)S(1)}, u32[]{:S(2)}, u32[]{:S(2)}) collective-permute-start(bf16[128,256]{1,0:T(8,128)(2,1)S(1)} %get-tuple-element.56), channel_id=1, source_target_pairs={{0,12},{2,14},{4,8},{6,10},{8,4},{10,6},{12,0},{14,2},{1,13},{3,15... | collective-permute-start | bytes 196616 | tf_op jit(solution)/shard_map/ppermute | solution.py:132
  62.6 23.5 %collective-permute-start.33 = (bf16[1024,128]{1,0:T(8,128)(2,1)S(1)}, bf16[1024,128]{1,0:T(8,128)(2,1)S(1)}, u32[]{:S(2)}, u32[]{:S(2)}) collective-permute-start(bf16[1024,128]{1,0:T(8,128)(2,1)S(1)} %shard_map.81), channel_id=1, source_target_pairs={{0,2},{2,0},{4,6},{6,4},{8,10},{10,8},{12,14},{14,12},{1,3},{3,1},... | collective-permute-start | bytes 786440 | tf_op jit(solution)/shard_map/ppermute | solution.py:132
  64.7 6.1 %collective-permute-start.14 = (bf16[128,256]{1,0:T(8,128)(2,1)S(1)}, bf16[128,256]{1,0:T(8,128)(2,1)S(1)}, u32[]{:S(2)}, u32[]{:S(2)}) collective-permute-start(bf16[128,256]{1,0:T(8,128)(2,1)S(1)} %get-tuple-element.40), channel_id=1, source_target_pairs={{0,10},{2,8},{4,14},{6,12},{8,2},{10,0},{12,6},{14,4},{1,11},{3,9}... | collective-permute-start | bytes 196616 | tf_op jit(solution)/shard_map/ppermute | solution.py:132
  66.1 7.3 %collective-permute-start.15 = (bf16[128,256]{1,0:T(8,128)(2,1)S(1)}, bf16[128,256]{1,0:T(8,128)(2,1)S(1)}, u32[]{:S(2)}, u32[]{:S(2)}) collective-permute-start(bf16[128,256]{1,0:T(8,128)(2,1)S(1)} %get-tuple-element.41), channel_id=1, source_target_pairs={{0,14},{2,12},{4,10},{6,8},{8,6},{10,4},{12,2},{14,0},{1,15},{3,13... | collective-permute-start | bytes 196616 | tf_op jit(solution)/shard_map/ppermute | solution.py:132
  69.3 8.4 %collective-permute-start.13 = (bf16[128,512]{1,0:T(8,128)(2,1)S(1)}, bf16[128,512]{1,0:T(8,128)(2,1)S(1)}, u32[]{:S(2)}, u32[]{:S(2)}) collective-permute-start(bf16[128,512]{1,0:T(8,128)(2,1)S(1)} %collective-permute-done.12.refs_2_), channel_id=1, source_target_pairs={{0,4},{2,6},{4,0},{6,2},{8,12},{10,14},{12,8},{14,10},{1,5},{3,7},... | collective-permute-start | bytes 393224 | tf_op jit(solution)/shard_map/ppermute | solution.py:132
  70.7 6.2 %collective-permute-start.16 = (bf16[128,256]{1,0:T(8,128)(2,1)S(1)}, bf16[128,256]{1,0:T(8,128)(2,1)S(1)}, u32[]{:S(2)}, u32[]{:S(2)}) collective-permute-start(bf16[128,256]{1,0:T(8,128)(2,1)S(1)} %collective-permute-done.14.refs_4_), channel_id=1, source_target_pairs={{0,4},{2,6},{4,0},{6,2},{8,12},{10,14},{12,8},{14,10},{1,5},{3,7},... | collective-permute-start | bytes 196616 | tf_op jit(solution)/shard_map/ppermute | solution.py:132
  77.8 5.2 %collective-permute-start.19 = (bf16[128,256]{1,0:T(8,128)(2,1)S(1)}, bf16[128,256]{1,0:T(8,128)(2,1)S(1)}, u32[]{:S(2)}, u32[]{:S(2)}) collective-permute-start(bf16[128,256]{1,0:T(8,128)(2,1)S(1)} %get-tuple-element.44), channel_id=1, source_target_pairs={{0,8},{2,10},{4,12},{6,14},{8,0},{10,2},{12,4},{14,6},{1,9},{3,11}... | collective-permute-start | bytes 196616 | tf_op jit(solution)/shard_map/ppermute | solution.py:132
  80.1 6.1 %collective-permute-start.20 = (bf16[128,256]{1,0:T(8,128)(2,1)S(1)}, bf16[128,256]{1,0:T(8,128)(2,1)S(1)}, u32[]{:S(2)}, u32[]{:S(2)}) collective-permute-start(bf16[128,256]{1,0:T(8,128)(2,1)S(1)} %get-tuple-element.45), channel_id=1, source_target_pairs={{0,12},{2,14},{4,8},{6,10},{8,4},{10,6},{12,0},{14,2},{1,13},{3,15... | collective-permute-start | bytes 196616 | tf_op jit(solution)/shard_map/ppermute | solution.py:132
  (8 other events, 42.0 us)

commit v3 on v2

--- a/solution.py
+++ b/solution.py
@@ -8,15 +8,23 @@
 from jax.sharding import PartitionSpec as P
 
 CEILING = 4.0
-
-
-def order_kernel(links, own_tiles, other_tiles, bias, ordered, shifts):
+LAG = 1
+TAIL = 10**10
+
+
+def order_kernel(links, own_tiles, other_tiles, bias, ordered, shifts, own_here, bias_here, arrivals):
+    own_copy = pltpu.make_async_copy(own_tiles, own_here, arrivals.at[0])
+    bias_copy = pltpu.make_async_copy(bias, bias_here, arrivals.at[1])
+    own_copy.start()
+    bias_copy.start()
     owner_count = ordered.shape[0]
     me, rep = lax.axis_index("owners"), lax.axis_index("rep")
     half, _, size = own_tiles.shape
     slots = links.shape[1]
     width = 2 * size
-    for ours, source in ((True, own_tiles), (False, other_tiles)):
+    for ours, source in ((False, other_tiles), (True, own_here)):
+        if ours:
+            own_copy.wait()
         first = (rep if ours else 1 - rep) * half
         for block in range(half):
             row = first + block
@@ -33,22 +41,29 @@
                 ordered[distance, pl.ds(low, size), pl.ds(block % 2 * size, size)] = source[
                     block, pl.ds(slot * size, size), :
                 ]
+    bias_copy.wait()
     for distance in range(owner_count):
         for j in range(2):
-            shifts[pl.ds(distance, 1), pl.ds(j * size, size)] = bias[pl.ds(2 * (me ^ distance) + j, 1), :]
+            shifts[pl.ds(distance, 1), pl.ds(j * size, size)] = bias_here[pl.ds(2 * (me ^ distance) + j, 1), :]
 
 
 def order_weights(links, own_tiles, other_tiles, bias):
     half, depth, size = own_tiles.shape
     vmem = pl.BlockSpec(memory_space=pltpu.VMEM)
+    hbm = pl.BlockSpec(memory_space=pl.ANY)
     return pl.pallas_call(
         order_kernel,
         out_shape=[
             jax.ShapeDtypeStruct((half, depth, 2 * size), jnp.bfloat16),
             jax.ShapeDtypeStruct((half, 2 * size), jnp.float32),
         ],
-        in_specs=[pl.BlockSpec(memory_space=pltpu.SMEM), vmem, vmem, vmem],
+        in_specs=[pl.BlockSpec(memory_space=pltpu.SMEM), hbm, vmem, hbm],
         out_specs=[vmem, vmem],
+        scratch_shapes=[
+            pltpu.VMEM(own_tiles.shape, jnp.bfloat16),
+            pltpu.VMEM(bias.shape, jnp.float32),
+            pltpu.SemaphoreType.DMA((2,)),
+        ],
         compiler_params=pltpu.CompilerParams(vmem_limit_bytes=24 * 2**20),
         cost_estimate=pl.CostEstimate(flops=1, bytes_accessed=1, transcendentals=0),
     )(links, own_tiles, other_tiles, bias)
@@ -96,7 +111,7 @@
             outs[0][...] = settled[...]
 
 
-def layer(ordered, shifts, buffers, tile_list, out_groups, active_section, raw=False, final=None, settled=None):
+def layer(ordered, shifts, buffers, tile_list, out_groups, active_section, raw=False, final=None, settled=None, cost=1):
     count, depth, width = ordered.shape
     rows = buffers[0].shape[1] if raw else buffers[0].shape[0]
     if final:
@@ -112,7 +127,7 @@
         out_specs=[vmem] * len(shapes),
         scratch_shapes=[pltpu.VMEM((len(tile_list), rows, width), jnp.bfloat16)] if raw else [],
         compiler_params=pltpu.CompilerParams(vmem_limit_bytes=16 * 2**20),
-        cost_estimate=pl.CostEstimate(flops=1, bytes_accessed=1, transcendentals=0),
+        cost_estimate=pl.CostEstimate(flops=cost, bytes_accessed=1, transcendentals=0),
     )(*operands)
 
 
@@ -123,13 +138,20 @@
     features = inputs[0]
     piece = features.shape[0] // owner_count
 
-    def moved(value, distance, cross):
+    def moved(value, route):
         pairs = []
         for owner in range(owner_count):
             for place in range(2):
-                target = (owner ^ distance) * 2 + (1 - place if cross else place)
-                pairs.append((owner * 2 + place, target))
-        return lax.ppermute(value, ("owners", "section"), pairs)
+                for core in range(2):
+                    to_owner, to_place, to_core = route(owner, place, core)
+                    pairs.append(((owner * 2 + place) * 2 + core, (to_owner * 2 + to_place) * 2 + to_core))
+        return lax.ppermute(value, ("owners", "section", "rep"), pairs)
+
+    def within(distance, section):
+        return lambda owner, place, core: (owner ^ distance, place, core) if place == section else (owner, place, 1 - core)
+
+    def across(distance, section):
+        return lambda owner, place, core: (owner ^ distance if place == section else owner, 1 - place, core)
 
     def other_core(value):
         return lax.ppermute(value, "rep", [(0, 1), (1, 0)])
@@ -137,42 +159,53 @@
     halves = features.reshape(2, 2 * piece, features.shape[1])
     near = lax.dynamic_index_in_dim(halves, me // 2, 0, keepdims=False)
     far = lax.dynamic_index_in_dim(halves, 1 - me // 2, 0, keepdims=False)
-    three, two, one = moved(far, 3, False), moved(far, 2, False), moved(near, 1, False)
-    start = [near, one, two, three]
+    def after(value, *others):
+        return lax.optimization_barrier((value, *others))[0]
+
+    def gathered(close, apart, section):
+        beside = within(1, section)
+        return [close, moved(close, beside), apart, moved(apart, beside)]
+
     first_own, second_own = weight_first[0], weight_second[0]
-    first = order_weights(links_first[0], first_own, other_core(first_own), bias_first[0].reshape(-1, size))
-    second = order_weights(links_second[0], second_own, other_core(second_own), bias_second[0].reshape(-1, size))
+    first_other = other_core(first_own)
+    far_two, near_one = moved(far, within(2, 0)), moved(near, within(1, 0))
+    crossed = moved(far, across(2, 1)), moved(near, across(0, 1))
+    first = order_weights(links_first[0], first_own, first_other, bias_first[0].reshape(-1, size))
+    second_other = other_core(second_own)
+    second = order_weights(links_second[0], second_own, second_other, bias_second[0].reshape(-1, size))
+    start = [near, near_one, far_two, moved(after(far_two, first[0]), within(1, 0))]
+    later = gathered(crossed[1], crossed[0], 0)
 
     raw_tiles = [(buffer, column * piece, 2 * buffer + column) for buffer in range(4) for column in range(2)]
-    relayed = [(0, 0), (0, 1), (1, 1), (1, 0), (2, 0), (3, 0), (3, 1), (2, 1)]
-    relayed_spots = [(0, 0), (0, piece), (1, 0), (1, piece), (2, 0), (3, 0), (4, 0), (5, 0)]
-    relayed_tiles = [
-        (*spot, 2 * sender + part) for spot, (sender, part) in zip(relayed_spots, relayed, strict=True)
-    ]
+    order = [(0, 0), (0, 1), (1, 1), (1, 0), (2, 0), (2, 1), (3, 1), (3, 0)]
+    later_tiles = [(place // 2, place % 2 * piece, 2 * sender + part) for place, (sender, part) in enumerate(order)]
     second_tiles = [(buffer, 0, buffer) for buffer in range(4)]
 
     apart = [[0], [1], [2], [3]]
-    joined = [[0, 1], [2], [3]]
-
-    def first_layer(buffers, active, raw):
-        return layer(*first, buffers, raw_tiles if raw else relayed_tiles, apart, active, raw=raw)
-
-    def second_layer(parts, active, **more):
-        arrived = [moved(parts[distance], distance, False) for distance in (3, 2, 1)]
-        return layer(*second, [parts[0], *arrived[::-1]], second_tiles, joined, active, **more)
+    joined = [[0, 1], [2, 3]]
+
+    def first_layer(buffers, active, raw, cost=1):
+        spots = raw_tiles if raw else later_tiles
+        return layer(*first, buffers, spots, apart, active, raw=raw, cost=cost)
+
+    def second_layer(parts, active, earlier, **more):
+        arrived = [moved(parts[distance], within(distance, active)) for distance in (3, 2, 1)]
+        buffers = after([parts[0], *arrived[::-1]], earlier)
+        return layer(*second, buffers, second_tiles, joined, active, **more)
 
     def hand_over(result):
-        close, far_two, far_three = result
-        two, three = moved(far_two, 2, True), moved(far_three, 3, True)
-        close = moved(close, 0, True)
-        return [close, moved(close, 1, False), two, three, moved(two, 1, False), moved(three, 1, False)]
-
-    later = [moved(value, 0, True) for value in start]
-    zero = second_layer(first_layer(start, 0, True), 0)
-    one = second_layer(first_layer(later, 0, True), 0)
-    settled = second_layer(first_layer(hand_over(zero), 1, False), 1, final="plain")[0]
-    settled = moved(settled, 0, True)
-    return second_layer(first_layer(hand_over(one), 1, False), 1, final="merge", settled=settled)[0][None]
+        close, apart = result
+        return gathered(moved(close, across(0, 0)), moved(apart, across(2, 0)), 1)
+
+    parts_zero = first_layer(start, 0, True, cost=LAG)
+    parts_one = first_layer(after(later, parts_zero), 0, True)
+    zero = second_layer(parts_zero, 0, parts_one, cost=LAG)
+    one = second_layer(parts_one, 0, zero)
+    parts_zero = first_layer(after(hand_over(zero), one), 1, False, cost=LAG)
+    parts_one = first_layer(after(hand_over(one), parts_zero), 1, False)
+    settled = second_layer(parts_zero, 1, parts_one, final="plain", cost=LAG)
+    last = second_layer(parts_one, 1, settled, final="plain", cost=TAIL)[0]
+    return jnp.where(lax.axis_index("section") == 0, moved(settled[0], across(0, 1)), last)[None]
 
 
 def from_behind(value, axis, steps):

time: 87.6 us -> 69.4 us (0.79)
  waiting for transfers between devices: 33 us -> 11.8 us
  starting transfers between devices: 42.4 us -> 45.5 us
    ppermute x32 -> x28, waiting for transfers between devices: 33 us -> 11.8 us  [moved(): return lax.ppermute(value, ('owners', 'section', 'rep'), pairs)]
    ppermute x32 -> x28, starting transfers between devices: 41.9 us -> 45 us  [moved(): return lax.ppermute(value, ('owners', 'section', 'rep'), pairs)]
  transfers between devices with their start and end apart: 34 -> 30, of which waited for: 18 -> 6; matrix products, arithmetic and copies ran while one was open for 1% -> 1% of each run, Pallas kernels for 8% -> 10%
where the time goes in v3:
time: 69.4 us; the launch traced here: 69.2 us
  starting transfers between devices  45.5 us (66%)
  waiting for transfers between devices  11.8 us (17%)
  Pallas kernels  7.02 us (10%)
  local copies, waits for them, and re-layouts  3.96 us (6%)
  other arithmetic  0.73 us (1%)
    ppermute x28, starting transfers between devices, moved(): return lax.ppermute(value, ('owners', 'section', 'rep'), pairs)  45 us
    ppermute x28, waiting for transfers between devices, moved(): return lax.ppermute(value, ('owners', 'section', 'rep'), pairs)  11.8 us
    pallas_call x2, Pallas kernels, order_weights(): pl.pallas_call(order_kernel, out_shape=[jax.ShapeDtypeStruct((half, depth...  4.53 us
    unnamed x12, local copies, waits for them, and re-layouts  2.97 us
    pallas_call x8, Pallas kernels, layer(): pl.pallas_call(functools.partial(layer_kernel, tile_list, out_groups, raw...  2.49 us
  transfers between devices with their start and end apart: 30, of which 6 were waited for; matrix products, arithmetic and copies ran while one was open for 1% of the time, Pallas kernels for 10%

profile of v3, /device:TPU:0, one launch (start us, length us, event | category | flops | bytes accessed | tf_op | source)
XLA Modules:
  0.0 69.2 jit_solution(2719712505051869087)
XLA Ops:
  0.0 0.5 collective-permute-start.1
  0.5 1.0 %dynamic-slice_bitcast_fusion = (bf16[512,128]{1,0:T(8,128)(2,1)S(1)}, bf16[512,128]{1,0:T(8,128)(2,1)S(1)}) fusion(bf16[2,512,128]{2,1,0:T(8,128)(2,1)} %bitcast.21, s32[]{:T(128)S(6)} %select_n.24, s32[]{:T(128)S(6)} %select_n.23), kind=kLoop, calls=%fused_computation.1 | loop fusion | bytes 524296 | tf_op jit(solution)/shard_map/jit(dynamic_index_in_dim)/squeeze | solution.py:161
  1.5 4.1 %collective-permute-start.3 = (bf16[512,128]{1,0:T(8,128)(2,1)S(1)}, bf16[512,128]{1,0:T(8,128)(2,1)S(1)}, u32[]{:S(2)}, u32[]{:S(2)}) collective-permute-start(bf16[512,128]{1,0:T(8,128)(2,1)S(1)} %get-tuple-element.111), channel_id=1, source_target_pairs={{0,8},{1,9},{2,3},{3,2},{4,12},{5,13},{6,7},{7,6},{8,0},{9,1},{10,... | collective-permute-start | bytes 393224 | tf_op jit(solution)/shard_map/ppermute | solution.py:148
  5.6 1.5 %collective-permute-start.8 = (bf16[512,128]{1,0:T(8,128)(2,1)S(1)}, bf16[512,128]{1,0:T(8,128)(2,1)S(1)}, u32[]{:S(2)}, u32[]{:S(2)}) collective-permute-start(bf16[512,128]{1,0:T(8,128)(2,1)S(1)} %get-tuple-element.112.refs_2_), channel_id=1, source_target_pairs={{0,2},{1,3},{2,0},{3,1},{4,6},{5,7},{6,4},{7,5},{8,10},{9,11},{10,... | collective-permute-start | bytes 393224 | tf_op jit(solution)/shard_map/ppermute | solution.py:148
  7.1 1.8 %collective-permute-start.2 = (bf16[512,128]{1,0:T(8,128)(2,1)S(1)}, bf16[512,128]{1,0:T(8,128)(2,1)S(1)}, u32[]{:S(2)}, u32[]{:S(2)}) collective-permute-start(bf16[512,128]{1,0:T(8,128)(2,1)S(1)} %get-tuple-element.112.refs_2_), channel_id=1, source_target_pairs={{0,4},{1,5},{2,3},{3,2},{4,0},{5,1},{6,7},{7,6},{8,12},{9,13},{10,... | collective-permute-start | bytes 393224 | tf_op jit(solution)/shard_map/ppermute | solution.py:148
  9.0 1.6 %copy-done = bf16[1,4,2048,128]{3,2,1,0:T(8,128)(2,1)S(1)} copy-done((bf16[1,4,2048,128]{3,2,1,0:T(8,128)(2,1)S(1)}, bf16[1,4,2048,128]{3,2,1,0:T(8,128)(2,1)}, u32[]{:S(2)}) %copy-start) | copy-done | bytes 2097176
  10.6 0.7 copy-done.4
  11.3 0.7 copy-done.5
  11.9 2.9 %shard_map.74 = (bf16[4,2048,256]{2,1,0:T(8,128)(2,1)S(1)}, f32[4,256]{1,0:T(4,128)S(1)}) custom-call(s32[8,16]{1,0:T(8,128)S(1)} %bitcast.19, bf16[4,2048,128]{2,1,0:T(8,128)(2,1)S(1)} %bitcast.14, bf16[4,2048,128]{2,1,0:T(8,128)(2,1)S(1)} %collective-permute-done.1.other_tiles, f32[8,128]{1,0:T(8,128)S(1)} %bitcast.20), custom_call_target="tpu_custom_call" | custom-call | flops 1 | bytes 1 | tf_op jit(solution)/shard_map/pallas_call | solution.py:54
  15.3 1.7 %collective-permute-start.11 = (bf16[512,128]{1,0:T(8,128)(2,1)S(1)}, bf16[512,128]{1,0:T(8,128)(2,1)S(1)}, u32[]{:S(2)}, u32[]{:S(2)}) collective-permute-start(bf16[512,128]{1,0:T(8,128)(2,1)S(1)} %collective-permute-done.10.refs_4_), channel_id=1, source_target_pairs={{0,4},{1,5},{2,3},{3,2},{4,0},{5,1},{6,7},{7,6},{8,12},{9,13},{10,... | collective-permute-start | bytes 393224 | tf_op jit(solution)/shard_map/ppermute | solution.py:148
  17.0 0.3 collective-permute-start.9
  17.4 4.1 %collective-permute-done.4.refs_5_ = bf16[512,128]{1,0:T(8,128)(2,1)S(1)} collective-permute-done((bf16[512,128]{1,0:T(8,128)(2,1)S(1)}, bf16[512,128]{1,0:T(8,128)(2,1)S(1)}, u32[]{:S(2)}, u32[]{:S(2)}) %collective-permute-start.4) | collective-permute-done | bytes 131104 | tf_op jit(solution)/shard_map/ppermute | solution.py:148
  21.4 0.8 %shard_map.75 = (bf16[128,256]{1,0:T(8,128)(2,1)S(1)}, bf16[128,256]{1,0:T(8,128)(2,1)S(1)}, bf16[128,256]{1,0:T(8,128)(2,1)S(1)}, bf16[128,256]{1,0:T(8,128)(2,1)S(1)}) custom-call(bf16[4,2048,256]{2,1,0:T(8,128)(2,1)S(1)} %get-tuple-element.60.refs_0_, f32[4,256]{1,0:T(4,128)S(1)} %get-tuple-element.61.refs_1_, ...), custom_call_target="tpu_custom_call" | custom-call | flops 1 | bytes 1 | tf_op jit(solution)/shard_map/pallas_call | solution.py:123
  22.4 2.9 %collective-permute-start.6 = (bf16[128,256]{1,0:T(8,128)(2,1)S(1)}, bf16[128,256]{1,0:T(8,128)(2,1)S(1)}, u32[]{:S(2)}, u32[]{:S(2)}) collective-permute-start(bf16[128,256]{1,0:T(8,128)(2,1)S(1)} %get-tuple-element.65), channel_id=1, source_target_pairs={{0,8},{1,9},{2,3},{3,2},{4,12},{5,13},{6,7},{7,6},{8,0},{9,1},{10,... | collective-permute-start | bytes 196616 | tf_op jit(solution)/shard_map/ppermute | solution.py:148
  25.3 1.4 %collective-permute-start.7 = (bf16[128,256]{1,0:T(8,128)(2,1)S(1)}, bf16[128,256]{1,0:T(8,128)(2,1)S(1)}, u32[]{:S(2)}, u32[]{:S(2)}) collective-permute-start(bf16[128,256]{1,0:T(8,128)(2,1)S(1)} %get-tuple-element.66), channel_id=1, source_target_pairs={{0,12},{1,13},{2,3},{3,2},{4,8},{5,9},{6,7},{7,6},{8,4},{9,5},{10,... | collective-permute-start | bytes 196616 | tf_op jit(solution)/shard_map/ppermute | solution.py:148
  26.7 1.6 %shard_map.73 = (bf16[4,1024,256]{2,1,0:T(8,128)(2,1)S(1)}, f32[4,256]{1,0:T(4,128)S(1)}) custom-call(s32[8,8]{1,0:T(8,128)S(1)} %bitcast.17, bf16[4,1024,128]{2,1,0:T(8,128)(2,1)S(1)} %bitcast.16, bf16[4,1024,128]{2,1,0:T(8,128)(2,1)S(1)} %collective-permute-done.other_tiles, f32[8,128]{1,0:T(8,128)S(1)} %bitcast.18), custom_call_target="tpu_custom_call" | custom-call | flops 1 | bytes 1 | tf_op jit(solution)/shard_map/pallas_call | solution.py:54
  28.3 0.8 %shard_map.76 = (bf16[128,256]{1,0:T(8,128)(2,1)S(1)}, bf16[128,256]{1,0:T(8,128)(2,1)S(1)}, bf16[128,256]{1,0:T(8,128)(2,1)S(1)}, bf16[128,256]{1,0:T(8,128)(2,1)S(1)}) custom-call(bf16[4,2048,256]{2,1,0:T(8,128)(2,1)S(1)} %get-tuple-element.60.refs_0_, f32[4,256]{1,0:T(4,128)S(1)} %get-tuple-element.61.refs_1_, ...), custom_call_target="tpu_custom_call" | custom-call | flops 1 | bytes 1 | tf_op jit(solution)/shard_map/pallas_call | solution.py:123
  29.4 2.8 %collective-permute-start.17 = (bf16[128,256]{1,0:T(8,128)(2,1)S(1)}, bf16[128,256]{1,0:T(8,128)(2,1)S(1)}, u32[]{:S(2)}, u32[]{:S(2)}) collective-permute-start(bf16[128,256]{1,0:T(8,128)(2,1)S(1)} %get-tuple-element.73), channel_id=1, source_target_pairs={{0,8},{1,9},{2,3},{3,2},{4,12},{5,13},{6,7},{7,6},{8,0},{9,1},{10,... | collective-permute-start | bytes 196616 | tf_op jit(solution)/shard_map/ppermute | solution.py:148
  32.1 1.4 %collective-permute-start.18 = (bf16[128,256]{1,0:T(8,128)(2,1)S(1)}, bf16[128,256]{1,0:T(8,128)(2,1)S(1)}, u32[]{:S(2)}, u32[]{:S(2)}) collective-permute-start(bf16[128,256]{1,0:T(8,128)(2,1)S(1)} %get-tuple-element.74), channel_id=1, source_target_pairs={{0,12},{1,13},{2,3},{3,2},{4,8},{5,9},{6,7},{7,6},{8,4},{9,5},{10,... | collective-permute-start | bytes 196616 | tf_op jit(solution)/shard_map/ppermute | solution.py:148
  33.5 0.5 shard_map.77
  34.1 5.4 %collective-permute-start.14 = (bf16[128,512]{1,0:T(8,128)(2,1)S(1)}, bf16[128,512]{1,0:T(8,128)(2,1)S(1)}, u32[]{:S(2)}, u32[]{:S(2)}) collective-permute-start(bf16[128,512]{1,0:T(8,128)(2,1)S(1)} %get-tuple-element.80), channel_id=1, source_target_pairs={{0,10},{1,11},{2,0},{3,1},{4,14},{5,15},{6,4},{7,5},{8,2},{9,3},{1... | collective-permute-start | bytes 393224 | tf_op jit(solution)/shard_map/ppermute | solution.py:148
  39.5 0.5 shard_map.78
  40.0 2.9 %collective-permute-start.24 = (bf16[128,512]{1,0:T(8,128)(2,1)S(1)}, bf16[128,512]{1,0:T(8,128)(2,1)S(1)}, u32[]{:S(2)}, u32[]{:S(2)}) collective-permute-start(bf16[128,512]{1,0:T(8,128)(2,1)S(1)} %get-tuple-element.86), channel_id=1, source_target_pairs={{0,10},{1,11},{2,0},{3,1},{4,14},{5,15},{6,4},{7,5},{8,2},{9,3},{1... | collective-permute-start | bytes 393224 | tf_op jit(solution)/shard_map/ppermute | solution.py:148
  43.0 0.5 collective-permute-start.15
  43.5 1.5 %collective-permute-done.22.refs_2_ = bf16[128,512]{1,0:T(8,128)(2,1)S(1)} collective-permute-done((bf16[128,512]{1,0:T(8,128)(2,1)S(1)}, bf16[128,512]{1,0:T(8,128)(2,1)S(1)}, u32[]{:S(2)}, u32[]{:S(2)}) %collective-permute-start.22) | collective-permute-done | bytes 131104 | tf_op jit(solution)/shard_map/ppermute | solution.py:148
  45.0 1.4 %collective-permute-done.24.refs_4_ = bf16[128,512]{1,0:T(8,128)(2,1)S(1)} collective-permute-done((bf16[128,512]{1,0:T(8,128)(2,1)S(1)}, bf16[128,512]{1,0:T(8,128)(2,1)S(1)}, u32[]{:S(2)}, u32[]{:S(2)}) %collective-permute-start.24) | collective-permute-done | bytes 131104 | tf_op jit(solution)/shard_map/ppermute | solution.py:148
  46.4 0.5 collective-permute-start.19
  47.0 0.4 collective-permute-start.21
  47.9 0.4 collective-permute-start.28
  48.4 15.7 %collective-permute-start.26 = (bf16[1024,128]{1,0:T(8,128)(2,1)S(1)}, bf16[1024,128]{1,0:T(8,128)(2,1)S(1)}, u32[]{:S(2)}, u32[]{:S(2)}) collective-permute-start(bf16[1024,128]{1,0:T(8,128)(2,1)S(1)} %shard_map.81), channel_id=1, source_target_pairs={{0,2},{1,3},{2,0},{3,1},{4,6},{5,7},{6,4},{7,5},{8,10},{9,11},{10,... | collective-permute-start | bytes 786440 | tf_op jit(solution)/shard_map/ppermute | solution.py:148
  64.1 4.3 %collective-permute-done.26 = bf16[1024,128]{1,0:T(8,128)(2,1)S(1)} collective-permute-done((bf16[1024,128]{1,0:T(8,128)(2,1)S(1)}, bf16[1024,128]{1,0:T(8,128)(2,1)S(1)}, u32[]{:S(2)}, u32[]{:S(2)}) %collective-permute-start.26) | collective-permute-done | bytes 262176 | tf_op jit(solution)/shard_map/ppermute | solution.py:148
  68.4 0.7 %select_bitcast_fusion = bf16[1,1024,128]{2,1,0:T(8,128)(2,1)} fusion(bf16[1024,128]{1,0:T(8,128)(2,1)S(1)} %collective-permute-done.26, bf16[1024,128]{1,0:T(8,128)(2,1)S(1)} %shard_map.82, pred[]{:T(512)S(6)} %eq.3), kind=kLoop, calls=%fused_computation | loop fusion | flops 131072 | bytes 786433 | tf_op jit(solution)/shard_map/broadcast_in_dim | solution.py:208
  (52 shorter events, 2.0 us)
Async XLA Ops:
  0.0 7.1 %collective-permute-start.1 = (bf16[4,2048,128]{2,1,0:T(8,128)(2,1)}, bf16[4,2048,128]{2,1,0:T(8,128)(2,1)S(1)}, u32[]{:S(2)}, u32[]{:S(2)}) collective-permute-start(bf16[4,2048,128]{2,1,0:T(8,128)(2,1)} %bitcast.13), channel_id=1, source_target_pairs={{0,1},{1,0},{2,3},{3,2},{4,5},{5,4},{6,7},{7,6},{8,9},{9,8},{10,11... | collective-permute-start | bytes 6291464 | tf_op jit(solution)/shard_map/ppermute | solution.py:157
  0.5 24.8 %collective-permute-start = (bf16[4,1024,128]{2,1,0:T(8,128)(2,1)}, bf16[4,1024,128]{2,1,0:T(8,128)(2,1)S(1)}, u32[]{:S(2)}, u32[]{:S(2)}) collective-permute-start(bf16[4,1024,128]{2,1,0:T(8,128)(2,1)} %bitcast.15), channel_id=1, source_target_pairs={{0,1},{1,0},{2,3},{3,2},{4,5},{5,4},{6,7},{7,6},{8,9},{9,8},{10,11... | collective-permute-start | bytes 3145736 | tf_op jit(solution)/shard_map/ppermute | solution.py:157
  1.5 13.4 %collective-permute-start.3 = (bf16[512,128]{1,0:T(8,128)(2,1)S(1)}, bf16[512,128]{1,0:T(8,128)(2,1)S(1)}, u32[]{:S(2)}, u32[]{:S(2)}) collective-permute-start(bf16[512,128]{1,0:T(8,128)(2,1)S(1)} %get-tuple-element.111), channel_id=1, source_target_pairs={{0,8},{1,9},{2,3},{3,2},{4,12},{5,13},{6,7},{7,6},{8,0},{9,1},{10,... | collective-permute-start | bytes 393224 | tf_op jit(solution)/shard_map/ppermute | solution.py:148
  5.6 9.7 %collective-permute-start.10 = (bf16[512,128]{1,0:T(8,128)(2,1)S(1)}, bf16[512,128]{1,0:T(8,128)(2,1)S(1)}, u32[]{:S(2)}, u32[]{:S(2)}) collective-permute-start(bf16[512,128]{1,0:T(8,128)(2,1)S(1)} %get-tuple-element.111), channel_id=1, source_target_pairs={{0,2},{1,3},{2,8},{3,9},{4,6},{5,7},{6,12},{7,13},{8,10},{9,11},{1... | collective-permute-start | bytes 393224 | tf_op jit(solution)/shard_map/ppermute | solution.py:148
  5.6 11.4 %collective-permute-start.8 = (bf16[512,128]{1,0:T(8,128)(2,1)S(1)}, bf16[512,128]{1,0:T(8,128)(2,1)S(1)}, u32[]{:S(2)}, u32[]{:S(2)}) collective-permute-start(bf16[512,128]{1,0:T(8,128)(2,1)S(1)} %get-tuple-element.112.refs_2_), channel_id=1, source_target_pairs={{0,2},{1,3},{2,0},{3,1},{4,6},{5,7},{6,4},{7,5},{8,10},{9,11},{10,... | collective-permute-start | bytes 393224 | tf_op jit(solution)/shard_map/ppermute | solution.py:148
  7.1 10.2 %collective-permute-start.2 = (bf16[512,128]{1,0:T(8,128)(2,1)S(1)}, bf16[512,128]{1,0:T(8,128)(2,1)S(1)}, u32[]{:S(2)}, u32[]{:S(2)}) collective-permute-start(bf16[512,128]{1,0:T(8,128)(2,1)S(1)} %get-tuple-element.112.refs_2_), channel_id=1, source_target_pairs={{0,4},{1,5},{2,3},{3,2},{4,0},{5,1},{6,7},{7,6},{8,12},{9,13},{10,... | collective-permute-start | bytes 393224 | tf_op jit(solution)/shard_map/ppermute | solution.py:148
  14.9 6.5 %collective-permute-start.4 = (bf16[512,128]{1,0:T(8,128)(2,1)S(1)}, bf16[512,128]{1,0:T(8,128)(2,1)S(1)}, u32[]{:S(2)}, u32[]{:S(2)}) collective-permute-start(bf16[512,128]{1,0:T(8,128)(2,1)S(1)} %collective-permute-done.3.refs_4_), channel_id=1, source_target_pairs={{0,4},{1,5},{2,3},{3,2},{4,0},{5,1},{6,7},{7,6},{8,12},{9,13},{10,... | collective-permute-start | bytes 393224 | tf_op jit(solution)/shard_map/ppermute | solution.py:148
  15.3 12.9 %collective-permute-start.11 = (bf16[512,128]{1,0:T(8,128)(2,1)S(1)}, bf16[512,128]{1,0:T(8,128)(2,1)S(1)}, u32[]{:S(2)}, u32[]{:S(2)}) collective-permute-start(bf16[512,128]{1,0:T(8,128)(2,1)S(1)} %collective-permute-done.10.refs_4_), channel_id=1, source_target_pairs={{0,4},{1,5},{2,3},{3,2},{4,0},{5,1},{6,7},{7,6},{8,12},{9,13},{10,... | collective-permute-start | bytes 393224 | tf_op jit(solution)/shard_map/ppermute | solution.py:148
  17.0 11.2 %collective-permute-start.9 = (bf16[512,128]{1,0:T(8,128)(2,1)S(1)}, bf16[512,128]{1,0:T(8,128)(2,1)S(1)}, u32[]{:S(2)}, u32[]{:S(2)}) collective-permute-start(bf16[512,128]{1,0:T(8,128)(2,1)S(1)} %collective-permute-done.8.refs_2_), channel_id=1, source_target_pairs={{0,4},{1,5},{2,3},{3,2},{4,0},{5,1},{6,7},{7,6},{8,12},{9,13},{10,... | collective-permute-start | bytes 393224 | tf_op jit(solution)/shard_map/ppermute | solution.py:148
  21.4 5.2 %copy-start.2 = (s32[1,8,8]{2,1,0:T(8,128)S(1)}, s32[1,8,8]{2,1,0:T(8,128)}, u32[]{:S(2)}) copy-start(s32[1,8,8]{2,1,0:T(8,128)} %param.13) | copy-start | bytes 772
  21.4 5.2 %copy-start.3 = (f32[1,1024]{1,0:T(1,128)S(1)}, f32[1,1024]{1,0:T(1,128)}, u32[]{:S(2)}) copy-start(f32[1,1024]{1,0:T(1,128)} %param.11) | copy-start | bytes 12292
  22.2 9.9 %collective-permute-start.5 = (bf16[128,256]{1,0:T(8,128)(2,1)S(1)}, bf16[128,256]{1,0:T(8,128)(2,1)S(1)}, u32[]{:S(2)}, u32[]{:S(2)}) collective-permute-start(bf16[128,256]{1,0:T(8,128)(2,1)S(1)} %get-tuple-element.64), channel_id=1, source_target_pairs={{0,4},{1,5},{2,3},{3,2},{4,0},{5,1},{6,7},{7,6},{8,12},{9,13},{10,... | collective-permute-start | bytes 196616 | tf_op jit(solution)/shard_map/ppermute | solution.py:148
  22.4 11.1 %collective-permute-start.6 = (bf16[128,256]{1,0:T(8,128)(2,1)S(1)}, bf16[128,256]{1,0:T(8,128)(2,1)S(1)}, u32[]{:S(2)}, u32[]{:S(2)}) collective-permute-start(bf16[128,256]{1,0:T(8,128)(2,1)S(1)} %get-tuple-element.65), channel_id=1, source_target_pairs={{0,8},{1,9},{2,3},{3,2},{4,12},{5,13},{6,7},{7,6},{8,0},{9,1},{10,... | collective-permute-start | bytes 196616 | tf_op jit(solution)/shard_map/ppermute | solution.py:148
  25.3 8.2 %collective-permute-start.7 = (bf16[128,256]{1,0:T(8,128)(2,1)S(1)}, bf16[128,256]{1,0:T(8,128)(2,1)S(1)}, u32[]{:S(2)}, u32[]{:S(2)}) collective-permute-start(bf16[128,256]{1,0:T(8,128)(2,1)S(1)} %get-tuple-element.66), channel_id=1, source_target_pairs={{0,12},{1,13},{2,3},{3,2},{4,8},{5,9},{6,7},{7,6},{8,4},{9,5},{10,... | collective-permute-start | bytes 196616 | tf_op jit(solution)/shard_map/ppermute | solution.py:148
  29.0 10.4 %collective-permute-start.16 = (bf16[128,256]{1,0:T(8,128)(2,1)S(1)}, bf16[128,256]{1,0:T(8,128)(2,1)S(1)}, u32[]{:S(2)}, u32[]{:S(2)}) collective-permute-start(bf16[128,256]{1,0:T(8,128)(2,1)S(1)} %get-tuple-element.72), channel_id=1, source_target_pairs={{0,4},{1,5},{2,3},{3,2},{4,0},{5,1},{6,7},{7,6},{8,12},{9,13},{10,... | collective-permute-start | bytes 196616 | tf_op jit(solution)/shard_map/ppermute | solution.py:148
  29.4 10.1 %collective-permute-start.17 = (bf16[128,256]{1,0:T(8,128)(2,1)S(1)}, bf16[128,256]{1,0:T(8,128)(2,1)S(1)}, u32[]{:S(2)}, u32[]{:S(2)}) collective-permute-start(bf16[128,256]{1,0:T(8,128)(2,1)S(1)} %get-tuple-element.73), channel_id=1, source_target_pairs={{0,8},{1,9},{2,3},{3,2},{4,12},{5,13},{6,7},{7,6},{8,0},{9,1},{10,... | collective-permute-start | bytes 196616 | tf_op jit(solution)/shard_map/ppermute | solution.py:148
  32.1 7.3 %collective-permute-start.18 = (bf16[128,256]{1,0:T(8,128)(2,1)S(1)}, bf16[128,256]{1,0:T(8,128)(2,1)S(1)}, u32[]{:S(2)}, u32[]{:S(2)}) collective-permute-start(bf16[128,256]{1,0:T(8,128)(2,1)S(1)} %get-tuple-element.74), channel_id=1, source_target_pairs={{0,12},{1,13},{2,3},{3,2},{4,8},{5,9},{6,7},{7,6},{8,4},{9,5},{10,... | collective-permute-start | bytes 196616 | tf_op jit(solution)/shard_map/ppermute | solution.py:148
  34.0 9.0 %collective-permute-start.12 = (bf16[128,512]{1,0:T(8,128)(2,1)S(1)}, bf16[128,512]{1,0:T(8,128)(2,1)S(1)}, u32[]{:S(2)}, u32[]{:S(2)}) collective-permute-start(bf16[128,512]{1,0:T(8,128)(2,1)S(1)} %get-tuple-element.79), channel_id=1, source_target_pairs={{0,2},{1,3},{2,0},{3,1},{4,6},{5,7},{6,4},{7,5},{8,10},{9,11},{10,... | collective-permute-start | bytes 393224 | tf_op jit(solution)/shard_map/ppermute | solution.py:148
  34.1 8.9 %collective-permute-start.14 = (bf16[128,512]{1,0:T(8,128)(2,1)S(1)}, bf16[128,512]{1,0:T(8,128)(2,1)S(1)}, u32[]{:S(2)}, u32[]{:S(2)}) collective-permute-start(bf16[128,512]{1,0:T(8,128)(2,1)S(1)} %get-tuple-element.80), channel_id=1, source_target_pairs={{0,10},{1,11},{2,0},{3,1},{4,14},{5,15},{6,4},{7,5},{8,2},{9,3},{1... | collective-permute-start | bytes 393224 | tf_op jit(solution)/shard_map/ppermute | solution.py:148
  40.0 5.0 %collective-permute-start.22 = (bf16[128,512]{1,0:T(8,128)(2,1)S(1)}, bf16[128,512]{1,0:T(8,128)(2,1)S(1)}, u32[]{:S(2)}, u32[]{:S(2)}) collective-permute-start(bf16[128,512]{1,0:T(8,128)(2,1)S(1)} %get-tuple-element.85), channel_id=1, source_target_pairs={{0,2},{1,3},{2,0},{3,1},{4,6},{5,7},{6,4},{7,5},{8,10},{9,11},{10,... | collective-permute-start | bytes 393224 | tf_op jit(solution)/shard_map/ppermute | solution.py:148
  40.0 6.4 %collective-permute-start.24 = (bf16[128,512]{1,0:T(8,128)(2,1)S(1)}, bf16[128,512]{1,0:T(8,128)(2,1)S(1)}, u32[]{:S(2)}, u32[]{:S(2)}) collective-permute-start(bf16[128,512]{1,0:T(8,128)(2,1)S(1)} %get-tuple-element.86), channel_id=1, source_target_pairs={{0,10},{1,11},{2,0},{3,1},{4,14},{5,15},{6,4},{7,5},{8,2},{9,3},{1... | collective-permute-start | bytes 393224 | tf_op jit(solution)/shard_map/ppermute | solution.py:148
  43.0 3.4 %collective-permute-start.13 = (bf16[128,512]{1,0:T(8,128)(2,1)S(1)}, bf16[128,512]{1,0:T(8,128)(2,1)S(1)}, u32[]{:S(2)}, u32[]{:S(2)}) collective-permute-start(bf16[128,512]{1,0:T(8,128)(2,1)S(1)} %collective-permute-done.12.refs_2_), channel_id=1, source_target_pairs={{0,1},{1,0},{2,6},{3,7},{4,5},{5,4},{6,2},{7,3},{8,9},{9,8},{10,14... | collective-permute-start | bytes 393224 | tf_op jit(solution)/shard_map/ppermute | solution.py:148
  43.0 3.4 %collective-permute-start.15 = (bf16[128,512]{1,0:T(8,128)(2,1)S(1)}, bf16[128,512]{1,0:T(8,128)(2,1)S(1)}, u32[]{:S(2)}, u32[]{:S(2)}) collective-permute-start(bf16[128,512]{1,0:T(8,128)(2,1)S(1)} %collective-permute-done.14.refs_4_), channel_id=1, source_target_pairs={{0,1},{1,0},{2,6},{3,7},{4,5},{5,4},{6,2},{7,3},{8,9},{9,8},{10,14... | collective-permute-start | bytes 393224 | tf_op jit(solution)/shard_map/ppermute | solution.py:148
  45.0 2.4 %collective-permute-start.23 = (bf16[128,512]{1,0:T(8,128)(2,1)S(1)}, bf16[128,512]{1,0:T(8,128)(2,1)S(1)}, u32[]{:S(2)}, u32[]{:S(2)}) collective-permute-start(bf16[128,512]{1,0:T(8,128)(2,1)S(1)} %collective-permute-done.22.refs_2_), channel_id=1, source_target_pairs={{0,1},{1,0},{2,6},{3,7},{4,5},{5,4},{6,2},{7,3},{8,9},{9,8},{10,14... | collective-permute-start | bytes 393224 | tf_op jit(solution)/shard_map/ppermute | solution.py:148
  46.4 1.3 %collective-permute-start.25 = (bf16[128,512]{1,0:T(8,128)(2,1)S(1)}, bf16[128,512]{1,0:T(8,128)(2,1)S(1)}, u32[]{:S(2)}, u32[]{:S(2)}) collective-permute-start(bf16[128,512]{1,0:T(8,128)(2,1)S(1)} %collective-permute-done.24.refs_4_), channel_id=1, source_target_pairs={{0,1},{1,0},{2,6},{3,7},{4,5},{5,4},{6,2},{7,3},{8,9},{9,8},{10,14... | collective-permute-start | bytes 393224 | tf_op jit(solution)/shard_map/ppermute | solution.py:148
  46.4 1.8 %collective-permute-start.19 = (bf16[128,256]{1,0:T(8,128)(2,1)S(1)}, bf16[128,256]{1,0:T(8,128)(2,1)S(1)}, u32[]{:S(2)}, u32[]{:S(2)}) collective-permute-start(bf16[128,256]{1,0:T(8,128)(2,1)S(1)} %get-tuple-element.92), channel_id=1, source_target_pairs={{0,1},{1,0},{2,6},{3,7},{4,5},{5,4},{6,2},{7,3},{8,9},{9,8},{10,14... | collective-permute-start | bytes 196616 | tf_op jit(solution)/shard_map/ppermute | solution.py:148
  46.9 1.5 %collective-permute-start.20 = (bf16[128,256]{1,0:T(8,128)(2,1)S(1)}, bf16[128,256]{1,0:T(8,128)(2,1)S(1)}, u32[]{:S(2)}, u32[]{:S(2)}) collective-permute-start(bf16[128,256]{1,0:T(8,128)(2,1)S(1)} %get-tuple-element.93), channel_id=1, source_target_pairs={{0,1},{1,0},{2,10},{3,11},{4,5},{5,4},{6,14},{7,15},{8,9},{9,8},{1... | collective-permute-start | bytes 196616 | tf_op jit(solution)/shard_map/ppermute | solution.py:148
  47.0 1.4 %collective-permute-start.21 = (bf16[128,256]{1,0:T(8,128)(2,1)S(1)}, bf16[128,256]{1,0:T(8,128)(2,1)S(1)}, u32[]{:S(2)}, u32[]{:S(2)}) collective-permute-start(bf16[128,256]{1,0:T(8,128)(2,1)S(1)} %get-tuple-element.94), channel_id=1, source_target_pairs={{0,1},{1,0},{2,14},{3,15},{4,5},{5,4},{6,10},{7,11},{8,9},{9,8},{1... | collective-permute-start | bytes 196616 | tf_op jit(solution)/shard_map/ppermute | solution.py:148
  47.8 16.3 %collective-permute-start.27 = (bf16[128,256]{1,0:T(8,128)(2,1)S(1)}, bf16[128,256]{1,0:T(8,128)(2,1)S(1)}, u32[]{:S(2)}, u32[]{:S(2)}) collective-permute-start(bf16[128,256]{1,0:T(8,128)(2,1)S(1)} %get-tuple-element.100), channel_id=1, source_target_pairs={{0,1},{1,0},{2,6},{3,7},{4,5},{5,4},{6,2},{7,3},{8,9},{9,8},{10,14... | collective-permute-start | bytes 196616 | tf_op jit(solution)/shard_map/ppermute | solution.py:148
  47.9 16.2 %collective-permute-start.28 = (bf16[128,256]{1,0:T(8,128)(2,1)S(1)}, bf16[128,256]{1,0:T(8,128)(2,1)S(1)}, u32[]{:S(2)}, u32[]{:S(2)}) collective-permute-start(bf16[128,256]{1,0:T(8,128)(2,1)S(1)} %get-tuple-element.101), channel_id=1, source_target_pairs={{0,1},{1,0},{2,10},{3,11},{4,5},{5,4},{6,14},{7,15},{8,9},{9,8},{1... | collective-permute-start | bytes 196616 | tf_op jit(solution)/shard_map/ppermute | solution.py:148
  48.3 15.8 %collective-permute-start.29 = (bf16[128,256]{1,0:T(8,128)(2,1)S(1)}, bf16[128,256]{1,0:T(8,128)(2,1)S(1)}, u32[]{:S(2)}, u32[]{:S(2)}) collective-permute-start(bf16[128,256]{1,0:T(8,128)(2,1)S(1)} %get-tuple-element.102), channel_id=1, source_target_pairs={{0,1},{1,0},{2,14},{3,15},{4,5},{5,4},{6,10},{7,11},{8,9},{9,8},{1... | collective-permute-start | bytes 196616 | tf_op jit(solution)/shard_map/ppermute | solution.py:148
  48.4 20.0 %collective-permute-start.26 = (bf16[1024,128]{1,0:T(8,128)(2,1)S(1)}, bf16[1024,128]{1,0:T(8,128)(2,1)S(1)}, u32[]{:S(2)}, u32[]{:S(2)}) collective-permute-start(bf16[1024,128]{1,0:T(8,128)(2,1)S(1)} %shard_map.81), channel_id=1, source_target_pairs={{0,2},{1,3},{2,0},{3,1},{4,6},{5,7},{6,4},{7,5},{8,10},{9,11},{10,... | collective-permute-start | bytes 786440 | tf_op jit(solution)/shard_map/ppermute | solution.py:148
  (4 other events, 8.2 us)

commit v4 on v3

--- a/solution.py
+++ b/solution.py
@@ -12,61 +12,62 @@
 TAIL = 10**10
 
 
-def order_kernel(links, own_tiles, other_tiles, bias, ordered, shifts, own_here, bias_here, arrivals):
-    own_copy = pltpu.make_async_copy(own_tiles, own_here, arrivals.at[0])
-    bias_copy = pltpu.make_async_copy(bias, bias_here, arrivals.at[1])
-    own_copy.start()
-    bias_copy.start()
+def place_tiles(links, source, ordered, first):
     owner_count = ordered.shape[0]
-    me, rep = lax.axis_index("owners"), lax.axis_index("rep")
-    half, _, size = own_tiles.shape
+    me = lax.axis_index("owners")
+    half, _, size = source.shape
     slots = links.shape[1]
     width = 2 * size
-    for ours, source in ((False, other_tiles), (True, own_here)):
-        if ours:
-            own_copy.wait()
-        first = (rep if ours else 1 - rep) * half
-        for block in range(half):
-            row = first + block
-            distance = (row // 2) ^ me
-            for slot in range(slots):
-                place = links[row, slot]
-                sender = ((place // 2) & (owner_count - 1)) ^ me
-                if slots > 2 * owner_count:
-                    part = (place // (2 * owner_count)) ^ (me & 1)
-                    key = 2 * sender + part
-                else:
-                    key = sender
-                low = pl.multiple_of(key * width + (place & 1) * size, size)
-                ordered[distance, pl.ds(low, size), pl.ds(block % 2 * size, size)] = source[
-                    block, pl.ds(slot * size, size), :
-                ]
-    bias_copy.wait()
-    for distance in range(owner_count):
+    for block in range(half):
+        row = first + block
+        distance = (row // 2) ^ me
+        for slot in range(slots):
+            place = links[row, slot]
+            sender = ((place // 2) & (owner_count - 1)) ^ me
+            if slots > 2 * owner_count:
+                part = (place // (2 * owner_count)) ^ (me & 1)
+                key = 2 * sender + part
+            else:
+                key = sender
+            low = pl.multiple_of(key * width + (place & 1) * size, size)
+            ordered[distance, pl.ds(low, size), pl.ds(block % 2 * size, size)] = source[
+                block, pl.ds(slot * size, size), :
+            ]
+
+
+def order_other_kernel(links, other_tiles, ordered):
+    place_tiles(links, other_tiles, ordered, (1 - lax.axis_index("rep")) * other_tiles.shape[0])
+
+
+def order_own_kernel(links, own_tiles, bias, half_ordered, ordered, shifts):
+    place_tiles(links, own_tiles, ordered, lax.axis_index("rep") * own_tiles.shape[0])
+    size = own_tiles.shape[2]
+    for distance in range(shifts.shape[0]):
         for j in range(2):
-            shifts[pl.ds(distance, 1), pl.ds(j * size, size)] = bias_here[pl.ds(2 * (me ^ distance) + j, 1), :]
+            row = 2 * (lax.axis_index("owners") ^ distance) + j
+            shifts[pl.ds(distance, 1), pl.ds(j * size, size)] = bias[pl.ds(row, 1), :]
 
 
 def order_weights(links, own_tiles, other_tiles, bias):
     half, depth, size = own_tiles.shape
     vmem = pl.BlockSpec(memory_space=pltpu.VMEM)
-    hbm = pl.BlockSpec(memory_space=pl.ANY)
-    return pl.pallas_call(
-        order_kernel,
-        out_shape=[
-            jax.ShapeDtypeStruct((half, depth, 2 * size), jnp.bfloat16),
-            jax.ShapeDtypeStruct((half, 2 * size), jnp.float32),
-        ],
-        in_specs=[pl.BlockSpec(memory_space=pltpu.SMEM), hbm, vmem, hbm],
-        out_specs=[vmem, vmem],
-        scratch_shapes=[
-            pltpu.VMEM(own_tiles.shape, jnp.bfloat16),
-            pltpu.VMEM(bias.shape, jnp.float32),
-            pltpu.SemaphoreType.DMA((2,)),
-        ],
+    smem = pl.BlockSpec(memory_space=pltpu.SMEM)
+    ordered = jax.ShapeDtypeStruct((half, depth, 2 * size), jnp.bfloat16)
+    common = dict(
         compiler_params=pltpu.CompilerParams(vmem_limit_bytes=24 * 2**20),
         cost_estimate=pl.CostEstimate(flops=1, bytes_accessed=1, transcendentals=0),
-    )(links, own_tiles, other_tiles, bias)
+    )
+    half_ordered = pl.pallas_call(
+        order_other_kernel, out_shape=ordered, in_specs=[smem, vmem], out_specs=vmem, **common
+    )(links, other_tiles)
+    return pl.pallas_call(
+        order_own_kernel,
+        out_shape=[ordered, jax.ShapeDtypeStruct((half, 2 * size), jnp.float32)],
+        in_specs=[smem, vmem, vmem, vmem],
+        out_specs=[vmem, vmem],
+        input_output_aliases={3: 0},
+        **common,
+    )(links, own_tiles, bias, half_ordered)
 
 
 def layer_kernel(tile_list, out_groups, raw, final, active_section, *refs):
@@ -151,7 +152,7 @@
         return lambda owner, place, core: (owner ^ distance, place, core) if place == section else (owner, place, 1 - core)
 
     def across(distance, section):
-        return lambda owner, place, core: (owner ^ distance if place == section else owner, 1 - place, core)
+        return lambda owner, place, core: (owner ^ distance if place == section else owner, 1 - place, 1 - core)
 
     def other_core(value):
         return lax.ppermute(value, "rep", [(0, 1), (1, 0)])
@@ -189,15 +190,15 @@
         return layer(*first, buffers, spots, apart, active, raw=raw, cost=cost)
 
     def second_layer(parts, active, earlier, **more):
-        arrived = [moved(parts[distance], within(distance, active)) for distance in (3, 2, 1)]
-        buffers = after([parts[0], *arrived[::-1]], earlier)
+        arrived = {distance: moved(parts[distance], within(distance, active)) for distance in (2, 1, 3)}
+        buffers = after([parts[0]] + [arrived[distance] for distance in range(1, owner_count)], earlier)
         return layer(*second, buffers, second_tiles, joined, active, **more)
 
     def hand_over(result):
         close, apart = result
         return gathered(moved(close, across(0, 0)), moved(apart, across(2, 0)), 1)
 
-    parts_zero = first_layer(start, 0, True, cost=LAG)
+    parts_zero = first_layer(after(start, second[0]), 0, True, cost=LAG)
     parts_one = first_layer(after(later, parts_zero), 0, True)
     zero = second_layer(parts_zero, 0, parts_one, cost=LAG)
     one = second_layer(parts_one, 0, zero)

time: 69.4 us -> 67.6 us (0.974); the launches traced: 69.2 us -> 66.7 us
  starting transfers between devices: 45.5 us -> 40.9 us
  waiting for transfers between devices: 11.8 us -> 15.2 us
  local copies, waits for them, and re-layouts: 3.96 us -> 1.7 us
  Pallas kernels: 7.02 us -> 7.96 us
    ppermute x28, starting transfers between devices: 45 us -> 40.4 us  [moved(): return lax.ppermute(value, ('owners', 'section', 'rep'), pairs)]
    ppermute x28, waiting for transfers between devices: 11.8 us -> 15.2 us  [moved(): return lax.ppermute(value, ('owners', 'section', 'rep'), pairs)]
    unnamed x12, local copies, waits for them, and re-layouts: 2.97 us -> 0.71 us
    pallas_call x2 -> x4, Pallas kernels: 4.53 us -> 5.49 us  [the longest x2 2.77 us: order_weights(): pl.pallas_call(order_own_kernel, out_shape=[ordered, jax.ShapeDtypeStruct...]
  transfers between devices with their start and end apart: 30 -> 30, of which waited for: 6 -> 7; matrix products, arithmetic and copies ran while one was open for 1% -> 1% of each run, Pallas kernels for 10% -> 12%
where the time goes in v4:
time: 67.6 us; the launch traced here: 66.7 us
  starting transfers between devices  40.9 us (61%)
  waiting for transfers between devices  15.2 us (22%)
  Pallas kernels  7.96 us (12%)
  local copies, waits for them, and re-layouts  1.7 us (3%)
  other arithmetic  0.73 us (1%)
    ppermute x28, starting transfers between devices, moved(): return lax.ppermute(value, ('owners', 'section', 'rep'), pairs)  40.4 us
    ppermute x28, waiting for transfers between devices, moved(): return lax.ppermute(value, ('owners', 'section', 'rep'), pairs)  15.2 us
    pallas_call x2, Pallas kernels, order_weights(): pl.pallas_call(order_own_kernel, out_shape=[ordered, jax.ShapeDtypeStruct...  2.77 us
    pallas_call x2, Pallas kernels, order_weights(): pl.pallas_call(order_other_kernel, out_shape=ordered, in_specs=[smem, vme...  2.72 us
    pallas_call x8, Pallas kernels, layer(): pl.pallas_call(functools.partial(layer_kernel, tile_list, out_groups, raw...  2.47 us
  transfers between devices with their start and end apart: 30, of which 7 were waited for; matrix products, arithmetic and copies ran while one was open for 1% of the time, Pallas kernels for 12%

profile of v4, /device:TPU:0, one launch (start us, length us, event | category | flops | bytes accessed | tf_op | source)
XLA Modules:
  0.0 66.7 jit_solution(17775038454854721577)
XLA Ops:
  0.0 0.5 collective-permute-start.1
  0.5 1.0 %dynamic-slice_bitcast_fusion = (bf16[512,128]{1,0:T(8,128)(2,1)S(1)}, bf16[512,128]{1,0:T(8,128)(2,1)S(1)}) fusion(bf16[2,512,128]{2,1,0:T(8,128)(2,1)} %bitcast.23, s32[]{:T(128)S(6)} %select_n.24, s32[]{:T(128)S(6)} %select_n.23), kind=kLoop, calls=%fused_computation.1 | loop fusion | bytes 524296 | tf_op jit(solution)/shard_map/jit(dynamic_index_in_dim)/squeeze | solution.py:162
  1.5 4.1 %collective-permute-start.3 = (bf16[512,128]{1,0:T(8,128)(2,1)S(1)}, bf16[512,128]{1,0:T(8,128)(2,1)S(1)}, u32[]{:S(2)}, u32[]{:S(2)}) collective-permute-start(bf16[512,128]{1,0:T(8,128)(2,1)S(1)} %get-tuple-element.119), channel_id=1, source_target_pairs={{0,8},{1,9},{2,3},{3,2},{4,12},{5,13},{6,7},{7,6},{8,0},{9,1},{10,... | collective-permute-start | bytes 393224 | tf_op jit(solution)/shard_map/ppermute | solution.py:149
  5.6 1.2 %collective-permute-start.8 = (bf16[512,128]{1,0:T(8,128)(2,1)S(1)}, bf16[512,128]{1,0:T(8,128)(2,1)S(1)}, u32[]{:S(2)}, u32[]{:S(2)}) collective-permute-start(bf16[512,128]{1,0:T(8,128)(2,1)S(1)} %get-tuple-element.67.refs_2_), channel_id=1, source_target_pairs={{0,3},{1,2},{2,1},{3,0},{4,7},{5,6},{6,5},{7,4},{8,11},{9,10},{10,... | collective-permute-start | bytes 393224 | tf_op jit(solution)/shard_map/ppermute | solution.py:149
  6.9 1.8 %collective-permute-start.2 = (bf16[512,128]{1,0:T(8,128)(2,1)S(1)}, bf16[512,128]{1,0:T(8,128)(2,1)S(1)}, u32[]{:S(2)}, u32[]{:S(2)}) collective-permute-start(bf16[512,128]{1,0:T(8,128)(2,1)S(1)} %get-tuple-element.67.refs_2_), channel_id=1, source_target_pairs={{0,4},{1,5},{2,3},{3,2},{4,0},{5,1},{6,7},{7,6},{8,12},{9,13},{10,... | collective-permute-start | bytes 393224 | tf_op jit(solution)/shard_map/ppermute | solution.py:149
  8.7 0.7 %copy-done.3 = s32[1,8,16]{2,1,0:T(8,128)S(1)} copy-done((s32[1,8,16]{2,1,0:T(8,128)S(1)}, s32[1,8,16]{2,1,0:T(8,128)}, u32[]{:S(2)}) %copy-start.3) | copy-done | bytes 536
  9.4 1.7 %shard_map.75.half_ordered = bf16[4,2048,256]{2,1,0:T(8,128)(2,1)S(1)} custom-call(s32[8,16]{1,0:T(8,128)S(1)} %bitcast.19, bf16[4,2048,128]{2,1,0:T(8,128)(2,1)S(1)} %collective-permute-done.1.other_tiles), custom_call_target="tpu_custom_call" | custom-call | flops 1 | bytes 1 | tf_op jit(solution)/shard_map/pallas_call | solution.py:60
  11.1 1.7 %shard_map.76 = (bf16[4,2048,256]{2,1,0:T(8,128)(2,1)S(1)}, f32[4,256]{1,0:T(4,128)S(1)}) custom-call(s32[8,16]{1,0:T(8,128)S(1)} %bitcast.20, bf16[4,2048,128]{2,1,0:T(8,128)(2,1)S(1)} %bitcast.14, f32[8,128]{1,0:T(8,128)S(1)} %bitcast.21, bf16[4,2048,256]{2,1,0:T(8,128)(2,1)S(1)} %shard_map.75.half_ordered), custom_call_target="tpu_custom_call", output_to_operand_aliasing={{0}: (3, {})} | custom-call | flops 1 | bytes 1 | tf_op jit(solution)/shard_map/pallas_call | solution.py:63
  13.1 2.8 %collective-permute-done.10.refs_4_ = bf16[512,128]{1,0:T(8,128)(2,1)S(1)} collective-permute-done((bf16[512,128]{1,0:T(8,128)(2,1)S(1)}, bf16[512,128]{1,0:T(8,128)(2,1)S(1)}, u32[]{:S(2)}, u32[]{:S(2)}) %collective-permute-start.10) | collective-permute-done | bytes 131104 | tf_op jit(solution)/shard_map/ppermute | solution.py:149
  15.9 2.0 %collective-permute-start.9 = (bf16[512,128]{1,0:T(8,128)(2,1)S(1)}, bf16[512,128]{1,0:T(8,128)(2,1)S(1)}, u32[]{:S(2)}, u32[]{:S(2)}) collective-permute-start(bf16[512,128]{1,0:T(8,128)(2,1)S(1)} %collective-permute-done.8.refs_2_), channel_id=1, source_target_pairs={{0,4},{1,5},{2,3},{3,2},{4,0},{5,1},{6,7},{7,6},{8,12},{9,13},{10,... | collective-permute-start | bytes 393224 | tf_op jit(solution)/shard_map/ppermute | solution.py:149
  17.9 1.0 %shard_map.73.half_ordered = bf16[4,1024,256]{2,1,0:T(8,128)(2,1)S(1)} custom-call(s32[8,8]{1,0:T(8,128)S(1)} %bitcast.17, bf16[4,1024,128]{2,1,0:T(8,128)(2,1)S(1)} %collective-permute-done.other_tiles), custom_call_target="tpu_custom_call" | custom-call | flops 1 | bytes 1 | tf_op jit(solution)/shard_map/pallas_call | solution.py:60
  19.0 1.1 %shard_map.74 = (bf16[4,1024,256]{2,1,0:T(8,128)(2,1)S(1)}, f32[4,256]{1,0:T(4,128)S(1)}) custom-call(s32[8,8]{1,0:T(8,128)S(1)} %bitcast.18, bf16[4,1024,128]{2,1,0:T(8,128)(2,1)S(1)} %bitcast.16, f32[8,128]{1,0:T(8,128)S(1)} %bitcast.22, bf16[4,1024,256]{2,1,0:T(8,128)(2,1)S(1)} %shard_map.73.half_ordered), custom_call_target="tpu_custom_call", output_to_operand_aliasing={{0}: (3, {})} | custom-call | flops 1 | bytes 1 | tf_op jit(solution)/shard_map/pallas_call | solution.py:63
  20.1 0.8 %shard_map.77 = (bf16[128,256]{1,0:T(8,128)(2,1)S(1)}, bf16[128,256]{1,0:T(8,128)(2,1)S(1)}, bf16[128,256]{1,0:T(8,128)(2,1)S(1)}, bf16[128,256]{1,0:T(8,128)(2,1)S(1)}) custom-call(bf16[4,2048,256]{2,1,0:T(8,128)(2,1)S(1)} %get-tuple-element.64.refs_0_, f32[4,256]{1,0:T(4,128)S(1)} %get-tuple-element.65.refs_1_, ...), custom_call_target="tpu_custom_call" | custom-call | flops 1 | bytes 1 | tf_op jit(solution)/shard_map/pallas_call | solution.py:124
  21.0 2.6 %collective-permute-start.6 = (bf16[128,256]{1,0:T(8,128)(2,1)S(1)}, bf16[128,256]{1,0:T(8,128)(2,1)S(1)}, u32[]{:S(2)}, u32[]{:S(2)}) collective-permute-start(bf16[128,256]{1,0:T(8,128)(2,1)S(1)} %get-tuple-element.73), channel_id=1, source_target_pairs={{0,8},{1,9},{2,3},{3,2},{4,12},{5,13},{6,7},{7,6},{8,0},{9,1},{10,... | collective-permute-start | bytes 196616 | tf_op jit(solution)/shard_map/ppermute | solution.py:149
  23.5 1.8 %collective-permute-start.7 = (bf16[128,256]{1,0:T(8,128)(2,1)S(1)}, bf16[128,256]{1,0:T(8,128)(2,1)S(1)}, u32[]{:S(2)}, u32[]{:S(2)}) collective-permute-start(bf16[128,256]{1,0:T(8,128)(2,1)S(1)} %get-tuple-element.74), channel_id=1, source_target_pairs={{0,12},{1,13},{2,3},{3,2},{4,8},{5,9},{6,7},{7,6},{8,4},{9,5},{10,... | collective-permute-start | bytes 196616 | tf_op jit(solution)/shard_map/ppermute | solution.py:149
  25.6 0.8 %shard_map.78 = (bf16[128,256]{1,0:T(8,128)(2,1)S(1)}, bf16[128,256]{1,0:T(8,128)(2,1)S(1)}, bf16[128,256]{1,0:T(8,128)(2,1)S(1)}, bf16[128,256]{1,0:T(8,128)(2,1)S(1)}) custom-call(bf16[4,2048,256]{2,1,0:T(8,128)(2,1)S(1)} %get-tuple-element.64.refs_0_, f32[4,256]{1,0:T(4,128)S(1)} %get-tuple-element.65.refs_1_, ...), custom_call_target="tpu_custom_call" | custom-call | flops 1 | bytes 1 | tf_op jit(solution)/shard_map/pallas_call | solution.py:124
  26.4 3.2 %collective-permute-start.17 = (bf16[128,256]{1,0:T(8,128)(2,1)S(1)}, bf16[128,256]{1,0:T(8,128)(2,1)S(1)}, u32[]{:S(2)}, u32[]{:S(2)}) collective-permute-start(bf16[128,256]{1,0:T(8,128)(2,1)S(1)} %get-tuple-element.81), channel_id=1, source_target_pairs={{0,8},{1,9},{2,3},{3,2},{4,12},{5,13},{6,7},{7,6},{8,0},{9,1},{10,... | collective-permute-start | bytes 196616 | tf_op jit(solution)/shard_map/ppermute | solution.py:149
  29.6 1.1 %collective-permute-start.18 = (bf16[128,256]{1,0:T(8,128)(2,1)S(1)}, bf16[128,256]{1,0:T(8,128)(2,1)S(1)}, u32[]{:S(2)}, u32[]{:S(2)}) collective-permute-start(bf16[128,256]{1,0:T(8,128)(2,1)S(1)} %get-tuple-element.82), channel_id=1, source_target_pairs={{0,12},{1,13},{2,3},{3,2},{4,8},{5,9},{6,7},{7,6},{8,4},{9,5},{10,... | collective-permute-start | bytes 196616 | tf_op jit(solution)/shard_map/ppermute | solution.py:149
  30.8 0.5 shard_map.79
  31.4 3.6 %collective-permute-start.14 = (bf16[128,512]{1,0:T(8,128)(2,1)S(1)}, bf16[128,512]{1,0:T(8,128)(2,1)S(1)}, u32[]{:S(2)}, u32[]{:S(2)}) collective-permute-start(bf16[128,512]{1,0:T(8,128)(2,1)S(1)} %get-tuple-element.88), channel_id=1, source_target_pairs={{0,11},{1,10},{2,1},{3,0},{4,15},{5,14},{6,5},{7,4},{8,3},{9,2},{1... | collective-permute-start | bytes 393224 | tf_op jit(solution)/shard_map/ppermute | solution.py:149
  35.0 2.6 %collective-permute-done.17.refs_4_ = bf16[128,256]{1,0:T(8,128)(2,1)S(1)} collective-permute-done((bf16[128,256]{1,0:T(8,128)(2,1)S(1)}, bf16[128,256]{1,0:T(8,128)(2,1)S(1)}, u32[]{:S(2)}, u32[]{:S(2)}) %collective-permute-start.17) | collective-permute-done | bytes 65568 | tf_op jit(solution)/shard_map/ppermute | solution.py:149
  37.6 0.5 shard_map.80
  38.1 2.7 %collective-permute-start.24 = (bf16[128,512]{1,0:T(8,128)(2,1)S(1)}, bf16[128,512]{1,0:T(8,128)(2,1)S(1)}, u32[]{:S(2)}, u32[]{:S(2)}) collective-permute-start(bf16[128,512]{1,0:T(8,128)(2,1)S(1)} %get-tuple-element.94), channel_id=1, source_target_pairs={{0,11},{1,10},{2,1},{3,0},{4,15},{5,14},{6,5},{7,4},{8,3},{9,2},{1... | collective-permute-start | bytes 393224 | tf_op jit(solution)/shard_map/ppermute | solution.py:149
  40.8 0.5 collective-permute-start.15
  41.3 1.8 %collective-permute-done.22.refs_2_ = bf16[128,512]{1,0:T(8,128)(2,1)S(1)} collective-permute-done((bf16[128,512]{1,0:T(8,128)(2,1)S(1)}, bf16[128,512]{1,0:T(8,128)(2,1)S(1)}, u32[]{:S(2)}, u32[]{:S(2)}) %collective-permute-start.22) | collective-permute-done | bytes 131104 | tf_op jit(solution)/shard_map/ppermute | solution.py:149
  43.1 0.8 %collective-permute-done.24.refs_4_ = bf16[128,512]{1,0:T(8,128)(2,1)S(1)} collective-permute-done((bf16[128,512]{1,0:T(8,128)(2,1)S(1)}, bf16[128,512]{1,0:T(8,128)(2,1)S(1)}, u32[]{:S(2)}, u32[]{:S(2)}) %collective-permute-start.24) | collective-permute-done | bytes 131104 | tf_op jit(solution)/shard_map/ppermute | solution.py:149
  43.9 0.5 collective-permute-start.19
  44.5 0.4 collective-permute-start.21
  45.4 0.4 collective-permute-start.28
  45.9 13.4 %collective-permute-start.26 = (bf16[1024,128]{1,0:T(8,128)(2,1)S(1)}, bf16[1024,128]{1,0:T(8,128)(2,1)S(1)}, u32[]{:S(2)}, u32[]{:S(2)}) collective-permute-start(bf16[1024,128]{1,0:T(8,128)(2,1)S(1)} %shard_map.83), channel_id=1, source_target_pairs={{0,3},{1,2},{2,1},{3,0},{4,7},{5,6},{6,5},{7,4},{8,11},{9,10},{10,... | collective-permute-start | bytes 786440 | tf_op jit(solution)/shard_map/ppermute | solution.py:149
  59.3 6.6 %collective-permute-done.26 = bf16[1024,128]{1,0:T(8,128)(2,1)S(1)} collective-permute-done((bf16[1024,128]{1,0:T(8,128)(2,1)S(1)}, bf16[1024,128]{1,0:T(8,128)(2,1)S(1)}, u32[]{:S(2)}, u32[]{:S(2)}) %collective-permute-start.26) | collective-permute-done | bytes 262176 | tf_op jit(solution)/shard_map/ppermute | solution.py:149
  65.9 0.7 %select_bitcast_fusion = bf16[1,1024,128]{2,1,0:T(8,128)(2,1)} fusion(bf16[1024,128]{1,0:T(8,128)(2,1)S(1)} %collective-permute-done.26, bf16[1024,128]{1,0:T(8,128)(2,1)S(1)} %shard_map.84, pred[]{:T(512)S(6)} %eq.3), kind=kLoop, calls=%fused_computation | loop fusion | flops 131072 | bytes 786433 | tf_op jit(solution)/shard_map/broadcast_in_dim | solution.py:209
  (54 shorter events, 1.7 us)
Async XLA Ops:
  0.0 6.9 %collective-permute-start.1 = (bf16[4,2048,128]{2,1,0:T(8,128)(2,1)}, bf16[4,2048,128]{2,1,0:T(8,128)(2,1)S(1)}, u32[]{:S(2)}, u32[]{:S(2)}) collective-permute-start(bf16[4,2048,128]{2,1,0:T(8,128)(2,1)} %bitcast.13), channel_id=1, source_target_pairs={{0,1},{1,0},{2,3},{3,2},{4,5},{5,4},{6,7},{7,6},{8,9},{9,8},{10,11... | collective-permute-start | bytes 6291464 | tf_op jit(solution)/shard_map/ppermute | solution.py:158
  0.5 17.5 %collective-permute-start = (bf16[4,1024,128]{2,1,0:T(8,128)(2,1)}, bf16[4,1024,128]{2,1,0:T(8,128)(2,1)S(1)}, u32[]{:S(2)}, u32[]{:S(2)}) collective-permute-start(bf16[4,1024,128]{2,1,0:T(8,128)(2,1)} %bitcast.15), channel_id=1, source_target_pairs={{0,1},{1,0},{2,3},{3,2},{4,5},{5,4},{6,7},{7,6},{8,9},{9,8},{10,11... | collective-permute-start | bytes 3145736 | tf_op jit(solution)/shard_map/ppermute | solution.py:158
  1.5 11.4 %collective-permute-start.3 = (bf16[512,128]{1,0:T(8,128)(2,1)S(1)}, bf16[512,128]{1,0:T(8,128)(2,1)S(1)}, u32[]{:S(2)}, u32[]{:S(2)}) collective-permute-start(bf16[512,128]{1,0:T(8,128)(2,1)S(1)} %get-tuple-element.119), channel_id=1, source_target_pairs={{0,8},{1,9},{2,3},{3,2},{4,12},{5,13},{6,7},{7,6},{8,0},{9,1},{10,... | collective-permute-start | bytes 393224 | tf_op jit(solution)/shard_map/ppermute | solution.py:149
  5.6 10.3 %collective-permute-start.10 = (bf16[512,128]{1,0:T(8,128)(2,1)S(1)}, bf16[512,128]{1,0:T(8,128)(2,1)S(1)}, u32[]{:S(2)}, u32[]{:S(2)}) collective-permute-start(bf16[512,128]{1,0:T(8,128)(2,1)S(1)} %get-tuple-element.119), channel_id=1, source_target_pairs={{0,3},{1,2},{2,9},{3,8},{4,7},{5,6},{6,13},{7,12},{8,11},{9,10},{1... | collective-permute-start | bytes 393224 | tf_op jit(solution)/shard_map/ppermute | solution.py:149
  5.6 10.3 %collective-permute-start.8 = (bf16[512,128]{1,0:T(8,128)(2,1)S(1)}, bf16[512,128]{1,0:T(8,128)(2,1)S(1)}, u32[]{:S(2)}, u32[]{:S(2)}) collective-permute-start(bf16[512,128]{1,0:T(8,128)(2,1)S(1)} %get-tuple-element.67.refs_2_), channel_id=1, source_target_pairs={{0,3},{1,2},{2,1},{3,0},{4,7},{5,6},{6,5},{7,4},{8,11},{9,10},{10,... | collective-permute-start | bytes 393224 | tf_op jit(solution)/shard_map/ppermute | solution.py:149
  6.9 13.2 %collective-permute-start.2 = (bf16[512,128]{1,0:T(8,128)(2,1)S(1)}, bf16[512,128]{1,0:T(8,128)(2,1)S(1)}, u32[]{:S(2)}, u32[]{:S(2)}) collective-permute-start(bf16[512,128]{1,0:T(8,128)(2,1)S(1)} %get-tuple-element.67.refs_2_), channel_id=1, source_target_pairs={{0,4},{1,5},{2,3},{3,2},{4,0},{5,1},{6,7},{7,6},{8,12},{9,13},{10,... | collective-permute-start | bytes 393224 | tf_op jit(solution)/shard_map/ppermute | solution.py:149
  11.1 6.8 %copy-start.2 = (s32[1,8,8]{2,1,0:T(8,128)S(1)}, s32[1,8,8]{2,1,0:T(8,128)}, u32[]{:S(2)}) copy-start(s32[1,8,8]{2,1,0:T(8,128)} %param.13) | copy-start | bytes 772
  12.8 6.2 %copy-start.1 = (bf16[1,4,1024,128]{3,2,1,0:T(8,128)(2,1)S(1)}, bf16[1,4,1024,128]{3,2,1,0:T(8,128)(2,1)}, u32[]{:S(2)}) copy-start(bf16[1,4,1024,128]{3,2,1,0:T(8,128)(2,1)} %param.9) | copy-start | bytes 3145732
  12.9 7.2 %collective-permute-start.4 = (bf16[512,128]{1,0:T(8,128)(2,1)S(1)}, bf16[512,128]{1,0:T(8,128)(2,1)S(1)}, u32[]{:S(2)}, u32[]{:S(2)}) collective-permute-start(bf16[512,128]{1,0:T(8,128)(2,1)S(1)} %collective-permute-done.3.refs_4_), channel_id=1, source_target_pairs={{0,4},{1,5},{2,3},{3,2},{4,0},{5,1},{6,7},{7,6},{8,12},{9,13},{10,... | collective-permute-start | bytes 393224 | tf_op jit(solution)/shard_map/ppermute | solution.py:149
  15.9 9.4 %collective-permute-start.11 = (bf16[512,128]{1,0:T(8,128)(2,1)S(1)}, bf16[512,128]{1,0:T(8,128)(2,1)S(1)}, u32[]{:S(2)}, u32[]{:S(2)}) collective-permute-start(bf16[512,128]{1,0:T(8,128)(2,1)S(1)} %collective-permute-done.10.refs_4_), channel_id=1, source_target_pairs={{0,4},{1,5},{2,3},{3,2},{4,0},{5,1},{6,7},{7,6},{8,12},{9,13},{10,... | collective-permute-start | bytes 393224 | tf_op jit(solution)/shard_map/ppermute | solution.py:149
  15.9 9.7 %collective-permute-start.9 = (bf16[512,128]{1,0:T(8,128)(2,1)S(1)}, bf16[512,128]{1,0:T(8,128)(2,1)S(1)}, u32[]{:S(2)}, u32[]{:S(2)}) collective-permute-start(bf16[512,128]{1,0:T(8,128)(2,1)S(1)} %collective-permute-done.8.refs_2_), channel_id=1, source_target_pairs={{0,4},{1,5},{2,3},{3,2},{4,0},{5,1},{6,7},{7,6},{8,12},{9,13},{10,... | collective-permute-start | bytes 393224 | tf_op jit(solution)/shard_map/ppermute | solution.py:149
  20.9 8.8 %collective-permute-start.5 = (bf16[128,256]{1,0:T(8,128)(2,1)S(1)}, bf16[128,256]{1,0:T(8,128)(2,1)S(1)}, u32[]{:S(2)}, u32[]{:S(2)}) collective-permute-start(bf16[128,256]{1,0:T(8,128)(2,1)S(1)} %get-tuple-element.72), channel_id=1, source_target_pairs={{0,4},{1,5},{2,3},{3,2},{4,0},{5,1},{6,7},{7,6},{8,12},{9,13},{10,... | collective-permute-start | bytes 196616 | tf_op jit(solution)/shard_map/ppermute | solution.py:149
  21.0 9.8 %collective-permute-start.6 = (bf16[128,256]{1,0:T(8,128)(2,1)S(1)}, bf16[128,256]{1,0:T(8,128)(2,1)S(1)}, u32[]{:S(2)}, u32[]{:S(2)}) collective-permute-start(bf16[128,256]{1,0:T(8,128)(2,1)S(1)} %get-tuple-element.73), channel_id=1, source_target_pairs={{0,8},{1,9},{2,3},{3,2},{4,12},{5,13},{6,7},{7,6},{8,0},{9,1},{10,... | collective-permute-start | bytes 196616 | tf_op jit(solution)/shard_map/ppermute | solution.py:149
  23.5 7.3 %collective-permute-start.7 = (bf16[128,256]{1,0:T(8,128)(2,1)S(1)}, bf16[128,256]{1,0:T(8,128)(2,1)S(1)}, u32[]{:S(2)}, u32[]{:S(2)}) collective-permute-start(bf16[128,256]{1,0:T(8,128)(2,1)S(1)} %get-tuple-element.74), channel_id=1, source_target_pairs={{0,12},{1,13},{2,3},{3,2},{4,8},{5,9},{6,7},{7,6},{8,4},{9,5},{10,... | collective-permute-start | bytes 196616 | tf_op jit(solution)/shard_map/ppermute | solution.py:149
  26.3 8.6 %collective-permute-start.16 = (bf16[128,256]{1,0:T(8,128)(2,1)S(1)}, bf16[128,256]{1,0:T(8,128)(2,1)S(1)}, u32[]{:S(2)}, u32[]{:S(2)}) collective-permute-start(bf16[128,256]{1,0:T(8,128)(2,1)S(1)} %get-tuple-element.80), channel_id=1, source_target_pairs={{0,4},{1,5},{2,3},{3,2},{4,0},{5,1},{6,7},{7,6},{8,12},{9,13},{10,... | collective-permute-start | bytes 196616 | tf_op jit(solution)/shard_map/ppermute | solution.py:149
  26.4 11.2 %collective-permute-start.17 = (bf16[128,256]{1,0:T(8,128)(2,1)S(1)}, bf16[128,256]{1,0:T(8,128)(2,1)S(1)}, u32[]{:S(2)}, u32[]{:S(2)}) collective-permute-start(bf16[128,256]{1,0:T(8,128)(2,1)S(1)} %get-tuple-element.81), channel_id=1, source_target_pairs={{0,8},{1,9},{2,3},{3,2},{4,12},{5,13},{6,7},{7,6},{8,0},{9,1},{10,... | collective-permute-start | bytes 196616 | tf_op jit(solution)/shard_map/ppermute | solution.py:149
  29.6 7.9 %collective-permute-start.18 = (bf16[128,256]{1,0:T(8,128)(2,1)S(1)}, bf16[128,256]{1,0:T(8,128)(2,1)S(1)}, u32[]{:S(2)}, u32[]{:S(2)}) collective-permute-start(bf16[128,256]{1,0:T(8,128)(2,1)S(1)} %get-tuple-element.82), channel_id=1, source_target_pairs={{0,12},{1,13},{2,3},{3,2},{4,8},{5,9},{6,7},{7,6},{8,4},{9,5},{10,... | collective-permute-start | bytes 196616 | tf_op jit(solution)/shard_map/ppermute | solution.py:149
  31.3 9.6 %collective-permute-start.12 = (bf16[128,512]{1,0:T(8,128)(2,1)S(1)}, bf16[128,512]{1,0:T(8,128)(2,1)S(1)}, u32[]{:S(2)}, u32[]{:S(2)}) collective-permute-start(bf16[128,512]{1,0:T(8,128)(2,1)S(1)} %get-tuple-element.87), channel_id=1, source_target_pairs={{0,3},{1,2},{2,1},{3,0},{4,7},{5,6},{6,5},{7,4},{8,11},{9,10},{10,... | collective-permute-start | bytes 393224 | tf_op jit(solution)/shard_map/ppermute | solution.py:149
  31.4 9.5 %collective-permute-start.14 = (bf16[128,512]{1,0:T(8,128)(2,1)S(1)}, bf16[128,512]{1,0:T(8,128)(2,1)S(1)}, u32[]{:S(2)}, u32[]{:S(2)}) collective-permute-start(bf16[128,512]{1,0:T(8,128)(2,1)S(1)} %get-tuple-element.88), channel_id=1, source_target_pairs={{0,11},{1,10},{2,1},{3,0},{4,15},{5,14},{6,5},{7,4},{8,3},{9,2},{1... | collective-permute-start | bytes 393224 | tf_op jit(solution)/shard_map/ppermute | solution.py:149
  38.0 5.1 %collective-permute-start.22 = (bf16[128,512]{1,0:T(8,128)(2,1)S(1)}, bf16[128,512]{1,0:T(8,128)(2,1)S(1)}, u32[]{:S(2)}, u32[]{:S(2)}) collective-permute-start(bf16[128,512]{1,0:T(8,128)(2,1)S(1)} %get-tuple-element.93), channel_id=1, source_target_pairs={{0,3},{1,2},{2,1},{3,0},{4,7},{5,6},{6,5},{7,4},{8,11},{9,10},{10,... | collective-permute-start | bytes 393224 | tf_op jit(solution)/shard_map/ppermute | solution.py:149
  38.1 5.8 %collective-permute-start.24 = (bf16[128,512]{1,0:T(8,128)(2,1)S(1)}, bf16[128,512]{1,0:T(8,128)(2,1)S(1)}, u32[]{:S(2)}, u32[]{:S(2)}) collective-permute-start(bf16[128,512]{1,0:T(8,128)(2,1)S(1)} %get-tuple-element.94), channel_id=1, source_target_pairs={{0,11},{1,10},{2,1},{3,0},{4,15},{5,14},{6,5},{7,4},{8,3},{9,2},{1... | collective-permute-start | bytes 393224 | tf_op jit(solution)/shard_map/ppermute | solution.py:149
  40.8 3.1 %collective-permute-start.13 = (bf16[128,512]{1,0:T(8,128)(2,1)S(1)}, bf16[128,512]{1,0:T(8,128)(2,1)S(1)}, u32[]{:S(2)}, u32[]{:S(2)}) collective-permute-start(bf16[128,512]{1,0:T(8,128)(2,1)S(1)} %collective-permute-done.12.refs_2_), channel_id=1, source_target_pairs={{0,1},{1,0},{2,6},{3,7},{4,5},{5,4},{6,2},{7,3},{8,9},{9,8},{10,14... | collective-permute-start | bytes 393224 | tf_op jit(solution)/shard_map/ppermute | solution.py:149
  40.8 3.1 %collective-permute-start.15 = (bf16[128,512]{1,0:T(8,128)(2,1)S(1)}, bf16[128,512]{1,0:T(8,128)(2,1)S(1)}, u32[]{:S(2)}, u32[]{:S(2)}) collective-permute-start(bf16[128,512]{1,0:T(8,128)(2,1)S(1)} %collective-permute-done.14.refs_4_), channel_id=1, source_target_pairs={{0,1},{1,0},{2,6},{3,7},{4,5},{5,4},{6,2},{7,3},{8,9},{9,8},{10,14... | collective-permute-start | bytes 393224 | tf_op jit(solution)/shard_map/ppermute | solution.py:149
  43.1 1.8 %collective-permute-start.23 = (bf16[128,512]{1,0:T(8,128)(2,1)S(1)}, bf16[128,512]{1,0:T(8,128)(2,1)S(1)}, u32[]{:S(2)}, u32[]{:S(2)}) collective-permute-start(bf16[128,512]{1,0:T(8,128)(2,1)S(1)} %collective-permute-done.22.refs_2_), channel_id=1, source_target_pairs={{0,1},{1,0},{2,6},{3,7},{4,5},{5,4},{6,2},{7,3},{8,9},{9,8},{10,14... | collective-permute-start | bytes 393224 | tf_op jit(solution)/shard_map/ppermute | solution.py:149
  43.9 1.3 %collective-permute-start.25 = (bf16[128,512]{1,0:T(8,128)(2,1)S(1)}, bf16[128,512]{1,0:T(8,128)(2,1)S(1)}, u32[]{:S(2)}, u32[]{:S(2)}) collective-permute-start(bf16[128,512]{1,0:T(8,128)(2,1)S(1)} %collective-permute-done.24.refs_4_), channel_id=1, source_target_pairs={{0,1},{1,0},{2,6},{3,7},{4,5},{5,4},{6,2},{7,3},{8,9},{9,8},{10,14... | collective-permute-start | bytes 393224 | tf_op jit(solution)/shard_map/ppermute | solution.py:149
  43.9 1.8 %collective-permute-start.19 = (bf16[128,256]{1,0:T(8,128)(2,1)S(1)}, bf16[128,256]{1,0:T(8,128)(2,1)S(1)}, u32[]{:S(2)}, u32[]{:S(2)}) collective-permute-start(bf16[128,256]{1,0:T(8,128)(2,1)S(1)} %get-tuple-element.100), channel_id=1, source_target_pairs={{0,1},{1,0},{2,6},{3,7},{4,5},{5,4},{6,2},{7,3},{8,9},{9,8},{10,14... | collective-permute-start | bytes 196616 | tf_op jit(solution)/shard_map/ppermute | solution.py:149
  44.4 1.5 %collective-permute-start.20 = (bf16[128,256]{1,0:T(8,128)(2,1)S(1)}, bf16[128,256]{1,0:T(8,128)(2,1)S(1)}, u32[]{:S(2)}, u32[]{:S(2)}) collective-permute-start(bf16[128,256]{1,0:T(8,128)(2,1)S(1)} %get-tuple-element.101), channel_id=1, source_target_pairs={{0,1},{1,0},{2,10},{3,11},{4,5},{5,4},{6,14},{7,15},{8,9},{9,8},{1... | collective-permute-start | bytes 196616 | tf_op jit(solution)/shard_map/ppermute | solution.py:149
  44.5 1.4 %collective-permute-start.21 = (bf16[128,256]{1,0:T(8,128)(2,1)S(1)}, bf16[128,256]{1,0:T(8,128)(2,1)S(1)}, u32[]{:S(2)}, u32[]{:S(2)}) collective-permute-start(bf16[128,256]{1,0:T(8,128)(2,1)S(1)} %get-tuple-element.102), channel_id=1, source_target_pairs={{0,1},{1,0},{2,14},{3,15},{4,5},{5,4},{6,10},{7,11},{8,9},{9,8},{1... | collective-permute-start | bytes 196616 | tf_op jit(solution)/shard_map/ppermute | solution.py:149
  45.2 14.1 %collective-permute-start.27 = (bf16[128,256]{1,0:T(8,128)(2,1)S(1)}, bf16[128,256]{1,0:T(8,128)(2,1)S(1)}, u32[]{:S(2)}, u32[]{:S(2)}) collective-permute-start(bf16[128,256]{1,0:T(8,128)(2,1)S(1)} %get-tuple-element.108), channel_id=1, source_target_pairs={{0,1},{1,0},{2,6},{3,7},{4,5},{5,4},{6,2},{7,3},{8,9},{9,8},{10,14... | collective-permute-start | bytes 196616 | tf_op jit(solution)/shard_map/ppermute | solution.py:149
  45.4 13.9 %collective-permute-start.28 = (bf16[128,256]{1,0:T(8,128)(2,1)S(1)}, bf16[128,256]{1,0:T(8,128)(2,1)S(1)}, u32[]{:S(2)}, u32[]{:S(2)}) collective-permute-start(bf16[128,256]{1,0:T(8,128)(2,1)S(1)} %get-tuple-element.109), channel_id=1, source_target_pairs={{0,1},{1,0},{2,10},{3,11},{4,5},{5,4},{6,14},{7,15},{8,9},{9,8},{1... | collective-permute-start | bytes 196616 | tf_op jit(solution)/shard_map/ppermute | solution.py:149
  45.8 13.6 %collective-permute-start.29 = (bf16[128,256]{1,0:T(8,128)(2,1)S(1)}, bf16[128,256]{1,0:T(8,128)(2,1)S(1)}, u32[]{:S(2)}, u32[]{:S(2)}) collective-permute-start(bf16[128,256]{1,0:T(8,128)(2,1)S(1)} %get-tuple-element.110), channel_id=1, source_target_pairs={{0,1},{1,0},{2,14},{3,15},{4,5},{5,4},{6,10},{7,11},{8,9},{9,8},{1... | collective-permute-start | bytes 196616 | tf_op jit(solution)/shard_map/ppermute | solution.py:149
  45.9 20.0 %collective-permute-start.26 = (bf16[1024,128]{1,0:T(8,128)(2,1)S(1)}, bf16[1024,128]{1,0:T(8,128)(2,1)S(1)}, u32[]{:S(2)}, u32[]{:S(2)}) collective-permute-start(bf16[1024,128]{1,0:T(8,128)(2,1)S(1)} %shard_map.83), channel_id=1, source_target_pairs={{0,3},{1,2},{2,1},{3,0},{4,7},{5,6},{6,5},{7,4},{8,11},{9,10},{10,... | collective-permute-start | bytes 786440 | tf_op jit(solution)/shard_map/ppermute | solution.py:149
  (4 other events, 10.2 us)

commit v5 on v4

--- a/solution.py
+++ b/solution.py
@@ -14,22 +14,22 @@
 
 def place_tiles(links, source, ordered, first):
     owner_count = ordered.shape[0]
+    owner_bits = owner_count.bit_length() - 1
     me = lax.axis_index("owners")
     half, _, size = source.shape
     slots = links.shape[1]
-    width = 2 * size
+    two_parts = slots > 2 * owner_count
+    flip = me * 4 + (me & 1) * 2 if two_parts else me * 2
     for block in range(half):
         row = first + block
-        distance = (row // 2) ^ me
+        distance = (row >> 1) ^ me
         for slot in range(slots):
             place = links[row, slot]
-            sender = ((place // 2) & (owner_count - 1)) ^ me
-            if slots > 2 * owner_count:
-                part = (place // (2 * owner_count)) ^ (me & 1)
-                key = 2 * sender + part
+            if two_parts:
+                key = ((place & (2 * owner_count - 2)) << 1) | ((place >> (owner_bits + 1)) << 1) | (place & 1)
             else:
-                key = sender
-            low = pl.multiple_of(key * width + (place & 1) * size, size)
+                key = place
+            low = pl.multiple_of((key ^ flip) * size, size)
             ordered[distance, pl.ds(low, size), pl.ds(block % 2 * size, size)] = source[
                 block, pl.ds(slot * size, size), :
             ]
@@ -170,12 +170,13 @@
     first_own, second_own = weight_first[0], weight_second[0]
     first_other = other_core(first_own)
     far_two, near_one = moved(far, within(2, 0)), moved(near, within(1, 0))
-    crossed = moved(far, across(2, 1)), moved(near, across(0, 1))
+    crossed_far = moved(far, across(2, 1))
+    crossed_near = [moved(near, across(distance, 1)) for distance in (0, 1)]
     first = order_weights(links_first[0], first_own, first_other, bias_first[0].reshape(-1, size))
     second_other = other_core(second_own)
     second = order_weights(links_second[0], second_own, second_other, bias_second[0].reshape(-1, size))
     start = [near, near_one, far_two, moved(after(far_two, first[0]), within(1, 0))]
-    later = gathered(crossed[1], crossed[0], 0)
+    later = [*crossed_near, crossed_far, moved(after(crossed_far, second[0]), within(1, 0))]
 
     raw_tiles = [(buffer, column * piece, 2 * buffer + column) for buffer in range(4) for column in range(2)]
     order = [(0, 0), (0, 1), (1, 1), (1, 0), (2, 0), (2, 1), (3, 1), (3, 0)]

time: 67.6 us -> 66 us (0.976); the launches traced: 66.7 us -> 65.8 us
  starting transfers between devices: 40.9 us -> 46.4 us
  waiting for transfers between devices: 15.2 us -> 9.76 us
  Pallas kernels: 7.96 us -> 6.72 us
    ppermute x28, starting transfers between devices: 40.4 us -> 45.9 us  [moved(): return lax.ppermute(value, ('owners', 'section', 'rep'), pairs)]
    ppermute x28, waiting for transfers between devices: 15.2 us -> 9.75 us  [moved(): return lax.ppermute(value, ('owners', 'section', 'rep'), pairs)]
  transfers between devices with their start and end apart: 30 -> 30, of which waited for: 7 -> 5; matrix products, arithmetic and copies ran while one was open for 1% -> 1% of each run, Pallas kernels for 12% -> 10%
where the time goes in v5:
time: 66 us; the launch traced here: 65.8 us
  starting transfers between devices  46.4 us (70%)
  waiting for transfers between devices  9.76 us (15%)
  Pallas kernels  6.72 us (10%)
  local copies, waits for them, and re-layouts  2.03 us (3%)
  other arithmetic  0.73 us (1%)
    ppermute x28, starting transfers between devices, moved(): return lax.ppermute(value, ('owners', 'section', 'rep'), pairs)  45.9 us
    ppermute x28, waiting for transfers between devices, moved(): return lax.ppermute(value, ('owners', 'section', 'rep'), pairs)  9.75 us
    pallas_call x8, Pallas kernels, layer(): pl.pallas_call(functools.partial(layer_kernel, tile_list, out_groups, raw...  2.47 us
    pallas_call x2, Pallas kernels, order_weights(): pl.pallas_call(order_own_kernel, out_shape=[ordered, jax.ShapeDtypeStruct...  2.13 us
    pallas_call x2, Pallas kernels, order_weights(): pl.pallas_call(order_other_kernel, out_shape=ordered, in_specs=[smem, vme...  2.12 us
  transfers between devices with their start and end apart: 30, of which 5 were waited for; matrix products, arithmetic and copies ran while one was open for 1% of the time, Pallas kernels for 10%

profile of v5, /device:TPU:0, one launch (start us, length us, event | category | flops | bytes accessed | tf_op | source)
XLA Modules:
  0.0 65.8 jit_solution(3905132593245362202)
XLA Ops:
  0.0 0.5 collective-permute-start.1
  0.5 1.0 %dynamic-slice_bitcast_fusion = (bf16[512,128]{1,0:T(8,128)(2,1)S(1)}, bf16[512,128]{1,0:T(8,128)(2,1)S(1)}) fusion(bf16[2,512,128]{2,1,0:T(8,128)(2,1)} %bitcast.23, s32[]{:T(128)S(6)} %select_n.24, s32[]{:T(128)S(6)} %select_n.23), kind=kLoop, calls=%fused_computation.1 | loop fusion | bytes 524296 | tf_op jit(solution)/shard_map/jit(dynamic_index_in_dim)/squeeze | solution.py:162
  1.5 4.1 %collective-permute-start.3 = (bf16[512,128]{1,0:T(8,128)(2,1)S(1)}, bf16[512,128]{1,0:T(8,128)(2,1)S(1)}, u32[]{:S(2)}, u32[]{:S(2)}) collective-permute-start(bf16[512,128]{1,0:T(8,128)(2,1)S(1)} %get-tuple-element.121), channel_id=1, source_target_pairs={{0,8},{1,9},{2,3},{3,2},{4,12},{5,13},{6,7},{7,6},{8,0},{9,1},{10,... | collective-permute-start | bytes 393224 | tf_op jit(solution)/shard_map/ppermute | solution.py:149
  5.6 1.6 %collective-permute-start.2 = (bf16[512,128]{1,0:T(8,128)(2,1)S(1)}, bf16[512,128]{1,0:T(8,128)(2,1)S(1)}, u32[]{:S(2)}, u32[]{:S(2)}) collective-permute-start(bf16[512,128]{1,0:T(8,128)(2,1)S(1)} %get-tuple-element.68.refs_2_), channel_id=1, source_target_pairs={{0,4},{1,5},{2,3},{3,2},{4,0},{5,1},{6,7},{7,6},{8,12},{9,13},{10,... | collective-permute-start | bytes 393224 | tf_op jit(solution)/shard_map/ppermute | solution.py:149
  7.2 0.7 %copy-done.3 = s32[1,8,16]{2,1,0:T(8,128)S(1)} copy-done((s32[1,8,16]{2,1,0:T(8,128)S(1)}, s32[1,8,16]{2,1,0:T(8,128)}, u32[]{:S(2)}) %copy-start.3) | copy-done | bytes 536
  7.9 1.2 %shard_map.75.half_ordered = bf16[4,2048,256]{2,1,0:T(8,128)(2,1)S(1)} custom-call(s32[8,16]{1,0:T(8,128)S(1)} %bitcast.19, bf16[4,2048,128]{2,1,0:T(8,128)(2,1)S(1)} %collective-permute-done.1.other_tiles), custom_call_target="tpu_custom_call" | custom-call | flops 1 | bytes 1 | tf_op jit(solution)/shard_map/pallas_call | solution.py:60
  9.5 1.2 %shard_map.76 = (bf16[4,2048,256]{2,1,0:T(8,128)(2,1)S(1)}, f32[4,256]{1,0:T(4,128)S(1)}) custom-call(s32[8,16]{1,0:T(8,128)S(1)} %bitcast.20, bf16[4,2048,128]{2,1,0:T(8,128)(2,1)S(1)} %bitcast.14, f32[8,128]{1,0:T(8,128)S(1)} %bitcast.21, bf16[4,2048,256]{2,1,0:T(8,128)(2,1)S(1)} %shard_map.75.half_ordered), custom_call_target="tpu_custom_call", output_to_operand_aliasing={{0}: (3, {})} | custom-call | flops 1 | bytes 1 | tf_op jit(solution)/shard_map/pallas_call | solution.py:63
  10.8 1.4 %collective-permute-done.3.refs_4_ = bf16[512,128]{1,0:T(8,128)(2,1)S(1)} collective-permute-done((bf16[512,128]{1,0:T(8,128)(2,1)S(1)}, bf16[512,128]{1,0:T(8,128)(2,1)S(1)}, u32[]{:S(2)}, u32[]{:S(2)}) %collective-permute-start.3) | collective-permute-done | bytes 131104 | tf_op jit(solution)/shard_map/ppermute | solution.py:149
  12.2 0.7 collective-permute-start.4
  12.8 1.7 %collective-permute-start.9 = (bf16[512,128]{1,0:T(8,128)(2,1)S(1)}, bf16[512,128]{1,0:T(8,128)(2,1)S(1)}, u32[]{:S(2)}, u32[]{:S(2)}) collective-permute-start(bf16[512,128]{1,0:T(8,128)(2,1)S(1)} %get-tuple-element.68.refs_2_), channel_id=1, source_target_pairs={{0,3},{1,2},{2,5},{3,4},{4,7},{5,6},{6,1},{7,0},{8,11},{9,10},{10,... | collective-permute-start | bytes 393224 | tf_op jit(solution)/shard_map/ppermute | solution.py:149
  14.6 0.9 %shard_map.73.half_ordered = bf16[4,1024,256]{2,1,0:T(8,128)(2,1)S(1)} custom-call(s32[8,8]{1,0:T(8,128)S(1)} %bitcast.17, bf16[4,1024,128]{2,1,0:T(8,128)(2,1)S(1)} %collective-permute-done.other_tiles), custom_call_target="tpu_custom_call" | custom-call | flops 1 | bytes 1 | tf_op jit(solution)/shard_map/pallas_call | solution.py:60
  15.5 0.9 %shard_map.74 = (bf16[4,1024,256]{2,1,0:T(8,128)(2,1)S(1)}, f32[4,256]{1,0:T(4,128)S(1)}) custom-call(s32[8,8]{1,0:T(8,128)S(1)} %bitcast.18, bf16[4,1024,128]{2,1,0:T(8,128)(2,1)S(1)} %bitcast.16, f32[8,128]{1,0:T(8,128)S(1)} %bitcast.22, bf16[4,1024,256]{2,1,0:T(8,128)(2,1)S(1)} %shard_map.73.half_ordered), custom_call_target="tpu_custom_call", output_to_operand_aliasing={{0}: (3, {})} | custom-call | flops 1 | bytes 1 | tf_op jit(solution)/shard_map/pallas_call | solution.py:63
  16.4 1.4 %collective-permute-start.11 = (bf16[512,128]{1,0:T(8,128)(2,1)S(1)}, bf16[512,128]{1,0:T(8,128)(2,1)S(1)}, u32[]{:S(2)}, u32[]{:S(2)}) collective-permute-start(bf16[512,128]{1,0:T(8,128)(2,1)S(1)} %collective-permute-done.10.refs_4_), channel_id=1, source_target_pairs={{0,4},{1,5},{2,3},{3,2},{4,0},{5,1},{6,7},{7,6},{8,12},{9,13},{10,... | collective-permute-start | bytes 393224 | tf_op jit(solution)/shard_map/ppermute | solution.py:149
  17.8 0.8 %shard_map.77 = (bf16[128,256]{1,0:T(8,128)(2,1)S(1)}, bf16[128,256]{1,0:T(8,128)(2,1)S(1)}, bf16[128,256]{1,0:T(8,128)(2,1)S(1)}, bf16[128,256]{1,0:T(8,128)(2,1)S(1)}) custom-call(bf16[4,2048,256]{2,1,0:T(8,128)(2,1)S(1)} %get-tuple-element.65.refs_0_, f32[4,256]{1,0:T(4,128)S(1)} %get-tuple-element.66.refs_1_, ...), custom_call_target="tpu_custom_call" | custom-call | flops 1 | bytes 1 | tf_op jit(solution)/shard_map/pallas_call | solution.py:124
  18.6 0.7 %collective-permute-start.5 = (bf16[128,256]{1,0:T(8,128)(2,1)S(1)}, bf16[128,256]{1,0:T(8,128)(2,1)S(1)}, u32[]{:S(2)}, u32[]{:S(2)}) collective-permute-start(bf16[128,256]{1,0:T(8,128)(2,1)S(1)} %get-tuple-element.73), channel_id=1, source_target_pairs={{0,4},{1,5},{2,3},{3,2},{4,0},{5,1},{6,7},{7,6},{8,12},{9,13},{10,... | collective-permute-start | bytes 196616 | tf_op jit(solution)/shard_map/ppermute | solution.py:149
  19.3 3.4 %collective-permute-start.6 = (bf16[128,256]{1,0:T(8,128)(2,1)S(1)}, bf16[128,256]{1,0:T(8,128)(2,1)S(1)}, u32[]{:S(2)}, u32[]{:S(2)}) collective-permute-start(bf16[128,256]{1,0:T(8,128)(2,1)S(1)} %get-tuple-element.74), channel_id=1, source_target_pairs={{0,8},{1,9},{2,3},{3,2},{4,12},{5,13},{6,7},{7,6},{8,0},{9,1},{10,... | collective-permute-start | bytes 196616 | tf_op jit(solution)/shard_map/ppermute | solution.py:149
  22.8 1.4 %collective-permute-start.7 = (bf16[128,256]{1,0:T(8,128)(2,1)S(1)}, bf16[128,256]{1,0:T(8,128)(2,1)S(1)}, u32[]{:S(2)}, u32[]{:S(2)}) collective-permute-start(bf16[128,256]{1,0:T(8,128)(2,1)S(1)} %get-tuple-element.75), channel_id=1, source_target_pairs={{0,12},{1,13},{2,3},{3,2},{4,8},{5,9},{6,7},{7,6},{8,4},{9,5},{10,... | collective-permute-start | bytes 196616 | tf_op jit(solution)/shard_map/ppermute | solution.py:149
  24.2 0.8 %shard_map.78 = (bf16[128,256]{1,0:T(8,128)(2,1)S(1)}, bf16[128,256]{1,0:T(8,128)(2,1)S(1)}, bf16[128,256]{1,0:T(8,128)(2,1)S(1)}, bf16[128,256]{1,0:T(8,128)(2,1)S(1)}) custom-call(bf16[4,2048,256]{2,1,0:T(8,128)(2,1)S(1)} %get-tuple-element.65.refs_0_, f32[4,256]{1,0:T(4,128)S(1)} %get-tuple-element.66.refs_1_, ...), custom_call_target="tpu_custom_call" | custom-call | flops 1 | bytes 1 | tf_op jit(solution)/shard_map/pallas_call | solution.py:124
  25.0 1.2 %collective-permute-start.16 = (bf16[128,256]{1,0:T(8,128)(2,1)S(1)}, bf16[128,256]{1,0:T(8,128)(2,1)S(1)}, u32[]{:S(2)}, u32[]{:S(2)}) collective-permute-start(bf16[128,256]{1,0:T(8,128)(2,1)S(1)} %get-tuple-element.82), channel_id=1, source_target_pairs={{0,4},{1,5},{2,3},{3,2},{4,0},{5,1},{6,7},{7,6},{8,12},{9,13},{10,... | collective-permute-start | bytes 196616 | tf_op jit(solution)/shard_map/ppermute | solution.py:149
  26.1 1.8 %collective-permute-start.17 = (bf16[128,256]{1,0:T(8,128)(2,1)S(1)}, bf16[128,256]{1,0:T(8,128)(2,1)S(1)}, u32[]{:S(2)}, u32[]{:S(2)}) collective-permute-start(bf16[128,256]{1,0:T(8,128)(2,1)S(1)} %get-tuple-element.83), channel_id=1, source_target_pairs={{0,8},{1,9},{2,3},{3,2},{4,12},{5,13},{6,7},{7,6},{8,0},{9,1},{10,... | collective-permute-start | bytes 196616 | tf_op jit(solution)/shard_map/ppermute | solution.py:149
  28.0 1.4 %collective-permute-start.18 = (bf16[128,256]{1,0:T(8,128)(2,1)S(1)}, bf16[128,256]{1,0:T(8,128)(2,1)S(1)}, u32[]{:S(2)}, u32[]{:S(2)}) collective-permute-start(bf16[128,256]{1,0:T(8,128)(2,1)S(1)} %get-tuple-element.84), channel_id=1, source_target_pairs={{0,12},{1,13},{2,3},{3,2},{4,8},{5,9},{6,7},{7,6},{8,4},{9,5},{10,... | collective-permute-start | bytes 196616 | tf_op jit(solution)/shard_map/ppermute | solution.py:149
  29.4 0.5 shard_map.79
  30.0 3.3 %collective-permute-start.14 = (bf16[128,512]{1,0:T(8,128)(2,1)S(1)}, bf16[128,512]{1,0:T(8,128)(2,1)S(1)}, u32[]{:S(2)}, u32[]{:S(2)}) collective-permute-start(bf16[128,512]{1,0:T(8,128)(2,1)S(1)} %get-tuple-element.90), channel_id=1, source_target_pairs={{0,11},{1,10},{2,1},{3,0},{4,15},{5,14},{6,5},{7,4},{8,3},{9,2},{1... | collective-permute-start | bytes 393224 | tf_op jit(solution)/shard_map/ppermute | solution.py:149
  33.2 1.0 %collective-permute-done.17.refs_4_ = bf16[128,256]{1,0:T(8,128)(2,1)S(1)} collective-permute-done((bf16[128,256]{1,0:T(8,128)(2,1)S(1)}, bf16[128,256]{1,0:T(8,128)(2,1)S(1)}, u32[]{:S(2)}, u32[]{:S(2)}) %collective-permute-start.17) | collective-permute-done | bytes 65568 | tf_op jit(solution)/shard_map/ppermute | solution.py:149
  34.2 0.5 shard_map.80
  34.8 6.9 %collective-permute-start.24 = (bf16[128,512]{1,0:T(8,128)(2,1)S(1)}, bf16[128,512]{1,0:T(8,128)(2,1)S(1)}, u32[]{:S(2)}, u32[]{:S(2)}) collective-permute-start(bf16[128,512]{1,0:T(8,128)(2,1)S(1)} %get-tuple-element.96), channel_id=1, source_target_pairs={{0,11},{1,10},{2,1},{3,0},{4,15},{5,14},{6,5},{7,4},{8,3},{9,2},{1... | collective-permute-start | bytes 393224 | tf_op jit(solution)/shard_map/ppermute | solution.py:149
  41.7 0.5 collective-permute-start.15
  42.3 1.9 %collective-permute-done.24.refs_4_ = bf16[128,512]{1,0:T(8,128)(2,1)S(1)} collective-permute-done((bf16[128,512]{1,0:T(8,128)(2,1)S(1)}, bf16[128,512]{1,0:T(8,128)(2,1)S(1)}, u32[]{:S(2)}, u32[]{:S(2)}) %collective-permute-start.24) | collective-permute-done | bytes 131104 | tf_op jit(solution)/shard_map/ppermute | solution.py:149
  44.2 0.5 collective-permute-start.19
  46.2 13.8 %collective-permute-start.26 = (bf16[1024,128]{1,0:T(8,128)(2,1)S(1)}, bf16[1024,128]{1,0:T(8,128)(2,1)S(1)}, u32[]{:S(2)}, u32[]{:S(2)}) collective-permute-start(bf16[1024,128]{1,0:T(8,128)(2,1)S(1)} %shard_map.83), channel_id=1, source_target_pairs={{0,3},{1,2},{2,1},{3,0},{4,7},{5,6},{6,5},{7,4},{8,11},{9,10},{10,... | collective-permute-start | bytes 786440 | tf_op jit(solution)/shard_map/ppermute | solution.py:149
  60.1 5.0 %collective-permute-done.26 = bf16[1024,128]{1,0:T(8,128)(2,1)S(1)} collective-permute-done((bf16[1024,128]{1,0:T(8,128)(2,1)S(1)}, bf16[1024,128]{1,0:T(8,128)(2,1)S(1)}, u32[]{:S(2)}, u32[]{:S(2)}) %collective-permute-start.26) | collective-permute-done | bytes 262176 | tf_op jit(solution)/shard_map/ppermute | solution.py:149
  65.1 0.7 %select_bitcast_fusion = bf16[1,1024,128]{2,1,0:T(8,128)(2,1)} fusion(bf16[1024,128]{1,0:T(8,128)(2,1)S(1)} %collective-permute-done.26, bf16[1024,128]{1,0:T(8,128)(2,1)S(1)} %shard_map.84, pred[]{:T(512)S(6)} %eq.3), kind=kLoop, calls=%fused_computation | loop fusion | flops 131072 | bytes 786433 | tf_op jit(solution)/shard_map/broadcast_in_dim | solution.py:210
  (54 shorter events, 2.2 us)
Async XLA Ops:
  0.0 7.2 %collective-permute-start.1 = (bf16[4,2048,128]{2,1,0:T(8,128)(2,1)}, bf16[4,2048,128]{2,1,0:T(8,128)(2,1)S(1)}, u32[]{:S(2)}, u32[]{:S(2)}) collective-permute-start(bf16[4,2048,128]{2,1,0:T(8,128)(2,1)} %bitcast.13), channel_id=1, source_target_pairs={{0,1},{1,0},{2,3},{3,2},{4,5},{5,4},{6,7},{7,6},{8,9},{9,8},{10,11... | collective-permute-start | bytes 6291464 | tf_op jit(solution)/shard_map/ppermute | solution.py:158
  0.5 12.4 %collective-permute-start = (bf16[4,1024,128]{2,1,0:T(8,128)(2,1)}, bf16[4,1024,128]{2,1,0:T(8,128)(2,1)S(1)}, u32[]{:S(2)}, u32[]{:S(2)}) collective-permute-start(bf16[4,1024,128]{2,1,0:T(8,128)(2,1)} %bitcast.15), channel_id=1, source_target_pairs={{0,1},{1,0},{2,3},{3,2},{4,5},{5,4},{6,7},{7,6},{8,9},{9,8},{10,11... | collective-permute-start | bytes 3145736 | tf_op jit(solution)/shard_map/ppermute | solution.py:158
  1.5 10.7 %collective-permute-start.3 = (bf16[512,128]{1,0:T(8,128)(2,1)S(1)}, bf16[512,128]{1,0:T(8,128)(2,1)S(1)}, u32[]{:S(2)}, u32[]{:S(2)}) collective-permute-start(bf16[512,128]{1,0:T(8,128)(2,1)S(1)} %get-tuple-element.121), channel_id=1, source_target_pairs={{0,8},{1,9},{2,3},{3,2},{4,12},{5,13},{6,7},{7,6},{8,0},{9,1},{10,... | collective-permute-start | bytes 393224 | tf_op jit(solution)/shard_map/ppermute | solution.py:149
  5.6 10.8 %collective-permute-start.10 = (bf16[512,128]{1,0:T(8,128)(2,1)S(1)}, bf16[512,128]{1,0:T(8,128)(2,1)S(1)}, u32[]{:S(2)}, u32[]{:S(2)}) collective-permute-start(bf16[512,128]{1,0:T(8,128)(2,1)S(1)} %get-tuple-element.121), channel_id=1, source_target_pairs={{0,3},{1,2},{2,9},{3,8},{4,7},{5,6},{6,13},{7,12},{8,11},{9,10},{1... | collective-permute-start | bytes 393224 | tf_op jit(solution)/shard_map/ppermute | solution.py:149
  5.6 12.2 %collective-permute-start.2 = (bf16[512,128]{1,0:T(8,128)(2,1)S(1)}, bf16[512,128]{1,0:T(8,128)(2,1)S(1)}, u32[]{:S(2)}, u32[]{:S(2)}) collective-permute-start(bf16[512,128]{1,0:T(8,128)(2,1)S(1)} %get-tuple-element.68.refs_2_), channel_id=1, source_target_pairs={{0,4},{1,5},{2,3},{3,2},{4,0},{5,1},{6,7},{7,6},{8,12},{9,13},{10,... | collective-permute-start | bytes 393224 | tf_op jit(solution)/shard_map/ppermute | solution.py:149
  9.5 5.1 %copy-start.2 = (s32[1,8,8]{2,1,0:T(8,128)S(1)}, s32[1,8,8]{2,1,0:T(8,128)}, u32[]{:S(2)}) copy-start(s32[1,8,8]{2,1,0:T(8,128)} %param.13) | copy-start | bytes 772
  10.7 4.8 %copy-start.1 = (bf16[1,4,1024,128]{3,2,1,0:T(8,128)(2,1)S(1)}, bf16[1,4,1024,128]{3,2,1,0:T(8,128)(2,1)}, u32[]{:S(2)}) copy-start(bf16[1,4,1024,128]{3,2,1,0:T(8,128)(2,1)} %param.9) | copy-start | bytes 3145732
  12.2 5.7 %collective-permute-start.4 = (bf16[512,128]{1,0:T(8,128)(2,1)S(1)}, bf16[512,128]{1,0:T(8,128)(2,1)S(1)}, u32[]{:S(2)}, u32[]{:S(2)}) collective-permute-start(bf16[512,128]{1,0:T(8,128)(2,1)S(1)} %collective-permute-done.3.refs_4_), channel_id=1, source_target_pairs={{0,4},{1,5},{2,3},{3,2},{4,0},{5,1},{6,7},{7,6},{8,12},{9,13},{10,... | collective-permute-start | bytes 393224 | tf_op jit(solution)/shard_map/ppermute | solution.py:149
  12.8 9.9 %collective-permute-start.8 = (bf16[512,128]{1,0:T(8,128)(2,1)S(1)}, bf16[512,128]{1,0:T(8,128)(2,1)S(1)}, u32[]{:S(2)}, u32[]{:S(2)}) collective-permute-start(bf16[512,128]{1,0:T(8,128)(2,1)S(1)} %get-tuple-element.68.refs_2_), channel_id=1, source_target_pairs={{0,3},{1,2},{2,1},{3,0},{4,7},{5,6},{6,5},{7,4},{8,11},{9,10},{10,... | collective-permute-start | bytes 393224 | tf_op jit(solution)/shard_map/ppermute | solution.py:149
  12.8 11.3 %collective-permute-start.9 = (bf16[512,128]{1,0:T(8,128)(2,1)S(1)}, bf16[512,128]{1,0:T(8,128)(2,1)S(1)}, u32[]{:S(2)}, u32[]{:S(2)}) collective-permute-start(bf16[512,128]{1,0:T(8,128)(2,1)S(1)} %get-tuple-element.68.refs_2_), channel_id=1, source_target_pairs={{0,3},{1,2},{2,5},{3,4},{4,7},{5,6},{6,1},{7,0},{8,11},{9,10},{10,... | collective-permute-start | bytes 393224 | tf_op jit(solution)/shard_map/ppermute | solution.py:149
  16.4 7.8 %collective-permute-start.11 = (bf16[512,128]{1,0:T(8,128)(2,1)S(1)}, bf16[512,128]{1,0:T(8,128)(2,1)S(1)}, u32[]{:S(2)}, u32[]{:S(2)}) collective-permute-start(bf16[512,128]{1,0:T(8,128)(2,1)S(1)} %collective-permute-done.10.refs_4_), channel_id=1, source_target_pairs={{0,4},{1,5},{2,3},{3,2},{4,0},{5,1},{6,7},{7,6},{8,12},{9,13},{10,... | collective-permute-start | bytes 393224 | tf_op jit(solution)/shard_map/ppermute | solution.py:149
  18.6 9.4 %collective-permute-start.5 = (bf16[128,256]{1,0:T(8,128)(2,1)S(1)}, bf16[128,256]{1,0:T(8,128)(2,1)S(1)}, u32[]{:S(2)}, u32[]{:S(2)}) collective-permute-start(bf16[128,256]{1,0:T(8,128)(2,1)S(1)} %get-tuple-element.73), channel_id=1, source_target_pairs={{0,4},{1,5},{2,3},{3,2},{4,0},{5,1},{6,7},{7,6},{8,12},{9,13},{10,... | collective-permute-start | bytes 196616 | tf_op jit(solution)/shard_map/ppermute | solution.py:149
  19.3 10.1 %collective-permute-start.6 = (bf16[128,256]{1,0:T(8,128)(2,1)S(1)}, bf16[128,256]{1,0:T(8,128)(2,1)S(1)}, u32[]{:S(2)}, u32[]{:S(2)}) collective-permute-start(bf16[128,256]{1,0:T(8,128)(2,1)S(1)} %get-tuple-element.74), channel_id=1, source_target_pairs={{0,8},{1,9},{2,3},{3,2},{4,12},{5,13},{6,7},{7,6},{8,0},{9,1},{10,... | collective-permute-start | bytes 196616 | tf_op jit(solution)/shard_map/ppermute | solution.py:149
  22.8 6.7 %collective-permute-start.7 = (bf16[128,256]{1,0:T(8,128)(2,1)S(1)}, bf16[128,256]{1,0:T(8,128)(2,1)S(1)}, u32[]{:S(2)}, u32[]{:S(2)}) collective-permute-start(bf16[128,256]{1,0:T(8,128)(2,1)S(1)} %get-tuple-element.75), channel_id=1, source_target_pairs={{0,12},{1,13},{2,3},{3,2},{4,8},{5,9},{6,7},{7,6},{8,4},{9,5},{10,... | collective-permute-start | bytes 196616 | tf_op jit(solution)/shard_map/ppermute | solution.py:149
  25.0 8.3 %collective-permute-start.16 = (bf16[128,256]{1,0:T(8,128)(2,1)S(1)}, bf16[128,256]{1,0:T(8,128)(2,1)S(1)}, u32[]{:S(2)}, u32[]{:S(2)}) collective-permute-start(bf16[128,256]{1,0:T(8,128)(2,1)S(1)} %get-tuple-element.82), channel_id=1, source_target_pairs={{0,4},{1,5},{2,3},{3,2},{4,0},{5,1},{6,7},{7,6},{8,12},{9,13},{10,... | collective-permute-start | bytes 196616 | tf_op jit(solution)/shard_map/ppermute | solution.py:149
  26.1 8.1 %collective-permute-start.17 = (bf16[128,256]{1,0:T(8,128)(2,1)S(1)}, bf16[128,256]{1,0:T(8,128)(2,1)S(1)}, u32[]{:S(2)}, u32[]{:S(2)}) collective-permute-start(bf16[128,256]{1,0:T(8,128)(2,1)S(1)} %get-tuple-element.83), channel_id=1, source_target_pairs={{0,8},{1,9},{2,3},{3,2},{4,12},{5,13},{6,7},{7,6},{8,0},{9,1},{10,... | collective-permute-start | bytes 196616 | tf_op jit(solution)/shard_map/ppermute | solution.py:149
  28.0 6.2 %collective-permute-start.18 = (bf16[128,256]{1,0:T(8,128)(2,1)S(1)}, bf16[128,256]{1,0:T(8,128)(2,1)S(1)}, u32[]{:S(2)}, u32[]{:S(2)}) collective-permute-start(bf16[128,256]{1,0:T(8,128)(2,1)S(1)} %get-tuple-element.84), channel_id=1, source_target_pairs={{0,12},{1,13},{2,3},{3,2},{4,8},{5,9},{6,7},{7,6},{8,4},{9,5},{10,... | collective-permute-start | bytes 196616 | tf_op jit(solution)/shard_map/ppermute | solution.py:149
  29.9 11.8 %collective-permute-start.12 = (bf16[128,512]{1,0:T(8,128)(2,1)S(1)}, bf16[128,512]{1,0:T(8,128)(2,1)S(1)}, u32[]{:S(2)}, u32[]{:S(2)}) collective-permute-start(bf16[128,512]{1,0:T(8,128)(2,1)S(1)} %get-tuple-element.89), channel_id=1, source_target_pairs={{0,3},{1,2},{2,1},{3,0},{4,7},{5,6},{6,5},{7,4},{8,11},{9,10},{10,... | collective-permute-start | bytes 393224 | tf_op jit(solution)/shard_map/ppermute | solution.py:149
  30.0 11.7 %collective-permute-start.14 = (bf16[128,512]{1,0:T(8,128)(2,1)S(1)}, bf16[128,512]{1,0:T(8,128)(2,1)S(1)}, u32[]{:S(2)}, u32[]{:S(2)}) collective-permute-start(bf16[128,512]{1,0:T(8,128)(2,1)S(1)} %get-tuple-element.90), channel_id=1, source_target_pairs={{0,11},{1,10},{2,1},{3,0},{4,15},{5,14},{6,5},{7,4},{8,3},{9,2},{1... | collective-permute-start | bytes 393224 | tf_op jit(solution)/shard_map/ppermute | solution.py:149
  34.7 7.5 %collective-permute-start.22 = (bf16[128,512]{1,0:T(8,128)(2,1)S(1)}, bf16[128,512]{1,0:T(8,128)(2,1)S(1)}, u32[]{:S(2)}, u32[]{:S(2)}) collective-permute-start(bf16[128,512]{1,0:T(8,128)(2,1)S(1)} %get-tuple-element.95), channel_id=1, source_target_pairs={{0,3},{1,2},{2,1},{3,0},{4,7},{5,6},{6,5},{7,4},{8,11},{9,10},{10,... | collective-permute-start | bytes 393224 | tf_op jit(solution)/shard_map/ppermute | solution.py:149
  34.8 9.4 %collective-permute-start.24 = (bf16[128,512]{1,0:T(8,128)(2,1)S(1)}, bf16[128,512]{1,0:T(8,128)(2,1)S(1)}, u32[]{:S(2)}, u32[]{:S(2)}) collective-permute-start(bf16[128,512]{1,0:T(8,128)(2,1)S(1)} %get-tuple-element.96), channel_id=1, source_target_pairs={{0,11},{1,10},{2,1},{3,0},{4,15},{5,14},{6,5},{7,4},{8,3},{9,2},{1... | collective-permute-start | bytes 393224 | tf_op jit(solution)/shard_map/ppermute | solution.py:149
  41.7 2.5 %collective-permute-start.13 = (bf16[128,512]{1,0:T(8,128)(2,1)S(1)}, bf16[128,512]{1,0:T(8,128)(2,1)S(1)}, u32[]{:S(2)}, u32[]{:S(2)}) collective-permute-start(bf16[128,512]{1,0:T(8,128)(2,1)S(1)} %collective-permute-done.12.refs_2_), channel_id=1, source_target_pairs={{0,1},{1,0},{2,6},{3,7},{4,5},{5,4},{6,2},{7,3},{8,9},{9,8},{10,14... | collective-permute-start | bytes 393224 | tf_op jit(solution)/shard_map/ppermute | solution.py:149
  41.7 2.5 %collective-permute-start.15 = (bf16[128,512]{1,0:T(8,128)(2,1)S(1)}, bf16[128,512]{1,0:T(8,128)(2,1)S(1)}, u32[]{:S(2)}, u32[]{:S(2)}) collective-permute-start(bf16[128,512]{1,0:T(8,128)(2,1)S(1)} %collective-permute-done.14.refs_4_), channel_id=1, source_target_pairs={{0,1},{1,0},{2,6},{3,7},{4,5},{5,4},{6,2},{7,3},{8,9},{9,8},{10,14... | collective-permute-start | bytes 393224 | tf_op jit(solution)/shard_map/ppermute | solution.py:149
  42.2 3.0 %collective-permute-start.23 = (bf16[128,512]{1,0:T(8,128)(2,1)S(1)}, bf16[128,512]{1,0:T(8,128)(2,1)S(1)}, u32[]{:S(2)}, u32[]{:S(2)}) collective-permute-start(bf16[128,512]{1,0:T(8,128)(2,1)S(1)} %collective-permute-done.22.refs_2_), channel_id=1, source_target_pairs={{0,1},{1,0},{2,6},{3,7},{4,5},{5,4},{6,2},{7,3},{8,9},{9,8},{10,14... | collective-permute-start | bytes 393224 | tf_op jit(solution)/shard_map/ppermute | solution.py:149
  44.2 1.3 %collective-permute-start.25 = (bf16[128,512]{1,0:T(8,128)(2,1)S(1)}, bf16[128,512]{1,0:T(8,128)(2,1)S(1)}, u32[]{:S(2)}, u32[]{:S(2)}) collective-permute-start(bf16[128,512]{1,0:T(8,128)(2,1)S(1)} %collective-permute-done.24.refs_4_), channel_id=1, source_target_pairs={{0,1},{1,0},{2,6},{3,7},{4,5},{5,4},{6,2},{7,3},{8,9},{9,8},{10,14... | collective-permute-start | bytes 393224 | tf_op jit(solution)/shard_map/ppermute | solution.py:149
  44.2 1.8 %collective-permute-start.19 = (bf16[128,256]{1,0:T(8,128)(2,1)S(1)}, bf16[128,256]{1,0:T(8,128)(2,1)S(1)}, u32[]{:S(2)}, u32[]{:S(2)}) collective-permute-start(bf16[128,256]{1,0:T(8,128)(2,1)S(1)} %get-tuple-element.102), channel_id=1, source_target_pairs={{0,1},{1,0},{2,6},{3,7},{4,5},{5,4},{6,2},{7,3},{8,9},{9,8},{10,14... | collective-permute-start | bytes 196616 | tf_op jit(solution)/shard_map/ppermute | solution.py:149
  44.7 1.5 %collective-permute-start.20 = (bf16[128,256]{1,0:T(8,128)(2,1)S(1)}, bf16[128,256]{1,0:T(8,128)(2,1)S(1)}, u32[]{:S(2)}, u32[]{:S(2)}) collective-permute-start(bf16[128,256]{1,0:T(8,128)(2,1)S(1)} %get-tuple-element.103), channel_id=1, source_target_pairs={{0,1},{1,0},{2,10},{3,11},{4,5},{5,4},{6,14},{7,15},{8,9},{9,8},{1... | collective-permute-start | bytes 196616 | tf_op jit(solution)/shard_map/ppermute | solution.py:149
  44.8 1.4 %collective-permute-start.21 = (bf16[128,256]{1,0:T(8,128)(2,1)S(1)}, bf16[128,256]{1,0:T(8,128)(2,1)S(1)}, u32[]{:S(2)}, u32[]{:S(2)}) collective-permute-start(bf16[128,256]{1,0:T(8,128)(2,1)S(1)} %get-tuple-element.104), channel_id=1, source_target_pairs={{0,1},{1,0},{2,14},{3,15},{4,5},{5,4},{6,10},{7,11},{8,9},{9,8},{1... | collective-permute-start | bytes 196616 | tf_op jit(solution)/shard_map/ppermute | solution.py:149
  45.5 14.5 %collective-permute-start.27 = (bf16[128,256]{1,0:T(8,128)(2,1)S(1)}, bf16[128,256]{1,0:T(8,128)(2,1)S(1)}, u32[]{:S(2)}, u32[]{:S(2)}) collective-permute-start(bf16[128,256]{1,0:T(8,128)(2,1)S(1)} %get-tuple-element.110), channel_id=1, source_target_pairs={{0,1},{1,0},{2,6},{3,7},{4,5},{5,4},{6,2},{7,3},{8,9},{9,8},{10,14... | collective-permute-start | bytes 196616 | tf_op jit(solution)/shard_map/ppermute | solution.py:149
  45.7 14.3 %collective-permute-start.28 = (bf16[128,256]{1,0:T(8,128)(2,1)S(1)}, bf16[128,256]{1,0:T(8,128)(2,1)S(1)}, u32[]{:S(2)}, u32[]{:S(2)}) collective-permute-start(bf16[128,256]{1,0:T(8,128)(2,1)S(1)} %get-tuple-element.111), channel_id=1, source_target_pairs={{0,1},{1,0},{2,10},{3,11},{4,5},{5,4},{6,14},{7,15},{8,9},{9,8},{1... | collective-permute-start | bytes 196616 | tf_op jit(solution)/shard_map/ppermute | solution.py:149
  46.0 14.0 %collective-permute-start.29 = (bf16[128,256]{1,0:T(8,128)(2,1)S(1)}, bf16[128,256]{1,0:T(8,128)(2,1)S(1)}, u32[]{:S(2)}, u32[]{:S(2)}) collective-permute-start(bf16[128,256]{1,0:T(8,128)(2,1)S(1)} %get-tuple-element.112), channel_id=1, source_target_pairs={{0,1},{1,0},{2,14},{3,15},{4,5},{5,4},{6,10},{7,11},{8,9},{9,8},{1... | collective-permute-start | bytes 196616 | tf_op jit(solution)/shard_map/ppermute | solution.py:149
  46.2 18.9 %collective-permute-start.26 = (bf16[1024,128]{1,0:T(8,128)(2,1)S(1)}, bf16[1024,128]{1,0:T(8,128)(2,1)S(1)}, u32[]{:S(2)}, u32[]{:S(2)}) collective-permute-start(bf16[1024,128]{1,0:T(8,128)(2,1)S(1)} %shard_map.83), channel_id=1, source_target_pairs={{0,3},{1,2},{2,1},{3,0},{4,7},{5,6},{6,5},{7,4},{8,11},{9,10},{10,... | collective-permute-start | bytes 786440 | tf_op jit(solution)/shard_map/ppermute | solution.py:149
  (4 other events, 8.6 us)

commit v6 on v5

--- a/solution.py
+++ b/solution.py
@@ -70,13 +70,13 @@
     )(links, own_tiles, bias, half_ordered)
 
 
-def layer_kernel(tile_list, out_groups, raw, final, active_section, *refs):
+def layer_kernel(tile_list, out_groups, raw, final, active_section, stage, *refs):
     ordered, shifts = refs[:2]
     buffer_count = 1 + max(buffer for buffer, _, _ in tile_list)
     buffers = refs[2 : 2 + buffer_count]
     rest = list(refs[2 + buffer_count :])
     settled = rest.pop(0) if final == "merge" else None
-    out_count = 1 if final else len(out_groups)
+    out_count = 1 if final or stage == "begin" else len(out_groups)
     outs = rest[:out_count]
     turned = rest[out_count] if raw else None
     section = lax.axis_index("section")
@@ -88,7 +88,7 @@
             for place, (buffer, column, _) in enumerate(tile_list):
                 turned[place] = buffers[buffer][pl.ds(column, width), :].T
         for distance in reversed(range(ordered.shape[0])):
-            total = shifts[pl.ds(distance, 1), :]
+            total = shifts[distance] if stage == "rest" else shifts[pl.ds(distance, 1), :]
             for place, (buffer, column, key) in enumerate(tile_list):
                 left = turned[place] if raw else buffers[buffer][:, pl.ds(column, width)]
                 if raw:
@@ -96,6 +96,9 @@
                 low = pl.multiple_of(key * width, width) if raw else key * width
                 right = ordered[distance, pl.ds(low, width), :]
                 total = total + jnp.dot(left, right, preferred_element_type=jnp.float32)
+            if stage == "begin":
+                outs[0][distance] = total
+                continue
             value = jnp.clip(total, 0.0, CEILING).astype(jnp.bfloat16)
             if final:
                 outs[0][pl.ds(pl.multiple_of((me ^ distance) * width, width), width), :] = value.T
@@ -112,17 +115,19 @@
             outs[0][...] = settled[...]
 
 
-def layer(ordered, shifts, buffers, tile_list, out_groups, active_section, raw=False, final=None, settled=None, cost=1):
+def layer(ordered, shifts, buffers, tile_list, out_groups, active_section, raw=False, final=None, settled=None, cost=1, stage=None):
     count, depth, width = ordered.shape
     rows = buffers[0].shape[1] if raw else buffers[0].shape[0]
-    if final:
+    if stage == "begin":
+        shapes = [jax.ShapeDtypeStruct((count, rows, width), jnp.float32)]
+    elif final:
         shapes = [jax.ShapeDtypeStruct((count * width, rows), jnp.bfloat16)]
     else:
         shapes = [jax.ShapeDtypeStruct((rows, len(group) * width), jnp.bfloat16) for group in out_groups]
     vmem = pl.BlockSpec(memory_space=pltpu.VMEM)
     operands = [ordered, shifts, *buffers] + ([settled] if final == "merge" else [])
     return pl.pallas_call(
-        functools.partial(layer_kernel, tile_list, out_groups, raw, final, active_section),
+        functools.partial(layer_kernel, tile_list, out_groups, raw, final, active_section, stage),
         out_shape=shapes,
         in_specs=[vmem] * len(operands),
         out_specs=[vmem] * len(shapes),
@@ -201,10 +206,16 @@
 
     parts_zero = first_layer(after(start, second[0]), 0, True, cost=LAG)
     parts_one = first_layer(after(later, parts_zero), 0, True)
+    def handed_layer(buffers, earlier, cost=1):
+        *ready, last = buffers
+        begun = layer(*first, after(ready, earlier), later_tiles[:6], apart, 1, stage="begin")[0]
+        rest = [(0, column, key) for _, column, key in later_tiles[6:]]
+        return layer(first[0], begun, [last], rest, apart, 1, cost=cost, stage="rest")
+
     zero = second_layer(parts_zero, 0, parts_one, cost=LAG)
     one = second_layer(parts_one, 0, zero)
-    parts_zero = first_layer(after(hand_over(zero), one), 1, False, cost=LAG)
-    parts_one = first_layer(after(hand_over(one), parts_zero), 1, False)
+    parts_zero = handed_layer(hand_over(zero), one, cost=LAG)
+    parts_one = handed_layer(hand_over(one), parts_zero)
     settled = second_layer(parts_zero, 1, parts_one, final="plain", cost=LAG)
     last = second_layer(parts_one, 1, settled, final="plain", cost=TAIL)[0]
     return jnp.where(lax.axis_index("section") == 0, moved(settled[0], across(0, 1)), last)[None]

time: 66 us -> 66 us (level)
    pallas_call x8 -> x10, Pallas kernels: 2.47 us -> 2.47 us  [layer(): pl.pallas_call(functools.partial(layer_kernel, tile_list, out_groups, raw...]
where the time goes in v6:
time: 66 us; the launch traced here: 65.8 us
  starting transfers between devices  46.7 us (71%)
  waiting for transfers between devices  9.42 us (14%)
  Pallas kernels  6.72 us (10%)
  local copies, waits for them, and re-layouts  2.03 us (3%)
  other arithmetic  0.73 us (1%)
    ppermute x28, starting transfers between devices, moved(): return lax.ppermute(value, ('owners', 'section', 'rep'), pairs)  46.2 us
    ppermute x28, waiting for transfers between devices, moved(): return lax.ppermute(value, ('owners', 'section', 'rep'), pairs)  9.41 us
    pallas_call x10, Pallas kernels, layer(): pl.pallas_call(functools.partial(layer_kernel, tile_list, out_groups, raw...  2.47 us
    pallas_call x2, Pallas kernels, order_weights(): pl.pallas_call(order_own_kernel, out_shape=[ordered, jax.ShapeDtypeStruct...  2.13 us
    pallas_call x2, Pallas kernels, order_weights(): pl.pallas_call(order_other_kernel, out_shape=ordered, in_specs=[smem, vme...  2.12 us
  transfers between devices with their start and end apart: 30, of which 5 were waited for; matrix products, arithmetic and copies ran while one was open for 1% of the time, Pallas kernels for 10%

profile of v6, /device:TPU:0, one launch (start us, length us, event | category | flops | bytes accessed | tf_op | source)
XLA Modules:
  0.0 65.8 jit_solution(12702620945305416466)
XLA Ops:
  0.0 0.5 collective-permute-start.1
  0.5 1.0 %dynamic-slice_bitcast_fusion = (bf16[512,128]{1,0:T(8,128)(2,1)S(1)}, bf16[512,128]{1,0:T(8,128)(2,1)S(1)}) fusion(bf16[2,512,128]{2,1,0:T(8,128)(2,1)} %bitcast.23, s32[]{:T(128)S(6)} %select_n.24, s32[]{:T(128)S(6)} %select_n.23), kind=kLoop, calls=%fused_computation.1 | loop fusion | bytes 524296 | tf_op jit(solution)/shard_map/jit(dynamic_index_in_dim)/squeeze | solution.py:167
  1.5 4.1 %collective-permute-start.3 = (bf16[512,128]{1,0:T(8,128)(2,1)S(1)}, bf16[512,128]{1,0:T(8,128)(2,1)S(1)}, u32[]{:S(2)}, u32[]{:S(2)}) collective-permute-start(bf16[512,128]{1,0:T(8,128)(2,1)S(1)} %get-tuple-element.117), channel_id=1, source_target_pairs={{0,8},{1,9},{2,3},{3,2},{4,12},{5,13},{6,7},{7,6},{8,0},{9,1},{10,... | collective-permute-start | bytes 393224 | tf_op jit(solution)/shard_map/ppermute | solution.py:154
  5.6 1.6 %collective-permute-start.2 = (bf16[512,128]{1,0:T(8,128)(2,1)S(1)}, bf16[512,128]{1,0:T(8,128)(2,1)S(1)}, u32[]{:S(2)}, u32[]{:S(2)}) collective-permute-start(bf16[512,128]{1,0:T(8,128)(2,1)S(1)} %get-tuple-element.66.refs_2_), channel_id=1, source_target_pairs={{0,4},{1,5},{2,3},{3,2},{4,0},{5,1},{6,7},{7,6},{8,12},{9,13},{10,... | collective-permute-start | bytes 393224 | tf_op jit(solution)/shard_map/ppermute | solution.py:154
  7.2 0.7 %copy-done.3 = s32[1,8,16]{2,1,0:T(8,128)S(1)} copy-done((s32[1,8,16]{2,1,0:T(8,128)S(1)}, s32[1,8,16]{2,1,0:T(8,128)}, u32[]{:S(2)}) %copy-start.3) | copy-done | bytes 536
  7.9 1.2 %shard_map.75.half_ordered = bf16[4,2048,256]{2,1,0:T(8,128)(2,1)S(1)} custom-call(s32[8,16]{1,0:T(8,128)S(1)} %bitcast.19, bf16[4,2048,128]{2,1,0:T(8,128)(2,1)S(1)} %collective-permute-done.1.other_tiles), custom_call_target="tpu_custom_call" | custom-call | flops 1 | bytes 1 | tf_op jit(solution)/shard_map/pallas_call | solution.py:60
  9.5 1.2 %shard_map.76 = (bf16[4,2048,256]{2,1,0:T(8,128)(2,1)S(1)}, f32[4,256]{1,0:T(4,128)S(1)}) custom-call(s32[8,16]{1,0:T(8,128)S(1)} %bitcast.20, bf16[4,2048,128]{2,1,0:T(8,128)(2,1)S(1)} %bitcast.14, f32[8,128]{1,0:T(8,128)S(1)} %bitcast.21, bf16[4,2048,256]{2,1,0:T(8,128)(2,1)S(1)} %shard_map.75.half_ordered), custom_call_target="tpu_custom_call", output_to_operand_aliasing={{0}: (3, {})} | custom-call | flops 1 | bytes 1 | tf_op jit(solution)/shard_map/pallas_call | solution.py:63
  10.8 1.4 %collective-permute-done.3.refs_4_ = bf16[512,128]{1,0:T(8,128)(2,1)S(1)} collective-permute-done((bf16[512,128]{1,0:T(8,128)(2,1)S(1)}, bf16[512,128]{1,0:T(8,128)(2,1)S(1)}, u32[]{:S(2)}, u32[]{:S(2)}) %collective-permute-start.3) | collective-permute-done | bytes 131104 | tf_op jit(solution)/shard_map/ppermute | solution.py:154
  12.2 0.7 collective-permute-start.4
  12.8 1.7 %collective-permute-start.9 = (bf16[512,128]{1,0:T(8,128)(2,1)S(1)}, bf16[512,128]{1,0:T(8,128)(2,1)S(1)}, u32[]{:S(2)}, u32[]{:S(2)}) collective-permute-start(bf16[512,128]{1,0:T(8,128)(2,1)S(1)} %get-tuple-element.66.refs_2_), channel_id=1, source_target_pairs={{0,3},{1,2},{2,5},{3,4},{4,7},{5,6},{6,1},{7,0},{8,11},{9,10},{10,... | collective-permute-start | bytes 393224 | tf_op jit(solution)/shard_map/ppermute | solution.py:154
  14.6 0.9 %shard_map.73.half_ordered = bf16[4,1024,256]{2,1,0:T(8,128)(2,1)S(1)} custom-call(s32[8,8]{1,0:T(8,128)S(1)} %bitcast.17, bf16[4,1024,128]{2,1,0:T(8,128)(2,1)S(1)} %collective-permute-done.other_tiles), custom_call_target="tpu_custom_call" | custom-call | flops 1 | bytes 1 | tf_op jit(solution)/shard_map/pallas_call | solution.py:60
  15.5 0.9 %shard_map.74 = (bf16[4,1024,256]{2,1,0:T(8,128)(2,1)S(1)}, f32[4,256]{1,0:T(4,128)S(1)}) custom-call(s32[8,8]{1,0:T(8,128)S(1)} %bitcast.18, bf16[4,1024,128]{2,1,0:T(8,128)(2,1)S(1)} %bitcast.16, f32[8,128]{1,0:T(8,128)S(1)} %bitcast.22, bf16[4,1024,256]{2,1,0:T(8,128)(2,1)S(1)} %shard_map.73.half_ordered), custom_call_target="tpu_custom_call", output_to_operand_aliasing={{0}: (3, {})} | custom-call | flops 1 | bytes 1 | tf_op jit(solution)/shard_map/pallas_call | solution.py:63
  16.4 1.4 %collective-permute-start.11 = (bf16[512,128]{1,0:T(8,128)(2,1)S(1)}, bf16[512,128]{1,0:T(8,128)(2,1)S(1)}, u32[]{:S(2)}, u32[]{:S(2)}) collective-permute-start(bf16[512,128]{1,0:T(8,128)(2,1)S(1)} %collective-permute-done.10.refs_4_), channel_id=1, source_target_pairs={{0,4},{1,5},{2,3},{3,2},{4,0},{5,1},{6,7},{7,6},{8,12},{9,13},{10,... | collective-permute-start | bytes 393224 | tf_op jit(solution)/shard_map/ppermute | solution.py:154
  17.8 0.8 %shard_map.77 = (bf16[128,256]{1,0:T(8,128)(2,1)S(1)}, bf16[128,256]{1,0:T(8,128)(2,1)S(1)}, bf16[128,256]{1,0:T(8,128)(2,1)S(1)}, bf16[128,256]{1,0:T(8,128)(2,1)S(1)}) custom-call(bf16[4,2048,256]{2,1,0:T(8,128)(2,1)S(1)} %get-tuple-element.63.refs_0_, f32[4,256]{1,0:T(4,128)S(1)} %get-tuple-element.64.refs_1_, ...), custom_call_target="tpu_custom_call" | custom-call | flops 1 | bytes 1 | tf_op jit(solution)/shard_map/pallas_call | solution.py:129
  18.6 0.7 %collective-permute-start.5 = (bf16[128,256]{1,0:T(8,128)(2,1)S(1)}, bf16[128,256]{1,0:T(8,128)(2,1)S(1)}, u32[]{:S(2)}, u32[]{:S(2)}) collective-permute-start(bf16[128,256]{1,0:T(8,128)(2,1)S(1)} %get-tuple-element.71), channel_id=1, source_target_pairs={{0,4},{1,5},{2,3},{3,2},{4,0},{5,1},{6,7},{7,6},{8,12},{9,13},{10,... | collective-permute-start | bytes 196616 | tf_op jit(solution)/shard_map/ppermute | solution.py:154
  19.3 3.4 %collective-permute-start.6 = (bf16[128,256]{1,0:T(8,128)(2,1)S(1)}, bf16[128,256]{1,0:T(8,128)(2,1)S(1)}, u32[]{:S(2)}, u32[]{:S(2)}) collective-permute-start(bf16[128,256]{1,0:T(8,128)(2,1)S(1)} %get-tuple-element.72), channel_id=1, source_target_pairs={{0,8},{1,9},{2,3},{3,2},{4,12},{5,13},{6,7},{7,6},{8,0},{9,1},{10,... | collective-permute-start | bytes 196616 | tf_op jit(solution)/shard_map/ppermute | solution.py:154
  22.8 1.4 %collective-permute-start.7 = (bf16[128,256]{1,0:T(8,128)(2,1)S(1)}, bf16[128,256]{1,0:T(8,128)(2,1)S(1)}, u32[]{:S(2)}, u32[]{:S(2)}) collective-permute-start(bf16[128,256]{1,0:T(8,128)(2,1)S(1)} %get-tuple-element.73), channel_id=1, source_target_pairs={{0,12},{1,13},{2,3},{3,2},{4,8},{5,9},{6,7},{7,6},{8,4},{9,5},{10,... | collective-permute-start | bytes 196616 | tf_op jit(solution)/shard_map/ppermute | solution.py:154
  24.2 0.8 %shard_map.78 = (bf16[128,256]{1,0:T(8,128)(2,1)S(1)}, bf16[128,256]{1,0:T(8,128)(2,1)S(1)}, bf16[128,256]{1,0:T(8,128)(2,1)S(1)}, bf16[128,256]{1,0:T(8,128)(2,1)S(1)}) custom-call(bf16[4,2048,256]{2,1,0:T(8,128)(2,1)S(1)} %get-tuple-element.63.refs_0_, f32[4,256]{1,0:T(4,128)S(1)} %get-tuple-element.64.refs_1_, ...), custom_call_target="tpu_custom_call" | custom-call | flops 1 | bytes 1 | tf_op jit(solution)/shard_map/pallas_call | solution.py:129
  25.0 1.2 %collective-permute-start.15 = (bf16[128,256]{1,0:T(8,128)(2,1)S(1)}, bf16[128,256]{1,0:T(8,128)(2,1)S(1)}, u32[]{:S(2)}, u32[]{:S(2)}) collective-permute-start(bf16[128,256]{1,0:T(8,128)(2,1)S(1)} %get-tuple-element.80), channel_id=1, source_target_pairs={{0,4},{1,5},{2,3},{3,2},{4,0},{5,1},{6,7},{7,6},{8,12},{9,13},{10,... | collective-permute-start | bytes 196616 | tf_op jit(solution)/shard_map/ppermute | solution.py:154
  26.1 1.8 %collective-permute-start.16 = (bf16[128,256]{1,0:T(8,128)(2,1)S(1)}, bf16[128,256]{1,0:T(8,128)(2,1)S(1)}, u32[]{:S(2)}, u32[]{:S(2)}) collective-permute-start(bf16[128,256]{1,0:T(8,128)(2,1)S(1)} %get-tuple-element.81), channel_id=1, source_target_pairs={{0,8},{1,9},{2,3},{3,2},{4,12},{5,13},{6,7},{7,6},{8,0},{9,1},{10,... | collective-permute-start | bytes 196616 | tf_op jit(solution)/shard_map/ppermute | solution.py:154
  28.0 1.4 %collective-permute-start.17 = (bf16[128,256]{1,0:T(8,128)(2,1)S(1)}, bf16[128,256]{1,0:T(8,128)(2,1)S(1)}, u32[]{:S(2)}, u32[]{:S(2)}) collective-permute-start(bf16[128,256]{1,0:T(8,128)(2,1)S(1)} %get-tuple-element.82), channel_id=1, source_target_pairs={{0,12},{1,13},{2,3},{3,2},{4,8},{5,9},{6,7},{7,6},{8,4},{9,5},{10,... | collective-permute-start | bytes 196616 | tf_op jit(solution)/shard_map/ppermute | solution.py:154
  29.4 0.5 shard_map.79
  30.0 3.3 %collective-permute-start.14 = (bf16[128,512]{1,0:T(8,128)(2,1)S(1)}, bf16[128,512]{1,0:T(8,128)(2,1)S(1)}, u32[]{:S(2)}, u32[]{:S(2)}) collective-permute-start(bf16[128,512]{1,0:T(8,128)(2,1)S(1)} %get-tuple-element.88), channel_id=1, source_target_pairs={{0,11},{1,10},{2,1},{3,0},{4,15},{5,14},{6,5},{7,4},{8,3},{9,2},{1... | collective-permute-start | bytes 393224 | tf_op jit(solution)/shard_map/ppermute | solution.py:154
  33.2 1.0 %collective-permute-done.16.refs_4_ = bf16[128,256]{1,0:T(8,128)(2,1)S(1)} collective-permute-done((bf16[128,256]{1,0:T(8,128)(2,1)S(1)}, bf16[128,256]{1,0:T(8,128)(2,1)S(1)}, u32[]{:S(2)}, u32[]{:S(2)}) %collective-permute-start.16) | collective-permute-done | bytes 65568 | tf_op jit(solution)/shard_map/ppermute | solution.py:154
  34.2 0.5 shard_map.80
  34.8 6.9 %collective-permute-start.24 = (bf16[128,512]{1,0:T(8,128)(2,1)S(1)}, bf16[128,512]{1,0:T(8,128)(2,1)S(1)}, u32[]{:S(2)}, u32[]{:S(2)}) collective-permute-start(bf16[128,512]{1,0:T(8,128)(2,1)S(1)} %get-tuple-element.94), channel_id=1, source_target_pairs={{0,11},{1,10},{2,1},{3,0},{4,15},{5,14},{6,5},{7,4},{8,3},{9,2},{1... | collective-permute-start | bytes 393224 | tf_op jit(solution)/shard_map/ppermute | solution.py:154
  41.7 0.5 collective-permute-start.18
  42.3 1.9 %collective-permute-done.24.refs_4_ = bf16[128,512]{1,0:T(8,128)(2,1)S(1)} collective-permute-done((bf16[128,512]{1,0:T(8,128)(2,1)S(1)}, bf16[128,512]{1,0:T(8,128)(2,1)S(1)}, u32[]{:S(2)}, u32[]{:S(2)}) %collective-permute-start.24) | collective-permute-done | bytes 131104 | tf_op jit(solution)/shard_map/ppermute | solution.py:154
  44.2 0.5 collective-permute-start.19
  46.2 14.1 %collective-permute-start.26 = (bf16[1024,128]{1,0:T(8,128)(2,1)S(1)}, bf16[1024,128]{1,0:T(8,128)(2,1)S(1)}, u32[]{:S(2)}, u32[]{:S(2)}) collective-permute-start(bf16[1024,128]{1,0:T(8,128)(2,1)S(1)} %shard_map.85), channel_id=1, source_target_pairs={{0,3},{1,2},{2,1},{3,0},{4,7},{5,6},{6,5},{7,4},{8,11},{9,10},{10,... | collective-permute-start | bytes 786440 | tf_op jit(solution)/shard_map/ppermute | solution.py:154
  60.3 4.8 %collective-permute-done.26 = bf16[1024,128]{1,0:T(8,128)(2,1)S(1)} collective-permute-done((bf16[1024,128]{1,0:T(8,128)(2,1)S(1)}, bf16[1024,128]{1,0:T(8,128)(2,1)S(1)}, u32[]{:S(2)}, u32[]{:S(2)}) %collective-permute-start.26) | collective-permute-done | bytes 262176 | tf_op jit(solution)/shard_map/ppermute | solution.py:154
  65.1 0.7 %select_bitcast_fusion = bf16[1,1024,128]{2,1,0:T(8,128)(2,1)} fusion(bf16[1024,128]{1,0:T(8,128)(2,1)S(1)} %collective-permute-done.26, bf16[1024,128]{1,0:T(8,128)(2,1)S(1)} %shard_map.86, pred[]{:T(512)S(6)} %eq.3), kind=kLoop, calls=%fused_computation | loop fusion | flops 131072 | bytes 786433 | tf_op jit(solution)/shard_map/broadcast_in_dim | solution.py:221
  (56 shorter events, 2.2 us)
Async XLA Ops:
  0.0 7.2 %collective-permute-start.1 = (bf16[4,2048,128]{2,1,0:T(8,128)(2,1)}, bf16[4,2048,128]{2,1,0:T(8,128)(2,1)S(1)}, u32[]{:S(2)}, u32[]{:S(2)}) collective-permute-start(bf16[4,2048,128]{2,1,0:T(8,128)(2,1)} %bitcast.13), channel_id=1, source_target_pairs={{0,1},{1,0},{2,3},{3,2},{4,5},{5,4},{6,7},{7,6},{8,9},{9,8},{10,11... | collective-permute-start | bytes 6291464 | tf_op jit(solution)/shard_map/ppermute | solution.py:163
  0.5 12.4 %collective-permute-start = (bf16[4,1024,128]{2,1,0:T(8,128)(2,1)}, bf16[4,1024,128]{2,1,0:T(8,128)(2,1)S(1)}, u32[]{:S(2)}, u32[]{:S(2)}) collective-permute-start(bf16[4,1024,128]{2,1,0:T(8,128)(2,1)} %bitcast.15), channel_id=1, source_target_pairs={{0,1},{1,0},{2,3},{3,2},{4,5},{5,4},{6,7},{7,6},{8,9},{9,8},{10,11... | collective-permute-start | bytes 3145736 | tf_op jit(solution)/shard_map/ppermute | solution.py:163
  1.5 10.7 %collective-permute-start.3 = (bf16[512,128]{1,0:T(8,128)(2,1)S(1)}, bf16[512,128]{1,0:T(8,128)(2,1)S(1)}, u32[]{:S(2)}, u32[]{:S(2)}) collective-permute-start(bf16[512,128]{1,0:T(8,128)(2,1)S(1)} %get-tuple-element.117), channel_id=1, source_target_pairs={{0,8},{1,9},{2,3},{3,2},{4,12},{5,13},{6,7},{7,6},{8,0},{9,1},{10,... | collective-permute-start | bytes 393224 | tf_op jit(solution)/shard_map/ppermute | solution.py:154
  5.6 10.8 %collective-permute-start.10 = (bf16[512,128]{1,0:T(8,128)(2,1)S(1)}, bf16[512,128]{1,0:T(8,128)(2,1)S(1)}, u32[]{:S(2)}, u32[]{:S(2)}) collective-permute-start(bf16[512,128]{1,0:T(8,128)(2,1)S(1)} %get-tuple-element.117), channel_id=1, source_target_pairs={{0,3},{1,2},{2,9},{3,8},{4,7},{5,6},{6,13},{7,12},{8,11},{9,10},{1... | collective-permute-start | bytes 393224 | tf_op jit(solution)/shard_map/ppermute | solution.py:154
  5.6 12.2 %collective-permute-start.2 = (bf16[512,128]{1,0:T(8,128)(2,1)S(1)}, bf16[512,128]{1,0:T(8,128)(2,1)S(1)}, u32[]{:S(2)}, u32[]{:S(2)}) collective-permute-start(bf16[512,128]{1,0:T(8,128)(2,1)S(1)} %get-tuple-element.66.refs_2_), channel_id=1, source_target_pairs={{0,4},{1,5},{2,3},{3,2},{4,0},{5,1},{6,7},{7,6},{8,12},{9,13},{10,... | collective-permute-start | bytes 393224 | tf_op jit(solution)/shard_map/ppermute | solution.py:154
  9.5 5.1 %copy-start.2 = (s32[1,8,8]{2,1,0:T(8,128)S(1)}, s32[1,8,8]{2,1,0:T(8,128)}, u32[]{:S(2)}) copy-start(s32[1,8,8]{2,1,0:T(8,128)} %param.13) | copy-start | bytes 772
  10.7 4.8 %copy-start.1 = (bf16[1,4,1024,128]{3,2,1,0:T(8,128)(2,1)S(1)}, bf16[1,4,1024,128]{3,2,1,0:T(8,128)(2,1)}, u32[]{:S(2)}) copy-start(bf16[1,4,1024,128]{3,2,1,0:T(8,128)(2,1)} %param.9) | copy-start | bytes 3145732
  12.2 5.7 %collective-permute-start.4 = (bf16[512,128]{1,0:T(8,128)(2,1)S(1)}, bf16[512,128]{1,0:T(8,128)(2,1)S(1)}, u32[]{:S(2)}, u32[]{:S(2)}) collective-permute-start(bf16[512,128]{1,0:T(8,128)(2,1)S(1)} %collective-permute-done.3.refs_4_), channel_id=1, source_target_pairs={{0,4},{1,5},{2,3},{3,2},{4,0},{5,1},{6,7},{7,6},{8,12},{9,13},{10,... | collective-permute-start | bytes 393224 | tf_op jit(solution)/shard_map/ppermute | solution.py:154
  12.8 9.9 %collective-permute-start.8 = (bf16[512,128]{1,0:T(8,128)(2,1)S(1)}, bf16[512,128]{1,0:T(8,128)(2,1)S(1)}, u32[]{:S(2)}, u32[]{:S(2)}) collective-permute-start(bf16[512,128]{1,0:T(8,128)(2,1)S(1)} %get-tuple-element.66.refs_2_), channel_id=1, source_target_pairs={{0,3},{1,2},{2,1},{3,0},{4,7},{5,6},{6,5},{7,4},{8,11},{9,10},{10,... | collective-permute-start | bytes 393224 | tf_op jit(solution)/shard_map/ppermute | solution.py:154
  12.8 11.3 %collective-permute-start.9 = (bf16[512,128]{1,0:T(8,128)(2,1)S(1)}, bf16[512,128]{1,0:T(8,128)(2,1)S(1)}, u32[]{:S(2)}, u32[]{:S(2)}) collective-permute-start(bf16[512,128]{1,0:T(8,128)(2,1)S(1)} %get-tuple-element.66.refs_2_), channel_id=1, source_target_pairs={{0,3},{1,2},{2,5},{3,4},{4,7},{5,6},{6,1},{7,0},{8,11},{9,10},{10,... | collective-permute-start | bytes 393224 | tf_op jit(solution)/shard_map/ppermute | solution.py:154
  16.4 7.8 %collective-permute-start.11 = (bf16[512,128]{1,0:T(8,128)(2,1)S(1)}, bf16[512,128]{1,0:T(8,128)(2,1)S(1)}, u32[]{:S(2)}, u32[]{:S(2)}) collective-permute-start(bf16[512,128]{1,0:T(8,128)(2,1)S(1)} %collective-permute-done.10.refs_4_), channel_id=1, source_target_pairs={{0,4},{1,5},{2,3},{3,2},{4,0},{5,1},{6,7},{7,6},{8,12},{9,13},{10,... | collective-permute-start | bytes 393224 | tf_op jit(solution)/shard_map/ppermute | solution.py:154
  18.6 9.4 %collective-permute-start.5 = (bf16[128,256]{1,0:T(8,128)(2,1)S(1)}, bf16[128,256]{1,0:T(8,128)(2,1)S(1)}, u32[]{:S(2)}, u32[]{:S(2)}) collective-permute-start(bf16[128,256]{1,0:T(8,128)(2,1)S(1)} %get-tuple-element.71), channel_id=1, source_target_pairs={{0,4},{1,5},{2,3},{3,2},{4,0},{5,1},{6,7},{7,6},{8,12},{9,13},{10,... | collective-permute-start | bytes 196616 | tf_op jit(solution)/shard_map/ppermute | solution.py:154
  19.3 10.1 %collective-permute-start.6 = (bf16[128,256]{1,0:T(8,128)(2,1)S(1)}, bf16[128,256]{1,0:T(8,128)(2,1)S(1)}, u32[]{:S(2)}, u32[]{:S(2)}) collective-permute-start(bf16[128,256]{1,0:T(8,128)(2,1)S(1)} %get-tuple-element.72), channel_id=1, source_target_pairs={{0,8},{1,9},{2,3},{3,2},{4,12},{5,13},{6,7},{7,6},{8,0},{9,1},{10,... | collective-permute-start | bytes 196616 | tf_op jit(solution)/shard_map/ppermute | solution.py:154
  22.8 6.7 %collective-permute-start.7 = (bf16[128,256]{1,0:T(8,128)(2,1)S(1)}, bf16[128,256]{1,0:T(8,128)(2,1)S(1)}, u32[]{:S(2)}, u32[]{:S(2)}) collective-permute-start(bf16[128,256]{1,0:T(8,128)(2,1)S(1)} %get-tuple-element.73), channel_id=1, source_target_pairs={{0,12},{1,13},{2,3},{3,2},{4,8},{5,9},{6,7},{7,6},{8,4},{9,5},{10,... | collective-permute-start | bytes 196616 | tf_op jit(solution)/shard_map/ppermute | solution.py:154
  25.0 8.3 %collective-permute-start.15 = (bf16[128,256]{1,0:T(8,128)(2,1)S(1)}, bf16[128,256]{1,0:T(8,128)(2,1)S(1)}, u32[]{:S(2)}, u32[]{:S(2)}) collective-permute-start(bf16[128,256]{1,0:T(8,128)(2,1)S(1)} %get-tuple-element.80), channel_id=1, source_target_pairs={{0,4},{1,5},{2,3},{3,2},{4,0},{5,1},{6,7},{7,6},{8,12},{9,13},{10,... | collective-permute-start | bytes 196616 | tf_op jit(solution)/shard_map/ppermute | solution.py:154
  26.1 8.1 %collective-permute-start.16 = (bf16[128,256]{1,0:T(8,128)(2,1)S(1)}, bf16[128,256]{1,0:T(8,128)(2,1)S(1)}, u32[]{:S(2)}, u32[]{:S(2)}) collective-permute-start(bf16[128,256]{1,0:T(8,128)(2,1)S(1)} %get-tuple-element.81), channel_id=1, source_target_pairs={{0,8},{1,9},{2,3},{3,2},{4,12},{5,13},{6,7},{7,6},{8,0},{9,1},{10,... | collective-permute-start | bytes 196616 | tf_op jit(solution)/shard_map/ppermute | solution.py:154
  28.0 6.2 %collective-permute-start.17 = (bf16[128,256]{1,0:T(8,128)(2,1)S(1)}, bf16[128,256]{1,0:T(8,128)(2,1)S(1)}, u32[]{:S(2)}, u32[]{:S(2)}) collective-permute-start(bf16[128,256]{1,0:T(8,128)(2,1)S(1)} %get-tuple-element.82), channel_id=1, source_target_pairs={{0,12},{1,13},{2,3},{3,2},{4,8},{5,9},{6,7},{7,6},{8,4},{9,5},{10,... | collective-permute-start | bytes 196616 | tf_op jit(solution)/shard_map/ppermute | solution.py:154
  29.9 11.8 %collective-permute-start.12 = (bf16[128,512]{1,0:T(8,128)(2,1)S(1)}, bf16[128,512]{1,0:T(8,128)(2,1)S(1)}, u32[]{:S(2)}, u32[]{:S(2)}) collective-permute-start(bf16[128,512]{1,0:T(8,128)(2,1)S(1)} %get-tuple-element.87), channel_id=1, source_target_pairs={{0,3},{1,2},{2,1},{3,0},{4,7},{5,6},{6,5},{7,4},{8,11},{9,10},{10,... | collective-permute-start | bytes 393224 | tf_op jit(solution)/shard_map/ppermute | solution.py:154
  30.0 11.7 %collective-permute-start.14 = (bf16[128,512]{1,0:T(8,128)(2,1)S(1)}, bf16[128,512]{1,0:T(8,128)(2,1)S(1)}, u32[]{:S(2)}, u32[]{:S(2)}) collective-permute-start(bf16[128,512]{1,0:T(8,128)(2,1)S(1)} %get-tuple-element.88), channel_id=1, source_target_pairs={{0,11},{1,10},{2,1},{3,0},{4,15},{5,14},{6,5},{7,4},{8,3},{9,2},{1... | collective-permute-start | bytes 393224 | tf_op jit(solution)/shard_map/ppermute | solution.py:154
  34.7 7.5 %collective-permute-start.22 = (bf16[128,512]{1,0:T(8,128)(2,1)S(1)}, bf16[128,512]{1,0:T(8,128)(2,1)S(1)}, u32[]{:S(2)}, u32[]{:S(2)}) collective-permute-start(bf16[128,512]{1,0:T(8,128)(2,1)S(1)} %get-tuple-element.93), channel_id=1, source_target_pairs={{0,3},{1,2},{2,1},{3,0},{4,7},{5,6},{6,5},{7,4},{8,11},{9,10},{10,... | collective-permute-start | bytes 393224 | tf_op jit(solution)/shard_map/ppermute | solution.py:154
  34.8 9.4 %collective-permute-start.24 = (bf16[128,512]{1,0:T(8,128)(2,1)S(1)}, bf16[128,512]{1,0:T(8,128)(2,1)S(1)}, u32[]{:S(2)}, u32[]{:S(2)}) collective-permute-start(bf16[128,512]{1,0:T(8,128)(2,1)S(1)} %get-tuple-element.94), channel_id=1, source_target_pairs={{0,11},{1,10},{2,1},{3,0},{4,15},{5,14},{6,5},{7,4},{8,3},{9,2},{1... | collective-permute-start | bytes 393224 | tf_op jit(solution)/shard_map/ppermute | solution.py:154
  41.7 2.5 %collective-permute-start.13 = (bf16[128,512]{1,0:T(8,128)(2,1)S(1)}, bf16[128,512]{1,0:T(8,128)(2,1)S(1)}, u32[]{:S(2)}, u32[]{:S(2)}) collective-permute-start(bf16[128,512]{1,0:T(8,128)(2,1)S(1)} %collective-permute-done.12.refs_2_), channel_id=1, source_target_pairs={{0,1},{1,0},{2,6},{3,7},{4,5},{5,4},{6,2},{7,3},{8,9},{9,8},{10,14... | collective-permute-start | bytes 393224 | tf_op jit(solution)/shard_map/ppermute | solution.py:154
  41.7 2.5 %collective-permute-start.18 = (bf16[128,512]{1,0:T(8,128)(2,1)S(1)}, bf16[128,512]{1,0:T(8,128)(2,1)S(1)}, u32[]{:S(2)}, u32[]{:S(2)}) collective-permute-start(bf16[128,512]{1,0:T(8,128)(2,1)S(1)} %collective-permute-done.14.refs_4_), channel_id=1, source_target_pairs={{0,1},{1,0},{2,6},{3,7},{4,5},{5,4},{6,2},{7,3},{8,9},{9,8},{10,14... | collective-permute-start | bytes 393224 | tf_op jit(solution)/shard_map/ppermute | solution.py:154
  42.2 3.1 %collective-permute-start.23 = (bf16[128,512]{1,0:T(8,128)(2,1)S(1)}, bf16[128,512]{1,0:T(8,128)(2,1)S(1)}, u32[]{:S(2)}, u32[]{:S(2)}) collective-permute-start(bf16[128,512]{1,0:T(8,128)(2,1)S(1)} %collective-permute-done.22.refs_2_), channel_id=1, source_target_pairs={{0,1},{1,0},{2,6},{3,7},{4,5},{5,4},{6,2},{7,3},{8,9},{9,8},{10,14... | collective-permute-start | bytes 393224 | tf_op jit(solution)/shard_map/ppermute | solution.py:154
  44.2 1.3 %collective-permute-start.25 = (bf16[128,512]{1,0:T(8,128)(2,1)S(1)}, bf16[128,512]{1,0:T(8,128)(2,1)S(1)}, u32[]{:S(2)}, u32[]{:S(2)}) collective-permute-start(bf16[128,512]{1,0:T(8,128)(2,1)S(1)} %collective-permute-done.24.refs_4_), channel_id=1, source_target_pairs={{0,1},{1,0},{2,6},{3,7},{4,5},{5,4},{6,2},{7,3},{8,9},{9,8},{10,14... | collective-permute-start | bytes 393224 | tf_op jit(solution)/shard_map/ppermute | solution.py:154
  44.2 1.8 %collective-permute-start.19 = (bf16[128,256]{1,0:T(8,128)(2,1)S(1)}, bf16[128,256]{1,0:T(8,128)(2,1)S(1)}, u32[]{:S(2)}, u32[]{:S(2)}) collective-permute-start(bf16[128,256]{1,0:T(8,128)(2,1)S(1)} %get-tuple-element.99), channel_id=1, source_target_pairs={{0,1},{1,0},{2,6},{3,7},{4,5},{5,4},{6,2},{7,3},{8,9},{9,8},{10,14... | collective-permute-start | bytes 196616 | tf_op jit(solution)/shard_map/ppermute | solution.py:154
  44.8 1.4 %collective-permute-start.20 = (bf16[128,256]{1,0:T(8,128)(2,1)S(1)}, bf16[128,256]{1,0:T(8,128)(2,1)S(1)}, u32[]{:S(2)}, u32[]{:S(2)}) collective-permute-start(bf16[128,256]{1,0:T(8,128)(2,1)S(1)} %get-tuple-element.100), channel_id=1, source_target_pairs={{0,1},{1,0},{2,10},{3,11},{4,5},{5,4},{6,14},{7,15},{8,9},{9,8},{1... | collective-permute-start | bytes 196616 | tf_op jit(solution)/shard_map/ppermute | solution.py:154
  44.8 1.4 %collective-permute-start.21 = (bf16[128,256]{1,0:T(8,128)(2,1)S(1)}, bf16[128,256]{1,0:T(8,128)(2,1)S(1)}, u32[]{:S(2)}, u32[]{:S(2)}) collective-permute-start(bf16[128,256]{1,0:T(8,128)(2,1)S(1)} %get-tuple-element.101), channel_id=1, source_target_pairs={{0,1},{1,0},{2,14},{3,15},{4,5},{5,4},{6,10},{7,11},{8,9},{9,8},{1... | collective-permute-start | bytes 196616 | tf_op jit(solution)/shard_map/ppermute | solution.py:154
  45.5 14.8 %collective-permute-start.27 = (bf16[128,256]{1,0:T(8,128)(2,1)S(1)}, bf16[128,256]{1,0:T(8,128)(2,1)S(1)}, u32[]{:S(2)}, u32[]{:S(2)}) collective-permute-start(bf16[128,256]{1,0:T(8,128)(2,1)S(1)} %get-tuple-element.106), channel_id=1, source_target_pairs={{0,1},{1,0},{2,6},{3,7},{4,5},{5,4},{6,2},{7,3},{8,9},{9,8},{10,14... | collective-permute-start | bytes 196616 | tf_op jit(solution)/shard_map/ppermute | solution.py:154
  45.7 14.6 %collective-permute-start.28 = (bf16[128,256]{1,0:T(8,128)(2,1)S(1)}, bf16[128,256]{1,0:T(8,128)(2,1)S(1)}, u32[]{:S(2)}, u32[]{:S(2)}) collective-permute-start(bf16[128,256]{1,0:T(8,128)(2,1)S(1)} %get-tuple-element.107), channel_id=1, source_target_pairs={{0,1},{1,0},{2,10},{3,11},{4,5},{5,4},{6,14},{7,15},{8,9},{9,8},{1... | collective-permute-start | bytes 196616 | tf_op jit(solution)/shard_map/ppermute | solution.py:154
  46.0 14.2 %collective-permute-start.29 = (bf16[128,256]{1,0:T(8,128)(2,1)S(1)}, bf16[128,256]{1,0:T(8,128)(2,1)S(1)}, u32[]{:S(2)}, u32[]{:S(2)}) collective-permute-start(bf16[128,256]{1,0:T(8,128)(2,1)S(1)} %get-tuple-element.108), channel_id=1, source_target_pairs={{0,1},{1,0},{2,14},{3,15},{4,5},{5,4},{6,10},{7,11},{8,9},{9,8},{1... | collective-permute-start | bytes 196616 | tf_op jit(solution)/shard_map/ppermute | solution.py:154
  46.2 18.9 %collective-permute-start.26 = (bf16[1024,128]{1,0:T(8,128)(2,1)S(1)}, bf16[1024,128]{1,0:T(8,128)(2,1)S(1)}, u32[]{:S(2)}, u32[]{:S(2)}) collective-permute-start(bf16[1024,128]{1,0:T(8,128)(2,1)S(1)} %shard_map.85), channel_id=1, source_target_pairs={{0,3},{1,2},{2,1},{3,0},{4,7},{5,6},{6,5},{7,4},{8,11},{9,10},{10,... | collective-permute-start | bytes 786440 | tf_op jit(solution)/shard_map/ppermute | solution.py:154
  (4 other events, 8.6 us)

commit v7 on v6

--- a/solution.py
+++ b/solution.py
@@ -202,7 +202,8 @@
 
     def hand_over(result):
         close, apart = result
-        return gathered(moved(close, across(0, 0)), moved(apart, across(2, 0)), 1)
+        apart = moved(apart, across(2, 0))
+        return gathered(moved(close, across(0, 0)), apart, 1)
 
     parts_zero = first_layer(after(start, second[0]), 0, True, cost=LAG)
     parts_one = first_layer(after(later, parts_zero), 0, True)

time: 66 us -> 66 us (level)
  no operation moved by 1% of the time
where the time goes in v7:
time: 66 us; the launch traced here: 65.8 us
  starting transfers between devices  46.7 us (71%)
  waiting for transfers between devices  9.42 us (14%)
  Pallas kernels  6.72 us (10%)
  local copies, waits for them, and re-layouts  2.03 us (3%)
  other arithmetic  0.73 us (1%)
    ppermute x28, starting transfers between devices, moved(): return lax.ppermute(value, ('owners', 'section', 'rep'), pairs)  46.2 us
    ppermute x28, waiting for transfers between devices, moved(): return lax.ppermute(value, ('owners', 'section', 'rep'), pairs)  9.41 us
    pallas_call x10, Pallas kernels, layer(): pl.pallas_call(functools.partial(layer_kernel, tile_list, out_groups, raw...  2.47 us
    pallas_call x2, Pallas kernels, order_weights(): pl.pallas_call(order_own_kernel, out_shape=[ordered, jax.ShapeDtypeStruct...  2.13 us
    pallas_call x2, Pallas kernels, order_weights(): pl.pallas_call(order_other_kernel, out_shape=ordered, in_specs=[smem, vme...  2.12 us
  transfers between devices with their start and end apart: 30, of which 5 were waited for; matrix products, arithmetic and copies ran while one was open for 1% of the time, Pallas kernels for 10%

profile of v7, /device:TPU:0, one launch (start us, length us, event | category | flops | bytes accessed | tf_op | source)
XLA Modules:
  0.0 65.8 jit_solution(12702620945305416466)
XLA Ops:
  0.0 0.5 collective-permute-start.1
  0.5 1.0 %dynamic-slice_bitcast_fusion = (bf16[512,128]{1,0:T(8,128)(2,1)S(1)}, bf16[512,128]{1,0:T(8,128)(2,1)S(1)}) fusion(bf16[2,512,128]{2,1,0:T(8,128)(2,1)} %bitcast.23, s32[]{:T(128)S(6)} %select_n.24, s32[]{:T(128)S(6)} %select_n.23), kind=kLoop, calls=%fused_computation.1 | loop fusion | bytes 524296 | tf_op jit(solution)/shard_map/jit(dynamic_index_in_dim)/squeeze | solution.py:167
  1.5 4.1 %collective-permute-start.3 = (bf16[512,128]{1,0:T(8,128)(2,1)S(1)}, bf16[512,128]{1,0:T(8,128)(2,1)S(1)}, u32[]{:S(2)}, u32[]{:S(2)}) collective-permute-start(bf16[512,128]{1,0:T(8,128)(2,1)S(1)} %get-tuple-element.117), channel_id=1, source_target_pairs={{0,8},{1,9},{2,3},{3,2},{4,12},{5,13},{6,7},{7,6},{8,0},{9,1},{10,... | collective-permute-start | bytes 393224 | tf_op jit(solution)/shard_map/ppermute | solution.py:154
  5.6 1.6 %collective-permute-start.2 = (bf16[512,128]{1,0:T(8,128)(2,1)S(1)}, bf16[512,128]{1,0:T(8,128)(2,1)S(1)}, u32[]{:S(2)}, u32[]{:S(2)}) collective-permute-start(bf16[512,128]{1,0:T(8,128)(2,1)S(1)} %get-tuple-element.66.refs_2_), channel_id=1, source_target_pairs={{0,4},{1,5},{2,3},{3,2},{4,0},{5,1},{6,7},{7,6},{8,12},{9,13},{10,... | collective-permute-start | bytes 393224 | tf_op jit(solution)/shard_map/ppermute | solution.py:154
  7.2 0.7 %copy-done.3 = s32[1,8,16]{2,1,0:T(8,128)S(1)} copy-done((s32[1,8,16]{2,1,0:T(8,128)S(1)}, s32[1,8,16]{2,1,0:T(8,128)}, u32[]{:S(2)}) %copy-start.3) | copy-done | bytes 536
  7.9 1.2 %shard_map.75.half_ordered = bf16[4,2048,256]{2,1,0:T(8,128)(2,1)S(1)} custom-call(s32[8,16]{1,0:T(8,128)S(1)} %bitcast.19, bf16[4,2048,128]{2,1,0:T(8,128)(2,1)S(1)} %collective-permute-done.1.other_tiles), custom_call_target="tpu_custom_call" | custom-call | flops 1 | bytes 1 | tf_op jit(solution)/shard_map/pallas_call | solution.py:60
  9.5 1.2 %shard_map.76 = (bf16[4,2048,256]{2,1,0:T(8,128)(2,1)S(1)}, f32[4,256]{1,0:T(4,128)S(1)}) custom-call(s32[8,16]{1,0:T(8,128)S(1)} %bitcast.20, bf16[4,2048,128]{2,1,0:T(8,128)(2,1)S(1)} %bitcast.14, f32[8,128]{1,0:T(8,128)S(1)} %bitcast.21, bf16[4,2048,256]{2,1,0:T(8,128)(2,1)S(1)} %shard_map.75.half_ordered), custom_call_target="tpu_custom_call", output_to_operand_aliasing={{0}: (3, {})} | custom-call | flops 1 | bytes 1 | tf_op jit(solution)/shard_map/pallas_call | solution.py:63
  10.8 1.4 %collective-permute-done.3.refs_4_ = bf16[512,128]{1,0:T(8,128)(2,1)S(1)} collective-permute-done((bf16[512,128]{1,0:T(8,128)(2,1)S(1)}, bf16[512,128]{1,0:T(8,128)(2,1)S(1)}, u32[]{:S(2)}, u32[]{:S(2)}) %collective-permute-start.3) | collective-permute-done | bytes 131104 | tf_op jit(solution)/shard_map/ppermute | solution.py:154
  12.2 0.7 collective-permute-start.4
  12.8 1.7 %collective-permute-start.9 = (bf16[512,128]{1,0:T(8,128)(2,1)S(1)}, bf16[512,128]{1,0:T(8,128)(2,1)S(1)}, u32[]{:S(2)}, u32[]{:S(2)}) collective-permute-start(bf16[512,128]{1,0:T(8,128)(2,1)S(1)} %get-tuple-element.66.refs_2_), channel_id=1, source_target_pairs={{0,3},{1,2},{2,5},{3,4},{4,7},{5,6},{6,1},{7,0},{8,11},{9,10},{10,... | collective-permute-start | bytes 393224 | tf_op jit(solution)/shard_map/ppermute | solution.py:154
  14.6 0.9 %shard_map.73.half_ordered = bf16[4,1024,256]{2,1,0:T(8,128)(2,1)S(1)} custom-call(s32[8,8]{1,0:T(8,128)S(1)} %bitcast.17, bf16[4,1024,128]{2,1,0:T(8,128)(2,1)S(1)} %collective-permute-done.other_tiles), custom_call_target="tpu_custom_call" | custom-call | flops 1 | bytes 1 | tf_op jit(solution)/shard_map/pallas_call | solution.py:60
  15.5 0.9 %shard_map.74 = (bf16[4,1024,256]{2,1,0:T(8,128)(2,1)S(1)}, f32[4,256]{1,0:T(4,128)S(1)}) custom-call(s32[8,8]{1,0:T(8,128)S(1)} %bitcast.18, bf16[4,1024,128]{2,1,0:T(8,128)(2,1)S(1)} %bitcast.16, f32[8,128]{1,0:T(8,128)S(1)} %bitcast.22, bf16[4,1024,256]{2,1,0:T(8,128)(2,1)S(1)} %shard_map.73.half_ordered), custom_call_target="tpu_custom_call", output_to_operand_aliasing={{0}: (3, {})} | custom-call | flops 1 | bytes 1 | tf_op jit(solution)/shard_map/pallas_call | solution.py:63
  16.4 1.4 %collective-permute-start.11 = (bf16[512,128]{1,0:T(8,128)(2,1)S(1)}, bf16[512,128]{1,0:T(8,128)(2,1)S(1)}, u32[]{:S(2)}, u32[]{:S(2)}) collective-permute-start(bf16[512,128]{1,0:T(8,128)(2,1)S(1)} %collective-permute-done.10.refs_4_), channel_id=1, source_target_pairs={{0,4},{1,5},{2,3},{3,2},{4,0},{5,1},{6,7},{7,6},{8,12},{9,13},{10,... | collective-permute-start | bytes 393224 | tf_op jit(solution)/shard_map/ppermute | solution.py:154
  17.8 0.8 %shard_map.77 = (bf16[128,256]{1,0:T(8,128)(2,1)S(1)}, bf16[128,256]{1,0:T(8,128)(2,1)S(1)}, bf16[128,256]{1,0:T(8,128)(2,1)S(1)}, bf16[128,256]{1,0:T(8,128)(2,1)S(1)}) custom-call(bf16[4,2048,256]{2,1,0:T(8,128)(2,1)S(1)} %get-tuple-element.63.refs_0_, f32[4,256]{1,0:T(4,128)S(1)} %get-tuple-element.64.refs_1_, ...), custom_call_target="tpu_custom_call" | custom-call | flops 1 | bytes 1 | tf_op jit(solution)/shard_map/pallas_call | solution.py:129
  18.6 0.7 %collective-permute-start.5 = (bf16[128,256]{1,0:T(8,128)(2,1)S(1)}, bf16[128,256]{1,0:T(8,128)(2,1)S(1)}, u32[]{:S(2)}, u32[]{:S(2)}) collective-permute-start(bf16[128,256]{1,0:T(8,128)(2,1)S(1)} %get-tuple-element.71), channel_id=1, source_target_pairs={{0,4},{1,5},{2,3},{3,2},{4,0},{5,1},{6,7},{7,6},{8,12},{9,13},{10,... | collective-permute-start | bytes 196616 | tf_op jit(solution)/shard_map/ppermute | solution.py:154
  19.3 3.4 %collective-permute-start.6 = (bf16[128,256]{1,0:T(8,128)(2,1)S(1)}, bf16[128,256]{1,0:T(8,128)(2,1)S(1)}, u32[]{:S(2)}, u32[]{:S(2)}) collective-permute-start(bf16[128,256]{1,0:T(8,128)(2,1)S(1)} %get-tuple-element.72), channel_id=1, source_target_pairs={{0,8},{1,9},{2,3},{3,2},{4,12},{5,13},{6,7},{7,6},{8,0},{9,1},{10,... | collective-permute-start | bytes 196616 | tf_op jit(solution)/shard_map/ppermute | solution.py:154
  22.8 1.4 %collective-permute-start.7 = (bf16[128,256]{1,0:T(8,128)(2,1)S(1)}, bf16[128,256]{1,0:T(8,128)(2,1)S(1)}, u32[]{:S(2)}, u32[]{:S(2)}) collective-permute-start(bf16[128,256]{1,0:T(8,128)(2,1)S(1)} %get-tuple-element.73), channel_id=1, source_target_pairs={{0,12},{1,13},{2,3},{3,2},{4,8},{5,9},{6,7},{7,6},{8,4},{9,5},{10,... | collective-permute-start | bytes 196616 | tf_op jit(solution)/shard_map/ppermute | solution.py:154
  24.2 0.8 %shard_map.78 = (bf16[128,256]{1,0:T(8,128)(2,1)S(1)}, bf16[128,256]{1,0:T(8,128)(2,1)S(1)}, bf16[128,256]{1,0:T(8,128)(2,1)S(1)}, bf16[128,256]{1,0:T(8,128)(2,1)S(1)}) custom-call(bf16[4,2048,256]{2,1,0:T(8,128)(2,1)S(1)} %get-tuple-element.63.refs_0_, f32[4,256]{1,0:T(4,128)S(1)} %get-tuple-element.64.refs_1_, ...), custom_call_target="tpu_custom_call" | custom-call | flops 1 | bytes 1 | tf_op jit(solution)/shard_map/pallas_call | solution.py:129
  25.0 1.2 %collective-permute-start.15 = (bf16[128,256]{1,0:T(8,128)(2,1)S(1)}, bf16[128,256]{1,0:T(8,128)(2,1)S(1)}, u32[]{:S(2)}, u32[]{:S(2)}) collective-permute-start(bf16[128,256]{1,0:T(8,128)(2,1)S(1)} %get-tuple-element.80), channel_id=1, source_target_pairs={{0,4},{1,5},{2,3},{3,2},{4,0},{5,1},{6,7},{7,6},{8,12},{9,13},{10,... | collective-permute-start | bytes 196616 | tf_op jit(solution)/shard_map/ppermute | solution.py:154
  26.1 1.8 %collective-permute-start.16 = (bf16[128,256]{1,0:T(8,128)(2,1)S(1)}, bf16[128,256]{1,0:T(8,128)(2,1)S(1)}, u32[]{:S(2)}, u32[]{:S(2)}) collective-permute-start(bf16[128,256]{1,0:T(8,128)(2,1)S(1)} %get-tuple-element.81), channel_id=1, source_target_pairs={{0,8},{1,9},{2,3},{3,2},{4,12},{5,13},{6,7},{7,6},{8,0},{9,1},{10,... | collective-permute-start | bytes 196616 | tf_op jit(solution)/shard_map/ppermute | solution.py:154
  28.0 1.4 %collective-permute-start.17 = (bf16[128,256]{1,0:T(8,128)(2,1)S(1)}, bf16[128,256]{1,0:T(8,128)(2,1)S(1)}, u32[]{:S(2)}, u32[]{:S(2)}) collective-permute-start(bf16[128,256]{1,0:T(8,128)(2,1)S(1)} %get-tuple-element.82), channel_id=1, source_target_pairs={{0,12},{1,13},{2,3},{3,2},{4,8},{5,9},{6,7},{7,6},{8,4},{9,5},{10,... | collective-permute-start | bytes 196616 | tf_op jit(solution)/shard_map/ppermute | solution.py:154
  29.4 0.5 shard_map.79
  30.0 3.3 %collective-permute-start.14 = (bf16[128,512]{1,0:T(8,128)(2,1)S(1)}, bf16[128,512]{1,0:T(8,128)(2,1)S(1)}, u32[]{:S(2)}, u32[]{:S(2)}) collective-permute-start(bf16[128,512]{1,0:T(8,128)(2,1)S(1)} %get-tuple-element.88), channel_id=1, source_target_pairs={{0,11},{1,10},{2,1},{3,0},{4,15},{5,14},{6,5},{7,4},{8,3},{9,2},{1... | collective-permute-start | bytes 393224 | tf_op jit(solution)/shard_map/ppermute | solution.py:154
  33.2 1.0 %collective-permute-done.16.refs_4_ = bf16[128,256]{1,0:T(8,128)(2,1)S(1)} collective-permute-done((bf16[128,256]{1,0:T(8,128)(2,1)S(1)}, bf16[128,256]{1,0:T(8,128)(2,1)S(1)}, u32[]{:S(2)}, u32[]{:S(2)}) %collective-permute-start.16) | collective-permute-done | bytes 65568 | tf_op jit(solution)/shard_map/ppermute | solution.py:154
  34.2 0.5 shard_map.80
  34.8 6.9 %collective-permute-start.24 = (bf16[128,512]{1,0:T(8,128)(2,1)S(1)}, bf16[128,512]{1,0:T(8,128)(2,1)S(1)}, u32[]{:S(2)}, u32[]{:S(2)}) collective-permute-start(bf16[128,512]{1,0:T(8,128)(2,1)S(1)} %get-tuple-element.94), channel_id=1, source_target_pairs={{0,11},{1,10},{2,1},{3,0},{4,15},{5,14},{6,5},{7,4},{8,3},{9,2},{1... | collective-permute-start | bytes 393224 | tf_op jit(solution)/shard_map/ppermute | solution.py:154
  41.7 0.5 collective-permute-start.18
  42.3 1.9 %collective-permute-done.24.refs_4_ = bf16[128,512]{1,0:T(8,128)(2,1)S(1)} collective-permute-done((bf16[128,512]{1,0:T(8,128)(2,1)S(1)}, bf16[128,512]{1,0:T(8,128)(2,1)S(1)}, u32[]{:S(2)}, u32[]{:S(2)}) %collective-permute-start.24) | collective-permute-done | bytes 131104 | tf_op jit(solution)/shard_map/ppermute | solution.py:154
  44.2 0.5 collective-permute-start.19
  46.2 14.1 %collective-permute-start.26 = (bf16[1024,128]{1,0:T(8,128)(2,1)S(1)}, bf16[1024,128]{1,0:T(8,128)(2,1)S(1)}, u32[]{:S(2)}, u32[]{:S(2)}) collective-permute-start(bf16[1024,128]{1,0:T(8,128)(2,1)S(1)} %shard_map.85), channel_id=1, source_target_pairs={{0,3},{1,2},{2,1},{3,0},{4,7},{5,6},{6,5},{7,4},{8,11},{9,10},{10,... | collective-permute-start | bytes 786440 | tf_op jit(solution)/shard_map/ppermute | solution.py:154
  60.3 4.8 %collective-permute-done.26 = bf16[1024,128]{1,0:T(8,128)(2,1)S(1)} collective-permute-done((bf16[1024,128]{1,0:T(8,128)(2,1)S(1)}, bf16[1024,128]{1,0:T(8,128)(2,1)S(1)}, u32[]{:S(2)}, u32[]{:S(2)}) %collective-permute-start.26) | collective-permute-done | bytes 262176 | tf_op jit(solution)/shard_map/ppermute | solution.py:154
  65.1 0.7 %select_bitcast_fusion = bf16[1,1024,128]{2,1,0:T(8,128)(2,1)} fusion(bf16[1024,128]{1,0:T(8,128)(2,1)S(1)} %collective-permute-done.26, bf16[1024,128]{1,0:T(8,128)(2,1)S(1)} %shard_map.86, pred[]{:T(512)S(6)} %eq.3), kind=kLoop, calls=%fused_computation | loop fusion | flops 131072 | bytes 786433 | tf_op jit(solution)/shard_map/broadcast_in_dim | solution.py:222
  (56 shorter events, 2.2 us)
Async XLA Ops:
  0.0 7.2 %collective-permute-start.1 = (bf16[4,2048,128]{2,1,0:T(8,128)(2,1)}, bf16[4,2048,128]{2,1,0:T(8,128)(2,1)S(1)}, u32[]{:S(2)}, u32[]{:S(2)}) collective-permute-start(bf16[4,2048,128]{2,1,0:T(8,128)(2,1)} %bitcast.13), channel_id=1, source_target_pairs={{0,1},{1,0},{2,3},{3,2},{4,5},{5,4},{6,7},{7,6},{8,9},{9,8},{10,11... | collective-permute-start | bytes 6291464 | tf_op jit(solution)/shard_map/ppermute | solution.py:163
  0.5 12.4 %collective-permute-start = (bf16[4,1024,128]{2,1,0:T(8,128)(2,1)}, bf16[4,1024,128]{2,1,0:T(8,128)(2,1)S(1)}, u32[]{:S(2)}, u32[]{:S(2)}) collective-permute-start(bf16[4,1024,128]{2,1,0:T(8,128)(2,1)} %bitcast.15), channel_id=1, source_target_pairs={{0,1},{1,0},{2,3},{3,2},{4,5},{5,4},{6,7},{7,6},{8,9},{9,8},{10,11... | collective-permute-start | bytes 3145736 | tf_op jit(solution)/shard_map/ppermute | solution.py:163
  1.5 10.7 %collective-permute-start.3 = (bf16[512,128]{1,0:T(8,128)(2,1)S(1)}, bf16[512,128]{1,0:T(8,128)(2,1)S(1)}, u32[]{:S(2)}, u32[]{:S(2)}) collective-permute-start(bf16[512,128]{1,0:T(8,128)(2,1)S(1)} %get-tuple-element.117), channel_id=1, source_target_pairs={{0,8},{1,9},{2,3},{3,2},{4,12},{5,13},{6,7},{7,6},{8,0},{9,1},{10,... | collective-permute-start | bytes 393224 | tf_op jit(solution)/shard_map/ppermute | solution.py:154
  5.6 10.8 %collective-permute-start.10 = (bf16[512,128]{1,0:T(8,128)(2,1)S(1)}, bf16[512,128]{1,0:T(8,128)(2,1)S(1)}, u32[]{:S(2)}, u32[]{:S(2)}) collective-permute-start(bf16[512,128]{1,0:T(8,128)(2,1)S(1)} %get-tuple-element.117), channel_id=1, source_target_pairs={{0,3},{1,2},{2,9},{3,8},{4,7},{5,6},{6,13},{7,12},{8,11},{9,10},{1... | collective-permute-start | bytes 393224 | tf_op jit(solution)/shard_map/ppermute | solution.py:154
  5.6 12.2 %collective-permute-start.2 = (bf16[512,128]{1,0:T(8,128)(2,1)S(1)}, bf16[512,128]{1,0:T(8,128)(2,1)S(1)}, u32[]{:S(2)}, u32[]{:S(2)}) collective-permute-start(bf16[512,128]{1,0:T(8,128)(2,1)S(1)} %get-tuple-element.66.refs_2_), channel_id=1, source_target_pairs={{0,4},{1,5},{2,3},{3,2},{4,0},{5,1},{6,7},{7,6},{8,12},{9,13},{10,... | collective-permute-start | bytes 393224 | tf_op jit(solution)/shard_map/ppermute | solution.py:154
  9.5 5.1 %copy-start.2 = (s32[1,8,8]{2,1,0:T(8,128)S(1)}, s32[1,8,8]{2,1,0:T(8,128)}, u32[]{:S(2)}) copy-start(s32[1,8,8]{2,1,0:T(8,128)} %param.13) | copy-start | bytes 772
  10.7 4.8 %copy-start.1 = (bf16[1,4,1024,128]{3,2,1,0:T(8,128)(2,1)S(1)}, bf16[1,4,1024,128]{3,2,1,0:T(8,128)(2,1)}, u32[]{:S(2)}) copy-start(bf16[1,4,1024,128]{3,2,1,0:T(8,128)(2,1)} %param.9) | copy-start | bytes 3145732
  12.2 5.7 %collective-permute-start.4 = (bf16[512,128]{1,0:T(8,128)(2,1)S(1)}, bf16[512,128]{1,0:T(8,128)(2,1)S(1)}, u32[]{:S(2)}, u32[]{:S(2)}) collective-permute-start(bf16[512,128]{1,0:T(8,128)(2,1)S(1)} %collective-permute-done.3.refs_4_), channel_id=1, source_target_pairs={{0,4},{1,5},{2,3},{3,2},{4,0},{5,1},{6,7},{7,6},{8,12},{9,13},{10,... | collective-permute-start | bytes 393224 | tf_op jit(solution)/shard_map/ppermute | solution.py:154
  12.8 9.9 %collective-permute-start.8 = (bf16[512,128]{1,0:T(8,128)(2,1)S(1)}, bf16[512,128]{1,0:T(8,128)(2,1)S(1)}, u32[]{:S(2)}, u32[]{:S(2)}) collective-permute-start(bf16[512,128]{1,0:T(8,128)(2,1)S(1)} %get-tuple-element.66.refs_2_), channel_id=1, source_target_pairs={{0,3},{1,2},{2,1},{3,0},{4,7},{5,6},{6,5},{7,4},{8,11},{9,10},{10,... | collective-permute-start | bytes 393224 | tf_op jit(solution)/shard_map/ppermute | solution.py:154
  12.8 11.3 %collective-permute-start.9 = (bf16[512,128]{1,0:T(8,128)(2,1)S(1)}, bf16[512,128]{1,0:T(8,128)(2,1)S(1)}, u32[]{:S(2)}, u32[]{:S(2)}) collective-permute-start(bf16[512,128]{1,0:T(8,128)(2,1)S(1)} %get-tuple-element.66.refs_2_), channel_id=1, source_target_pairs={{0,3},{1,2},{2,5},{3,4},{4,7},{5,6},{6,1},{7,0},{8,11},{9,10},{10,... | collective-permute-start | bytes 393224 | tf_op jit(solution)/shard_map/ppermute | solution.py:154
  16.4 7.8 %collective-permute-start.11 = (bf16[512,128]{1,0:T(8,128)(2,1)S(1)}, bf16[512,128]{1,0:T(8,128)(2,1)S(1)}, u32[]{:S(2)}, u32[]{:S(2)}) collective-permute-start(bf16[512,128]{1,0:T(8,128)(2,1)S(1)} %collective-permute-done.10.refs_4_), channel_id=1, source_target_pairs={{0,4},{1,5},{2,3},{3,2},{4,0},{5,1},{6,7},{7,6},{8,12},{9,13},{10,... | collective-permute-start | bytes 393224 | tf_op jit(solution)/shard_map/ppermute | solution.py:154
  18.6 9.4 %collective-permute-start.5 = (bf16[128,256]{1,0:T(8,128)(2,1)S(1)}, bf16[128,256]{1,0:T(8,128)(2,1)S(1)}, u32[]{:S(2)}, u32[]{:S(2)}) collective-permute-start(bf16[128,256]{1,0:T(8,128)(2,1)S(1)} %get-tuple-element.71), channel_id=1, source_target_pairs={{0,4},{1,5},{2,3},{3,2},{4,0},{5,1},{6,7},{7,6},{8,12},{9,13},{10,... | collective-permute-start | bytes 196616 | tf_op jit(solution)/shard_map/ppermute | solution.py:154
  19.3 10.1 %collective-permute-start.6 = (bf16[128,256]{1,0:T(8,128)(2,1)S(1)}, bf16[128,256]{1,0:T(8,128)(2,1)S(1)}, u32[]{:S(2)}, u32[]{:S(2)}) collective-permute-start(bf16[128,256]{1,0:T(8,128)(2,1)S(1)} %get-tuple-element.72), channel_id=1, source_target_pairs={{0,8},{1,9},{2,3},{3,2},{4,12},{5,13},{6,7},{7,6},{8,0},{9,1},{10,... | collective-permute-start | bytes 196616 | tf_op jit(solution)/shard_map/ppermute | solution.py:154
  22.8 6.7 %collective-permute-start.7 = (bf16[128,256]{1,0:T(8,128)(2,1)S(1)}, bf16[128,256]{1,0:T(8,128)(2,1)S(1)}, u32[]{:S(2)}, u32[]{:S(2)}) collective-permute-start(bf16[128,256]{1,0:T(8,128)(2,1)S(1)} %get-tuple-element.73), channel_id=1, source_target_pairs={{0,12},{1,13},{2,3},{3,2},{4,8},{5,9},{6,7},{7,6},{8,4},{9,5},{10,... | collective-permute-start | bytes 196616 | tf_op jit(solution)/shard_map/ppermute | solution.py:154
  25.0 8.3 %collective-permute-start.15 = (bf16[128,256]{1,0:T(8,128)(2,1)S(1)}, bf16[128,256]{1,0:T(8,128)(2,1)S(1)}, u32[]{:S(2)}, u32[]{:S(2)}) collective-permute-start(bf16[128,256]{1,0:T(8,128)(2,1)S(1)} %get-tuple-element.80), channel_id=1, source_target_pairs={{0,4},{1,5},{2,3},{3,2},{4,0},{5,1},{6,7},{7,6},{8,12},{9,13},{10,... | collective-permute-start | bytes 196616 | tf_op jit(solution)/shard_map/ppermute | solution.py:154
  26.1 8.1 %collective-permute-start.16 = (bf16[128,256]{1,0:T(8,128)(2,1)S(1)}, bf16[128,256]{1,0:T(8,128)(2,1)S(1)}, u32[]{:S(2)}, u32[]{:S(2)}) collective-permute-start(bf16[128,256]{1,0:T(8,128)(2,1)S(1)} %get-tuple-element.81), channel_id=1, source_target_pairs={{0,8},{1,9},{2,3},{3,2},{4,12},{5,13},{6,7},{7,6},{8,0},{9,1},{10,... | collective-permute-start | bytes 196616 | tf_op jit(solution)/shard_map/ppermute | solution.py:154
  28.0 6.2 %collective-permute-start.17 = (bf16[128,256]{1,0:T(8,128)(2,1)S(1)}, bf16[128,256]{1,0:T(8,128)(2,1)S(1)}, u32[]{:S(2)}, u32[]{:S(2)}) collective-permute-start(bf16[128,256]{1,0:T(8,128)(2,1)S(1)} %get-tuple-element.82), channel_id=1, source_target_pairs={{0,12},{1,13},{2,3},{3,2},{4,8},{5,9},{6,7},{7,6},{8,4},{9,5},{10,... | collective-permute-start | bytes 196616 | tf_op jit(solution)/shard_map/ppermute | solution.py:154
  29.9 11.8 %collective-permute-start.12 = (bf16[128,512]{1,0:T(8,128)(2,1)S(1)}, bf16[128,512]{1,0:T(8,128)(2,1)S(1)}, u32[]{:S(2)}, u32[]{:S(2)}) collective-permute-start(bf16[128,512]{1,0:T(8,128)(2,1)S(1)} %get-tuple-element.87), channel_id=1, source_target_pairs={{0,3},{1,2},{2,1},{3,0},{4,7},{5,6},{6,5},{7,4},{8,11},{9,10},{10,... | collective-permute-start | bytes 393224 | tf_op jit(solution)/shard_map/ppermute | solution.py:154
  30.0 11.7 %collective-permute-start.14 = (bf16[128,512]{1,0:T(8,128)(2,1)S(1)}, bf16[128,512]{1,0:T(8,128)(2,1)S(1)}, u32[]{:S(2)}, u32[]{:S(2)}) collective-permute-start(bf16[128,512]{1,0:T(8,128)(2,1)S(1)} %get-tuple-element.88), channel_id=1, source_target_pairs={{0,11},{1,10},{2,1},{3,0},{4,15},{5,14},{6,5},{7,4},{8,3},{9,2},{1... | collective-permute-start | bytes 393224 | tf_op jit(solution)/shard_map/ppermute | solution.py:154
  34.7 7.5 %collective-permute-start.22 = (bf16[128,512]{1,0:T(8,128)(2,1)S(1)}, bf16[128,512]{1,0:T(8,128)(2,1)S(1)}, u32[]{:S(2)}, u32[]{:S(2)}) collective-permute-start(bf16[128,512]{1,0:T(8,128)(2,1)S(1)} %get-tuple-element.93), channel_id=1, source_target_pairs={{0,3},{1,2},{2,1},{3,0},{4,7},{5,6},{6,5},{7,4},{8,11},{9,10},{10,... | collective-permute-start | bytes 393224 | tf_op jit(solution)/shard_map/ppermute | solution.py:154
  34.8 9.4 %collective-permute-start.24 = (bf16[128,512]{1,0:T(8,128)(2,1)S(1)}, bf16[128,512]{1,0:T(8,128)(2,1)S(1)}, u32[]{:S(2)}, u32[]{:S(2)}) collective-permute-start(bf16[128,512]{1,0:T(8,128)(2,1)S(1)} %get-tuple-element.94), channel_id=1, source_target_pairs={{0,11},{1,10},{2,1},{3,0},{4,15},{5,14},{6,5},{7,4},{8,3},{9,2},{1... | collective-permute-start | bytes 393224 | tf_op jit(solution)/shard_map/ppermute | solution.py:154
  41.7 2.5 %collective-permute-start.13 = (bf16[128,512]{1,0:T(8,128)(2,1)S(1)}, bf16[128,512]{1,0:T(8,128)(2,1)S(1)}, u32[]{:S(2)}, u32[]{:S(2)}) collective-permute-start(bf16[128,512]{1,0:T(8,128)(2,1)S(1)} %collective-permute-done.12.refs_2_), channel_id=1, source_target_pairs={{0,1},{1,0},{2,6},{3,7},{4,5},{5,4},{6,2},{7,3},{8,9},{9,8},{10,14... | collective-permute-start | bytes 393224 | tf_op jit(solution)/shard_map/ppermute | solution.py:154
  41.7 2.5 %collective-permute-start.18 = (bf16[128,512]{1,0:T(8,128)(2,1)S(1)}, bf16[128,512]{1,0:T(8,128)(2,1)S(1)}, u32[]{:S(2)}, u32[]{:S(2)}) collective-permute-start(bf16[128,512]{1,0:T(8,128)(2,1)S(1)} %collective-permute-done.14.refs_4_), channel_id=1, source_target_pairs={{0,1},{1,0},{2,6},{3,7},{4,5},{5,4},{6,2},{7,3},{8,9},{9,8},{10,14... | collective-permute-start | bytes 393224 | tf_op jit(solution)/shard_map/ppermute | solution.py:154
  42.2 3.1 %collective-permute-start.23 = (bf16[128,512]{1,0:T(8,128)(2,1)S(1)}, bf16[128,512]{1,0:T(8,128)(2,1)S(1)}, u32[]{:S(2)}, u32[]{:S(2)}) collective-permute-start(bf16[128,512]{1,0:T(8,128)(2,1)S(1)} %collective-permute-done.22.refs_2_), channel_id=1, source_target_pairs={{0,1},{1,0},{2,6},{3,7},{4,5},{5,4},{6,2},{7,3},{8,9},{9,8},{10,14... | collective-permute-start | bytes 393224 | tf_op jit(solution)/shard_map/ppermute | solution.py:154
  44.2 1.3 %collective-permute-start.25 = (bf16[128,512]{1,0:T(8,128)(2,1)S(1)}, bf16[128,512]{1,0:T(8,128)(2,1)S(1)}, u32[]{:S(2)}, u32[]{:S(2)}) collective-permute-start(bf16[128,512]{1,0:T(8,128)(2,1)S(1)} %collective-permute-done.24.refs_4_), channel_id=1, source_target_pairs={{0,1},{1,0},{2,6},{3,7},{4,5},{5,4},{6,2},{7,3},{8,9},{9,8},{10,14... | collective-permute-start | bytes 393224 | tf_op jit(solution)/shard_map/ppermute | solution.py:154
  44.2 1.8 %collective-permute-start.19 = (bf16[128,256]{1,0:T(8,128)(2,1)S(1)}, bf16[128,256]{1,0:T(8,128)(2,1)S(1)}, u32[]{:S(2)}, u32[]{:S(2)}) collective-permute-start(bf16[128,256]{1,0:T(8,128)(2,1)S(1)} %get-tuple-element.99), channel_id=1, source_target_pairs={{0,1},{1,0},{2,6},{3,7},{4,5},{5,4},{6,2},{7,3},{8,9},{9,8},{10,14... | collective-permute-start | bytes 196616 | tf_op jit(solution)/shard_map/ppermute | solution.py:154
  44.8 1.4 %collective-permute-start.20 = (bf16[128,256]{1,0:T(8,128)(2,1)S(1)}, bf16[128,256]{1,0:T(8,128)(2,1)S(1)}, u32[]{:S(2)}, u32[]{:S(2)}) collective-permute-start(bf16[128,256]{1,0:T(8,128)(2,1)S(1)} %get-tuple-element.100), channel_id=1, source_target_pairs={{0,1},{1,0},{2,10},{3,11},{4,5},{5,4},{6,14},{7,15},{8,9},{9,8},{1... | collective-permute-start | bytes 196616 | tf_op jit(solution)/shard_map/ppermute | solution.py:154
  44.8 1.4 %collective-permute-start.21 = (bf16[128,256]{1,0:T(8,128)(2,1)S(1)}, bf16[128,256]{1,0:T(8,128)(2,1)S(1)}, u32[]{:S(2)}, u32[]{:S(2)}) collective-permute-start(bf16[128,256]{1,0:T(8,128)(2,1)S(1)} %get-tuple-element.101), channel_id=1, source_target_pairs={{0,1},{1,0},{2,14},{3,15},{4,5},{5,4},{6,10},{7,11},{8,9},{9,8},{1... | collective-permute-start | bytes 196616 | tf_op jit(solution)/shard_map/ppermute | solution.py:154
  45.5 14.8 %collective-permute-start.27 = (bf16[128,256]{1,0:T(8,128)(2,1)S(1)}, bf16[128,256]{1,0:T(8,128)(2,1)S(1)}, u32[]{:S(2)}, u32[]{:S(2)}) collective-permute-start(bf16[128,256]{1,0:T(8,128)(2,1)S(1)} %get-tuple-element.106), channel_id=1, source_target_pairs={{0,1},{1,0},{2,6},{3,7},{4,5},{5,4},{6,2},{7,3},{8,9},{9,8},{10,14... | collective-permute-start | bytes 196616 | tf_op jit(solution)/shard_map/ppermute | solution.py:154
  45.7 14.6 %collective-permute-start.28 = (bf16[128,256]{1,0:T(8,128)(2,1)S(1)}, bf16[128,256]{1,0:T(8,128)(2,1)S(1)}, u32[]{:S(2)}, u32[]{:S(2)}) collective-permute-start(bf16[128,256]{1,0:T(8,128)(2,1)S(1)} %get-tuple-element.107), channel_id=1, source_target_pairs={{0,1},{1,0},{2,10},{3,11},{4,5},{5,4},{6,14},{7,15},{8,9},{9,8},{1... | collective-permute-start | bytes 196616 | tf_op jit(solution)/shard_map/ppermute | solution.py:154
  46.0 14.2 %collective-permute-start.29 = (bf16[128,256]{1,0:T(8,128)(2,1)S(1)}, bf16[128,256]{1,0:T(8,128)(2,1)S(1)}, u32[]{:S(2)}, u32[]{:S(2)}) collective-permute-start(bf16[128,256]{1,0:T(8,128)(2,1)S(1)} %get-tuple-element.108), channel_id=1, source_target_pairs={{0,1},{1,0},{2,14},{3,15},{4,5},{5,4},{6,10},{7,11},{8,9},{9,8},{1... | collective-permute-start | bytes 196616 | tf_op jit(solution)/shard_map/ppermute | solution.py:154
  46.2 18.9 %collective-permute-start.26 = (bf16[1024,128]{1,0:T(8,128)(2,1)S(1)}, bf16[1024,128]{1,0:T(8,128)(2,1)S(1)}, u32[]{:S(2)}, u32[]{:S(2)}) collective-permute-start(bf16[1024,128]{1,0:T(8,128)(2,1)S(1)} %shard_map.85), channel_id=1, source_target_pairs={{0,3},{1,2},{2,1},{3,0},{4,7},{5,6},{6,5},{7,4},{8,11},{9,10},{10,... | collective-permute-start | bytes 786440 | tf_op jit(solution)/shard_map/ppermute | solution.py:154
  (4 other events, 8.6 us)
